TPU v7x, 32 devices: a whole 2x2x4 slice. The times are simulated.
32 devices in a mesh: row: 4 (over y, core), col: 8 (over z, x).
Axes of the slice: x: 2, y: 2, z: 4, core: 2. Of those that a mesh axis runs over, the one named last changes fastest.
Arguments:
- probes: bfloat16 [4, 8192, 256], P(None, ('row', 'col')), may hold values from -6 to 6
- points: bfloat16 [16, 4, 8192], P(None, None, ('row', 'col')), may hold values from -8 to 8
- leaf_skeleton: int32 [64, 64], P(('row', 'col')), may hold values from 0 to 127, as said below
- skeleton_one: int32 [32, 64], P(('row', 'col')), may hold values from 0 to 127, as said below
- skeleton_two: int32 [16, 64], P('row'), may hold values from 0 to 127, as said below
- skeleton_three: int32 [8, 64], P('row'), may hold values from 0 to 127, as said below
Outputs:
- leaf_interp: float32 [64, 128, 64], P(('row', 'col'))
- upper_interp: float32 [3, 32, 128, 64], P(None, ('row', 'col'))
- top_state: float32 [2, 32, 64, 256], P(None, ('row', 'col'))
Inputs may be any that keep to these rules, and one draw needn't show every extreme that they name: `leaf_skeleton`: each row names 64 different rows of its leaf, in ascending order. `skeleton_one`: each row names 64 different rows of the node's stacked child skeletons, in ascending order. `skeleton_two`: each row names 64 different rows of the node's stacked child skeletons, in ascending order. `skeleton_three`: each row names 64 different rows of the node's stacked child skeletons, in ascending order.
All inputs are finite; a program needn't handle non-finite values.
Results may differ from a plain program's by a relative error of at most 0.0059.
Values may be sent and summed in bfloat16 or wider, within the bound.
No kernel may reach another device: no remote copies, remote signals or barrier semaphores. Data moves between devices by JAX's collectives and lax.ppermute only.
A program may use at most 64 MiB of HBM per device.

v0:
```python
import math

import jax
import jax.numpy as jnp
from jax import lax
from jax.experimental import pallas as pl
from jax.experimental.pallas import tpu as pltpu
from jax.sharding import PartitionSpec as P

LEAF = 128
F32 = jnp.float32
BF16 = jnp.bfloat16
DOUBLINGS = 9
VMEM = pl.BlockSpec(memory_space=pltpu.VMEM)


def vmem(shape, kind=F32):
    return pltpu.VMEM(tuple(shape), kind)


COST = pl.CostEstimate(flops=10**9, bytes_accessed=0, transcendentals=0)
SHORT = pl.CostEstimate(flops=0, bytes_accessed=0, transcendentals=0)
LONG = pl.CostEstimate(flops=10**10, bytes_accessed=0, transcendentals=0)
PARAMS = pltpu.CompilerParams(vmem_limit_bytes=16 << 20)


def chebyshev_constants():
    taus = [1282.0 / 1280.0]
    for _ in range(DOUBLINGS):
        taus.append(2.0 * taus[-1] * taus[-1] - 1.0)
    front = 2.0**DOUBLINGS * math.prod(taus[:-1]) / taus[-1]
    return taus[:-1], front


TAUS, FRONT = chebyshev_constants()


def over(first, second, first_dim, second_dim):
    return lax.dot_general(
        first,
        second,
        (((first_dim,), (second_dim,)), ((), ())),
        preferred_element_type=F32,
    )


def split(value):
    high = value.astype(BF16)
    rest = value - high.astype(F32)
    middle = rest.astype(BF16)
    return high, middle, (rest - middle.astype(F32)).astype(BF16)


def norm_rows(norm, first, width):
    parts = [part.astype(F32) for part in split(norm)]
    place = lax.broadcasted_iota(jnp.int32, (16, width), 0)
    extra = jnp.where(place < 6, 1.0, 0.0)
    for pos in range(3):
        extra = jnp.where(place == pos + first, parts[pos], extra)
    return extra


def row_features(feats, gain):
    feats = feats.astype(F32)
    depth, width = feats.shape
    unit = math.log2(math.e) / (2.0 * depth)
    norm = jnp.sum(feats * feats, axis=0, keepdims=True) * -unit + math.log2(gain)
    parts = [part.astype(F32) for part in split(feats * (2.0 * unit))]
    return jnp.concatenate([*parts, norm_rows(norm, 0, width)], axis=0)


def col_features(feats):
    feats = feats.astype(F32)
    depth, width = feats.shape
    unit = math.log2(math.e) / (2.0 * depth)
    norm = jnp.sum(feats * feats, axis=0, keepdims=True) * -unit
    return jnp.concatenate([feats, feats, feats, norm_rows(norm, 3, width)], axis=0).astype(BF16)


def pack_body(*refs):
    probes_ref, points_ref, *table_refs = refs[:6]
    first_ref, second_ref, own_ref, held_ref, rows_ref, *held_tables, sem = refs[6:]
    span = probes_ref.shape[1]
    pairs = [(points_ref, held_ref), *zip(table_refs, held_tables)]
    small = len(pairs)
    for quarter in range(4):
        target = (first_ref, second_ref)[quarter // 2].at[pl.ds(quarter % 2 * span, span)]
        pairs.append((probes_ref.at[quarter], target))
    copies = [
        pltpu.make_async_copy(source, target, sem.at[pos])
        for pos, (source, target) in enumerate(pairs)
    ]
    for copy in copies:
        copy.start()
    rows_ref[...] = jnp.zeros_like(rows_ref)
    for copy in copies[:small]:
        copy.wait()
    points = held_ref[...].astype(F32)
    for quarter in range(4):
        feats = points[:, quarter, :].astype(BF16)
        half_ref = (first_ref, second_ref)[quarter // 2]
        half_ref[pl.ds(2 * span + quarter % 2 * 16, 16), :] = feats
        if quarter == 0:
            own_ref[...] = feats
    start = 0
    for table in held_tables:
        count, rank = table.shape
        rows_ref[pl.ds(start, count), pl.ds(0, rank)] = table[...].astype(F32)
        start += count
    first_ref[pl.ds(second_ref.shape[0], rows_ref.shape[0]), :] = rows_ref[...].astype(BF16)
    for copy in copies[small:]:
        copy.wait()


def pack(probes, points, tables):
    _, span, samples = probes.shape
    table_rows = -(-sum(table.shape[0] for table in tables) // 16) * 16
    inputs = (probes, points, *tables)
    return pl.pallas_call(
        pack_body,
        out_shape=(
            vmem((2 * (span + 16) + table_rows, samples), BF16),
            vmem((2 * (span + 16), samples), BF16),
            vmem((16, span), BF16),
        ),
        in_specs=[pl.BlockSpec(memory_space=pltpu.HBM)] * len(inputs),
        scratch_shapes=[
            pltpu.VMEM(points.shape, BF16),
            pltpu.VMEM((table_rows, samples), F32),
            *[pltpu.VMEM(table.shape, jnp.int32) for table in tables],
            pltpu.SemaphoreType.DMA((5 + len(tables),)),
        ],
        cost_estimate=COST,
        compiler_params=PARAMS,
        name="pack",
    )(*(pltpu.with_memory_space_constraint(value, pltpu.HBM) for value in inputs))


def masked(entries):
    shape = entries.shape
    row_leaf = lax.broadcasted_iota(jnp.int32, shape, 0) // LEAF
    col_leaf = lax.broadcasted_iota(jnp.int32, shape, 1) // LEAF
    return jnp.where(row_leaf == col_leaf, 0.0, entries)


def add_halves(half_refs, row_refs, cols_ref, put, span, own):
    for number, half_ref in enumerate(half_refs):
        for quarter in range(2):
            feats = half_ref[pl.ds(2 * span + 16 * quarter, 16), :]
            cols_ref[:, pl.ds((2 * number + quarter) * span, span)] = col_features(feats)
    columns = 2 * span * len(half_refs)
    for group, rows_ref in enumerate(row_refs):
        for start in range(0, rows_ref.shape[0], span):
            feats = rows_ref[pl.ds(start, span), :]
            entries = jnp.exp2(over(feats, cols_ref[:, :columns], 1, 0))
            if own and group == 0 and start == 0:
                entries = jnp.concatenate([masked(entries[:, :span]), entries[:, span:]], axis=1)
            randoms = [half_ref[pl.ds(0, 2 * span), :] for half_ref in half_refs]
            put(group, start, over(entries.astype(BF16), jnp.concatenate(randoms, axis=0), 1, 0))


def first_product_body(gain, span, groups, point_count, *refs):
    half_refs, point_refs = refs[:2], refs[2 : point_count + 2]
    row_refs = refs[point_count + 2 : point_count + 2 + len(groups)]
    total_refs, cols_ref = refs[point_count + 2 + len(groups) : -1], refs[-1]
    for rows_ref, places in zip(row_refs, groups):
        for pos, (array, start) in enumerate(places):
            feats = point_refs[array][:, pl.ds(start, span)]
            rows_ref[pl.ds(pos * span, span), :] = row_features(feats, gain).T.astype(BF16)

    def put(group, start, value):
        total_refs[group][pl.ds(start, span), :] = value

    add_halves(half_refs, row_refs, cols_ref, put, span, True)


def first_product(halves, points, groups, span, gain):
    samples = halves[0].shape[1]
    rows = [len(places) * span for places in groups]
    out = pl.pallas_call(
        lambda *refs: first_product_body(gain, span, groups, len(points), *refs),
        out_shape=[vmem((count, 64), BF16) for count in rows]
        + [vmem((count, samples), F32) for count in rows],
        scratch_shapes=[pltpu.VMEM((64, 4 * span), BF16)],
        cost_estimate=COST,
        compiler_params=PARAMS,
        name="first_product",
    )(*halves, *points)
    return out[: len(groups)], out[len(groups) :]


def product_body(span, half_count, count, *refs):
    half_refs, refs = refs[:half_count], refs[half_count:]
    row_refs, old_refs, total_refs = refs[:count], refs[count : 2 * count], refs[2 * count : -1]
    cols_ref = refs[-1]
    for number in range(0, half_count, 2):

        def put(group, start, value):
            place = pl.ds(start, span)
            base = old_refs if number == 0 else total_refs
            total_refs[group][place, :] = base[group][place, :] + value

        add_halves(half_refs[number : number + 2], row_refs, cols_ref, put, span, False)


def product(halves, rows, totals, span, cost=COST):
    return pl.pallas_call(
        lambda *refs: product_body(span, len(halves), len(rows), *refs),
        out_shape=[vmem(total.shape, F32) for total in totals],
        scratch_shapes=[pltpu.VMEM((64, 4 * span), BF16)],
        cost_estimate=cost,
        compiler_params=PARAMS,
        name="product",
    )(*halves, *rows, *totals)


def add_up_body(span, outs, mine_ref, theirs_ref, *refs):
    for (chunks, _), out_ref in zip(outs, refs[-len(outs) :]):
        for pos, chunk in enumerate(chunks):
            place = pl.ds(chunk * span, span)
            value = mine_ref[place, :] + theirs_ref[place, :].astype(F32)
            out_ref[pl.ds(pos * span, span), :] = value.astype(out_ref.dtype)


def add_up(mine, theirs, outs, span, after=(), cost=COST):
    samples = mine.shape[1]
    return pl.pallas_call(
        lambda *refs: add_up_body(span, outs, *refs),
        out_shape=[vmem((len(chunks) * span, samples), kind) for chunks, kind in outs],
        cost_estimate=cost,
        compiler_params=PARAMS,
        name="add_up",
    )(mine, theirs, *after)


def wide_product(first, second, second_dim):
    high, middle, low = split(first)
    other_high, other_middle, other_low = split(second)
    return over(
        jnp.concatenate([high, high, middle, middle, low, high], axis=1),
        jnp.concatenate(
            [other_high, other_middle, other_high, other_middle, other_high, other_low],
            axis=second_dim,
        ),
        1,
        second_dim,
    )


def exact_product(first, second):
    second = second.astype(BF16)
    return over(
        jnp.concatenate(split(first), axis=1), jnp.concatenate([second] * 3, axis=0), 1, 0
    )


def twice_product(twice_parts, parts):
    high, middle, low = twice_parts
    other_high, other_middle, other_low = parts
    left = lax.broadcasted_iota(jnp.int32, high.shape, 1) < high.shape[1] // 2
    last = jnp.where(left, low.astype(F32), high.astype(F32)).astype(BF16)
    return over(
        jnp.concatenate([high, middle, last], axis=1),
        jnp.concatenate(
            [other_high, other_middle, other_high, other_middle, other_high, other_low], axis=0
        ),
        1,
        0,
    )


def select_rows(picks, value):
    return over(
        jnp.concatenate([picks] * 3, axis=1), jnp.concatenate(split(value), axis=0), 1, 0
    )


def interpolate(stacks, skeletons):
    rank, pool = skeletons[0].shape[0], stacks[0].shape[0]
    place = lax.broadcasted_iota(jnp.int32, (rank, 2 * rank), 0)
    other = lax.broadcasted_iota(jnp.int32, (rank, 2 * rank), 1)
    eyes = jnp.where((other == place) | (other == place + rank), 1.0, 0.0)
    states = []
    for skeleton, stack in zip(skeletons, stacks):
        products = wide_product(skeleton, jnp.concatenate([stack, skeleton, skeleton], axis=0), 1)
        ridge = 0.05 * jnp.sum(skeleton * skeleton, keepdims=True) / rank + 1e-05
        inverse = 1.0 / (640.0 * ridge)
        states.append((products[:, :pool], eyes - products[:, pool:] * inverse, inverse))
    for number, tau in enumerate(TAUS):
        last = number == DOUBLINGS - 1
        later = []
        for solved, power, inverse in states:
            power_parts = split(power)
            parts = split(solved)
            if not last:
                parts = [jnp.concatenate(pair, axis=1) for pair in zip(parts, power_parts)]
            both = twice_product(power_parts, parts)
            solved = solved + both[:, :pool] * (1.0 / tau)
            later.append((solved, None if last else 2.0 * both[:, pool:] - eyes, inverse))
        states = later
    return [solved * (inverse * FRONT) for solved, _, inverse in states]


def merge(nodes, early=None):
    stacks, skeletons = [], []
    for samples, reduced, coupling, picks in nodes:
        pool = samples.shape[0]
        high, middle, low = split(reduced)
        coupled = over(
            coupling, jnp.concatenate([high, middle, high, middle, high, low], axis=0), 1, 0
        )
        stacks.append(samples - coupled[:pool])
        skeletons.append(select_rows(picks, samples) - coupled[pool:])
    if early is not None:
        early(skeletons[0])
    interps = interpolate(stacks, skeletons)
    return [
        (interp, skeleton, wide_product(interp, node[1], 0))
        for interp, skeleton, node in zip(interps, skeletons, nodes)
    ]


def leaves_body(received, *refs):
    own_ref, *others = refs[: received + 1]
    source_ref, picks_ref, couplings_ref = refs[received + 1 : received + 4]
    leaf_ref, upper_ref, skeleton_ref, reduced_ref, sent_ref, held_ref, sem = refs[-7:]
    total = own_ref[...]
    for other in others:
        total = total + other[...].astype(F32)
    count = total.shape[0] // LEAF
    stacks = [total[leaf * LEAF : (leaf + 1) * LEAF] for leaf in range(count)]
    skeletons = [select_rows(picks_ref[leaf], stack) for leaf, stack in enumerate(stacks)]
    reduced = []
    for leaf, interp in enumerate(interpolate(stacks, skeletons)):
        held_ref[leaf] = interp
        reduced.append(exact_product(interp, source_ref[pl.ds(leaf * LEAF, LEAF), :]))
    copy = pltpu.make_async_copy(held_ref, leaf_ref, sem)
    copy.start()
    node = (
        jnp.concatenate(skeletons, axis=0),
        jnp.concatenate(reduced, axis=0),
        couplings_ref[...],
        picks_ref[count],
    )
    ((interp, skeleton, reduced),) = merge([node])
    upper_ref[...] = interp
    skeleton_ref[...] = skeleton
    reduced_ref[...] = reduced
    for pos, part in enumerate((*split(skeleton)[:2], reduced.astype(BF16))):
        sent_ref[pl.ds(pos * skeleton.shape[0], skeleton.shape[0]), :] = part
    copy.wait()


def leaves(own, others, source, picks, couplings, later, leaf_count):
    samples = own.shape[1]
    rank, pool = picks.shape[1:]
    return pl.pallas_call(
        lambda *refs: leaves_body(len(others), *refs),
        out_shape=(
            jax.ShapeDtypeStruct((leaf_count, rank, LEAF), F32),
            vmem((rank, pool), F32),
            vmem((rank, samples), F32),
            vmem((rank, samples), F32),
            vmem((3 * rank, samples), BF16),
        ),
        out_specs=(pl.BlockSpec(memory_space=pl.ANY), VMEM, VMEM, VMEM, VMEM),
        scratch_shapes=[pltpu.VMEM((leaf_count, rank, LEAF), F32), pltpu.SemaphoreType.DMA],
        cost_estimate=COST,
        compiler_params=PARAMS,
        name="leaves",
    )(own, *others, source, picks, couplings, *later)


def first_of_pair(number):
    return (lax.axis_index("col") >> (number - 2)) % 2 == 0


def pair(mine, theirs, mine_first):
    first = jnp.where(mine_first, mine, theirs)
    second = jnp.where(mine_first, theirs, mine)
    return jnp.concatenate([first, second], axis=0)


def upper_body(picks_count, *refs):
    states = [(refs[0][...], refs[1][...])]
    rank = refs[0].shape[0]
    for got_ref in refs[2:5]:
        high, middle, reduced = (got_ref[pl.ds(pos * rank, rank), :] for pos in range(3))
        states.append((high.astype(F32) + middle.astype(F32), reduced.astype(F32)))
    picks_ref, two_ref, other_ref, three_ref, one_ref, upper_out, top_out = refs[5:12]
    upper_ref, state_ref, sem = refs[12:]
    places = [
        (one_ref, upper_out.at[0, 0]),
        (upper_ref.at[0], upper_out.at[1, 0]),
        (upper_ref.at[1], upper_out.at[2, 0]),
        (state_ref.at[0], top_out.at[0, 0]),
        (state_ref.at[1], top_out.at[1, 0]),
    ]
    copies = [
        pltpu.make_async_copy(source, target, sem.at[pos])
        for pos, (source, target) in enumerate(places)
    ]
    copies[0].start()
    mine_first = first_of_pair(2)
    nodes = []
    for number, coupling_ref in enumerate((two_ref, other_ref)):
        mine, theirs = states[2 * number : 2 * number + 2]
        picks = picks_ref[picks_count - 3 + number]
        stacks = [pair(*parts, mine_first) for parts in zip(mine, theirs)]
        nodes.append((*stacks, coupling_ref[...], picks))
    mine, theirs = merge(nodes)
    upper_ref[0] = mine[0]
    copies[1].start()

    def early(skeleton):
        state_ref[0] = skeleton
        copies[3].start()

    mine_first = first_of_pair(3)
    stacks = [pair(*parts, mine_first) for parts in zip(mine[1:], theirs[1:])]
    ((interp, _, reduced),) = merge([(*stacks, three_ref[...], picks_ref[picks_count - 1])], early)
    upper_ref[1] = interp
    copies[2].start()
    state_ref[1] = reduced
    copies[4].start()
    for copy in copies:
        copy.wait()


def upper_levels(skeleton, reduced, got, picks, couplings, interp_one):
    rank, pool = picks.shape[1:]
    samples = skeleton.shape[1]
    return pl.pallas_call(
        lambda *refs: upper_body(picks.shape[0], *refs),
        out_shape=(
            jax.ShapeDtypeStruct((3, 1, rank, pool), F32),
            jax.ShapeDtypeStruct((2, 1, rank, samples), F32),
        ),
        out_specs=(pl.BlockSpec(memory_space=pl.ANY),) * 2,
        scratch_shapes=[
            pltpu.VMEM((2, rank, pool), F32),
            pltpu.VMEM((2, rank, samples), F32),
            pltpu.SemaphoreType.DMA((5,)),
        ],
        cost_estimate=COST,
        compiler_params=PARAMS,
        name="upper_levels",
    )(skeleton, reduced, *got, picks, *couplings, interp_one)


def one_hot(chosen, pool):
    place = lax.broadcasted_iota(jnp.int32, (pool, chosen.shape[1]), 0)
    return jnp.where(place.astype(F32) == chosen, 1.0, 0.0).astype(F32)


def couple(first, second, picks, gain, couplings_ref):
    rank = first.shape[1]
    points = jnp.concatenate([first, second], axis=1)
    entries = jnp.exp2(over(row_features(points, gain).astype(BF16), col_features(points), 0, 0))
    left = lax.broadcasted_iota(jnp.int32, entries.shape, 1) < rank
    upper = lax.broadcasted_iota(jnp.int32, entries.shape, 0) < rank
    entries = jnp.where(left == upper, 0.0, entries)
    chosen = select_rows(picks.T.astype(BF16), entries)
    high, middle, low = split(jnp.concatenate([entries, chosen], axis=0))
    couplings_ref[...] = jnp.concatenate([high, high, middle, middle, low, high], axis=1)


def coupling_shape(rank):
    return vmem((3 * rank, 12 * rank), BF16)


def skeletons_body(gain, span, counts, mine_ref, beside_ref, *refs):
    picks_ref, one_ref, two_ref, points_ref = refs
    rank, pool = picks_ref.shape[1:]
    leaf_count = counts[0]
    tables = 2 * (span + 16)
    nodes = []
    for source_ref in (mine_ref, beside_ref):
        rows = source_ref[pl.ds(tables, source_ref.shape[0] - tables), :rank].astype(F32)
        hots = [one_hot(rows[pos : pos + 1], pool) for pos in range(leaf_count + 1)]
        children = []
        for leaf in range(leaf_count):
            feats = source_ref[pl.ds(2 * span, 16), pl.ds(leaf * LEAF, LEAF)]
            children.append(over(feats, hots[leaf].astype(BF16), 1, 0))
        points = jnp.concatenate(children, axis=1)
        nodes.append(over(points, hots[leaf_count], 1, 0))
        if source_ref is mine_ref:
            couple(*children, hots[leaf_count], gain, one_ref)
            start = leaf_count + counts[1]
            level_two = lax.axis_index("col") // 2
            wanted = [level_two, level_two + 1 - 2 * (level_two % 2), counts[2] + level_two // 2]
            for row in wanted:
                place = lax.broadcasted_iota(jnp.int32, rows.shape, 0)
                named = jnp.where(place == start + row, rows, 0.0)
                hots.append(one_hot(jnp.sum(named, axis=0, keepdims=True), pool))
            for number, hot in enumerate(hots):
                picks_ref[number] = hot.T.astype(BF16)
            upper = hots[leaf_count + 1]
    mine, theirs = nodes
    mine_first = first_of_pair(2)
    first = jnp.where(mine_first, mine, theirs)
    second = jnp.where(mine_first, theirs, mine)
    couple(first, second, upper, gain, two_ref)
    points_ref[...] = jnp.concatenate([first, second], axis=1).astype(BF16)


def skeletons(packed, beside, tables, span, gain):
    leaf_count, rank = tables[0].shape
    counts = [table.shape[0] for table in tables]
    return pl.pallas_call(
        lambda *refs: skeletons_body(gain, span, counts, *refs),
        out_shape=(
            vmem((leaf_count + 4, rank, LEAF), BF16),
            coupling_shape(rank),
            coupling_shape(rank),
            vmem((16, 2 * rank), BF16),
        ),
        cost_estimate=COST,
        compiler_params=PARAMS,
        name="skeletons",
    )(packed, beside)


def top_couplings_body(gain, mine_ref, theirs_ref, picks_ref, other_ref, three_ref):
    count, rank, _ = picks_ref.shape
    picks = [picks_ref[count - pos].astype(F32).T for pos in (3, 2, 1)]
    mine, theirs = mine_ref[...].astype(F32), theirs_ref[...].astype(F32)
    couple(theirs[:, :rank], theirs[:, rank:], picks[1], gain, other_ref)
    mine, theirs = over(mine, picks[0], 1, 0), over(theirs, picks[1], 1, 0)
    mine_first = first_of_pair(3)
    first = jnp.where(mine_first, mine, theirs)
    second = jnp.where(mine_first, theirs, mine)
    couple(first, second, picks[2], gain, three_ref)


def top_couplings(mine, theirs, picks, gain):
    return pl.pallas_call(
        lambda *refs: top_couplings_body(gain, *refs),
        out_shape=[coupling_shape(picks.shape[1])] * 2,
        cost_estimate=LONG,
        compiler_params=PARAMS,
        name="top_couplings",
    )(mine, theirs, picks)


def local(probes, points, leaf_skeleton, skeleton_one, skeleton_two, skeleton_three):
    span = probes.shape[1]
    row_count = lax.axis_size("row")
    col_count = lax.axis_size("col")
    gain = 16.0 / math.sqrt(4 * span * row_count * col_count)

    def swap(value, row_bits, col_bits):
        pairs = [
            (r * col_count + c, (r ^ row_bits) * col_count + (c ^ col_bits))
            for r in range(row_count)
            for c in range(col_count)
        ]
        return lax.ppermute(value, ("row", "col"), pairs)

    tables = (leaf_skeleton, skeleton_one, skeleton_two, skeleton_three)
    first, second, own_points = pack(probes, points, tables)
    beside_first, across_second = swap(first, 0, 1), swap(second, 2, 0)
    line = col_count // 2
    line_points = own_points
    for bit in range(1, col_count.bit_length() - 1):
        line_points = jnp.concatenate([line_points, swap(line_points, 0, 1 << bit)], axis=1)
        if bit == 1:
            line_points, *late = lax.optimization_barrier((line_points, first, second))
    beside_second, across_first = swap(late[1], 0, 1), swap(late[0], 2, 0)
    line_points = [line_points, swap(line_points, 1, 0)]
    near, far = range(2), range(2, line)
    groups = [
        [(core, chunk * span) for chunk in group] for core in range(2) for group in (near, far)
    ]
    feats, totals = first_product((first, second), line_points, groups, span, gain)
    beside_first, across_second, *totals = lax.optimization_barrier(
        (beside_first, across_second, *totals)
    )
    diagonal = [swap(beside_first, 2, 0), swap(across_second, 0, 1)]
    totals = product([beside_first, across_second], feats, totals, span, SHORT)
    beside_second, across_first, *totals = lax.optimization_barrier(
        (beside_second, across_first, *totals)
    )
    totals = product([beside_second, across_first], feats, totals, span)
    first, *totals = lax.optimization_barrier((first, *totals))
    picks, couplings_one, couplings_two, points_two = skeletons(
        first, beside_first, tables, span, gain
    )
    points_two, *totals = lax.optimization_barrier((points_two, *totals))
    pieces = [first, second, beside_first, beside_second, across_first, across_second, *diagonal]
    for bit in range(2, row_count.bit_length() - 1):
        more = [swap(value, 1 << bit, 0) for value in pieces]
        totals = product(more, feats, totals, span)
        pieces += more
    (theirs,) = product(diagonal, feats[3:], totals[3:], span)
    from_sibling = swap(theirs, 1, 0)
    (mine,) = product(diagonal, feats[1:2], totals[1:2], span)
    outs = [(range(0, line - 2, 2), F32), (range(1, line - 2, 2), BF16)]
    kept, sent = add_up(mine, from_sibling, outs, span)
    (theirs,) = product(diagonal, feats[2:3], totals[2:3], span)
    sent, theirs, points_two = lax.optimization_barrier((sent, theirs, points_two))
    arrived = swap(sent, 0, 2)
    from_sibling = swap(theirs, 1, 0)
    (mine,) = product(diagonal, feats[:1], totals[:1], span)
    own_sum, near_sent = add_up(mine, from_sibling, [([0], F32), ([1], BF16)], span)
    near_sum = swap(near_sent, 0, 2)
    received = []
    chunks = list(range(2, line, 2))
    bit = 2
    while chunks:
        sent_places = [pos for pos, chunk in enumerate(chunks) if chunk & bit]
        kept_places = [pos for pos, chunk in enumerate(chunks) if not chunk & bit]
        outs = [(sent_places, BF16)] + [(kept_places, F32)] * (len(kept_places) > 0)
        sent, *kept = add_up(kept, arrived, outs, span, (near_sent,), LONG)
        arrived = swap(sent, 0, 2 * bit)
        received.append(arrived[:span] if len(sent_places) > 1 else arrived)
        if kept:
            (kept,) = kept
            arrived = arrived[span:]
        chunks = [chunks[pos] for pos in kept_places]
        bit *= 2
    received.append(near_sum)
    other_points = swap(points_two, 0, 2)
    later = top_couplings(points_two, other_points, picks, gain)

    leaf_interp, interp_one, skeleton, reduced, sent = leaves(
        own_sum, received, first, picks, couplings_one, later, leaf_skeleton.shape[0]
    )
    got = [swap(sent, 0, bits) for bits in (1, 2, 3)]
    upper_interp, top_state = upper_levels(
        skeleton, reduced, got, picks, (couplings_two, *later), interp_one
    )
    return jnp.swapaxes(leaf_interp, 1, 2), jnp.swapaxes(upper_interp, 2, 3), top_state


def solution(mesh):
    placed = (
        P(None, ("row", "col"), None),
        P(None, None, ("row", "col")),
        P(("row", "col"), None),
        P(("row", "col"), None),
        P("row", None),
        P("row", None),
    )
    return jax.shard_map(
        local,
        mesh=mesh,
        in_specs=placed,
        out_specs=(
            P(("row", "col"), None, None),
            P(None, ("row", "col"), None, None),
            P(None, ("row", "col"), None, None),
        ),
        check_vma=False,
    )
```

profile of v0, /device:TPU:0, one launch (start us, length us, event | category | flops | bytes accessed | tf_op | source)
XLA Modules:
  0.0 63.3 jit_solution(10764341202350173048)
XLA Ops:
  0.6 1.3 %pack.1 = (bf16[560,256]{1,0:T(8,128)(2,1)S(1)}, bf16[544,256]{1,0:T(8,128)(2,1)S(1)}, bf16[16,256]{1,0:T(8,128)(2,1)S(1)}) custom-call(bf16[4,256,256]{2,1,0:T(8,128)(2,1)} %refs_0_.1, bf16[16,4,256]{2,1,0:T(4,128)(2,1)} %refs_1_.1, s32[2,64]{1,0:T(2,128)} %refs_2_.1, s32[1,64]{1,0:T(1,128)} %refs_3_.1, s32[4,64]{1,0:T(4,128)} %refs_4_.1, s32[2,64]{1,0:T(2,128)} %refs_5_.1), custom_call_target="tpu_custom_call" | custom-call | flops 1000000000 | tf_op jit(solution)/shard_map/pack/pallas_call | solution.py:119
  1.9 3.1 %collective-permute-start.2 = (bf16[16,256]{1,0:T(8,128)(2,1)S(1)}, bf16[16,256]{1,0:T(8,128)(2,1)S(1)}, u32[]{:S(2)}, u32[]{:S(2)}) collective-permute-start(bf16[16,256]{1,0:T(8,128)(2,1)S(1)} %get-tuple-element.69), channel_id=1, source_target_pairs={{0,2},{1,3},{2,0},{3,1},{4,6},{5,7},{6,4},{7,5},{8,10},{9,11},{10,... | collective-permute-start | bytes 24584 | tf_op jit(solution)/shard_map/ppermute | solution.py:558
  5.0 1.5 %collective-permute-start.1 = (bf16[544,256]{1,0:T(8,128)(2,1)S(1)}, bf16[544,256]{1,0:T(8,128)(2,1)S(1)}, u32[]{:S(2)}, u32[]{:S(2)}) collective-permute-start(bf16[544,256]{1,0:T(8,128)(2,1)S(1)} %get-tuple-element.78.refs_1_), channel_id=1, source_target_pairs={{0,16},{1,17},{2,18},{3,19},{4,20},{5,21},{6,22},{7,23},{8,24},{9,... | collective-permute-start | bytes 835592 | tf_op jit(solution)/shard_map/ppermute | solution.py:558
  6.5 1.5 %collective-permute-start = (bf16[560,256]{1,0:T(8,128)(2,1)S(1)}, bf16[560,256]{1,0:T(8,128)(2,1)S(1)}, u32[]{:S(2)}, u32[]{:S(2)}) collective-permute-start(bf16[560,256]{1,0:T(8,128)(2,1)S(1)} %get-tuple-element.101.refs_0_.refs_3_), channel_id=1, source_target_pairs={{0,1},{1,0},{2,3},{3,2},{4,5},{5,4},{6,7},{7,6},{8,9},{9,8},{10,11... | collective-permute-start | bytes 860168 | tf_op jit(solution)/shard_map/ppermute | solution.py:558
  8.0 0.0 collective-permute-done.2
  8.0 2.6 %collective-permute-start.3 = (bf16[16,512]{1,0:T(8,128)(2,1)S(1)}, bf16[16,512]{1,0:T(8,128)(2,1)S(1)}, u32[]{:S(2)}, u32[]{:S(2)}) collective-permute-start(bf16[16,512]{1,0:T(8,128)(2,1)S(1)} %pad_maximum_fusion), channel_id=1, source_target_pairs={{0,4},{1,5},{2,6},{3,7},{4,0},{5,1},{6,2},{7,3},{8,12},{9,13},{10,... | collective-permute-start | bytes 49160 | tf_op jit(solution)/shard_map/ppermute | solution.py:558
  10.6 0.6 collective-permute-start.7
  11.1 1.5 %collective-permute-start.8 = (bf16[560,256]{1,0:T(8,128)(2,1)S(1)}, bf16[560,256]{1,0:T(8,128)(2,1)S(1)}, u32[]{:S(2)}, u32[]{:S(2)}) collective-permute-start(bf16[560,256]{1,0:T(8,128)(2,1)S(1)} %get-tuple-element.101.refs_0_.refs_3_), channel_id=1, source_target_pairs={{0,16},{1,17},{2,18},{3,19},{4,20},{5,21},{6,22},{7,23},{8,24},{9,... | collective-permute-start | bytes 860168 | tf_op jit(solution)/shard_map/ppermute | solution.py:558
  12.7 0.0 collective-permute-done.3
  12.7 0.0 collective-permute-start.4
  12.7 1.2 %collective-permute-done.4.refs_3_ = bf16[16,1024]{1,0:T(8,128)(2,1)S(1)} collective-permute-done((bf16[16,1024]{1,0:T(8,128)(2,1)S(1)}, bf16[16,1024]{1,0:T(8,128)(2,1)S(1)}, u32[]{:S(2)}, u32[]{:S(2)}) %collective-permute-start.4) | collective-permute-done | bytes 32800 | tf_op jit(solution)/shard_map/ppermute | solution.py:558
  13.9 2.5 %first_product.1 = (bf16[512,64]{1,0:T(8,128)(2,1)S(1)}, bf16[512,64]{1,0:T(8,128)(2,1)S(1)}, bf16[512,64]{1,0:T(8,128)(2,1)S(1)}, bf16[512,64]{1,0:T(8,128)(2,1...) custom-call(bf16[560,256]{1,0:T(8,128)(2,1)S(1)} %get-tuple-element.10, ...), custom_call_target="tpu_custom_call" | custom-call | flops 1000000000 | tf_op jit(solution)/shard_map/first_product/pallas_call | solution.py:180
  16.4 0.0 collective-permute-done.1.refs_1_
  16.4 0.0 collective-permute-done.refs_0_.refs_1_
  16.4 0.6 collective-permute-start.5
  17.1 1.5 %collective-permute-start.6 = (bf16[544,256]{1,0:T(8,128)(2,1)S(1)}, bf16[544,256]{1,0:T(8,128)(2,1)S(1)}, u32[]{:S(2)}, u32[]{:S(2)}) collective-permute-start(bf16[544,256]{1,0:T(8,128)(2,1)S(1)} %collective-permute-done.1.refs_1_), channel_id=1, source_target_pairs={{0,1},{1,0},{2,3},{3,2},{4,5},{5,4},{6,7},{7,6},{8,9},{9,8},{10,11... | collective-permute-start | bytes 835592 | tf_op jit(solution)/shard_map/ppermute | solution.py:558
  18.5 2.5 %product.6 = (f32[512,256]{1,0:T(8,128)S(1)}, f32[512,256]{1,0:T(8,128)S(1)}, f32[512,256]{1,0:T(8,128)S(1)}, f32[512,256]{1,0:T(8,128)S(1)}) custom-call(bf16[560,256]{1,0:T(8,128)(2,1)S(1)} %collective-permute-done.refs_0_.refs_1_, bf16[544,256]{1,0:T(8,128)(2,1)S(1)} %collective-permute-done.1.refs_1_, bf16[512,64]{1,0:T(8,128)(2,1)S(1)} %get-tuple-element.77.refs_2_, ...), custom_call_target="tpu_custom_call" | custom-call | tf_op jit(solution)/shard_map/product/pallas_call | solution.py:207
  21.0 0.3 collective-permute-done.7.refs_0_
  21.4 0.0 collective-permute-done.8.refs_1_
  21.4 2.5 %product.7 = (f32[512,256]{1,0:T(8,128)S(1)}, f32[512,256]{1,0:T(8,128)S(1)}, f32[512,256]{1,0:T(8,128)S(1)}, f32[512,256]{1,0:T(8,128)S(1)}) custom-call(bf16[544,256]{1,0:T(8,128)(2,1)S(1)} %collective-permute-done.7.refs_0_, bf16[560,256]{1,0:T(8,128)(2,1)S(1)} %collective-permute-done.8.refs_1_, bf16[512,64]{1,0:T(8,128)(2,1)S(1)} %get-tuple-element.77.refs_2_, ...), custom_call_target="tpu_custom_call" | custom-call | flops 1000000000 | tf_op jit(solution)/shard_map/product/pallas_call | solution.py:207
  23.9 1.2 %skeletons.1 = (bf16[6,64,128]{2,1,0:T(8,128)(2,1)S(1)}, bf16[192,768]{1,0:T(8,128)(2,1)S(1)}, bf16[192,768]{1,0:T(8,128)(2,1)S(1)}, bf16[16,128]{1,0:T(8,128)(2,1)S(1)}) custom-call(bf16[560,256]{1,0:T(8,128)(2,1)S(1)} %get-tuple-element.101.refs_0_.refs_3_, bf16[560,256]{1,0:T(8,128)(2,1)S(1)} %collective-permute-done.refs_0_.refs_1_), custom_call_target="tpu_custom_call" | custom-call | flops 1000000000 | tf_op jit(solution)/shard_map/skeletons/pallas_call | solution.py:510
  25.1 1.4 %collective-permute-done.6.refs_1_ = bf16[544,256]{1,0:T(8,128)(2,1)S(1)} collective-permute-done((bf16[544,256]{1,0:T(8,128)(2,1)S(1)}, bf16[544,256]{1,0:T(8,128)(2,1)S(1)}, u32[]{:S(2)}, u32[]{:S(2)}) %collective-permute-start.6) | collective-permute-done | bytes 278560 | tf_op jit(solution)/shard_map/ppermute | solution.py:558
  26.5 0.0 collective-permute-done.5.refs_0_
  26.5 0.8 %product.10 = f32[512,256]{1,0:T(8,128)S(1)} custom-call(bf16[560,256]{1,0:T(8,128)(2,1)S(1)} %collective-permute-done.5.refs_0_, bf16[544,256]{1,0:T(8,128)(2,1)S(1)} %collective-permute-done.6.refs_1_, bf16[512,64]{1,0:T(8,128)(2,1)S(1)} %get-tuple-element.82.refs_5_.refs_2_, f32[512,256]{1,0:T(8,128)S(1)} %get-tuple-element.109.refs_3_), custom_call_target="tpu_custom_call" | custom-call | flops 1000000000 | tf_op jit(solution)/shard_map/product/pallas_call | solution.py:207
  27.3 0.1 collective-permute-start.9
  27.4 0.8 %product.9.refs_0_ = f32[512,256]{1,0:T(8,128)S(1)} custom-call(bf16[560,256]{1,0:T(8,128)(2,1)S(1)} %collective-permute-done.5.refs_0_, bf16[544,256]{1,0:T(8,128)(2,1)S(1)} %collective-permute-done.6.refs_1_, bf16[512,64]{1,0:T(8,128)(2,1)S(1)} %get-tuple-element.80.refs_3_.refs_2_, f32[512,256]{1,0:T(8,128)S(1)} %get-tuple-element.108.refs_3_), custom_call_target="tpu_custom_call" | custom-call | flops 1000000000 | tf_op jit(solution)/shard_map/product/pallas_call | solution.py:207
  28.2 0.8 %product.11 = f32[512,256]{1,0:T(8,128)S(1)} custom-call(bf16[560,256]{1,0:T(8,128)(2,1)S(1)} %collective-permute-done.5.refs_0_, bf16[544,256]{1,0:T(8,128)(2,1)S(1)} %collective-permute-done.6.refs_1_, bf16[512,64]{1,0:T(8,128)(2,1)S(1)} %get-tuple-element.81.refs_4_.refs_2_, f32[512,256]{1,0:T(8,128)S(1)} %get-tuple-element.111.refs_3_), custom_call_target="tpu_custom_call" | custom-call | flops 1000000000 | tf_op jit(solution)/shard_map/product/pallas_call | solution.py:207
  29.0 0.2 collective-permute-done.9.refs_1_
  29.3 0.1 add_up.3
  29.3 0.3 collective-permute-start.10
  29.7 0.6 collective-permute-start.11
  30.3 0.8 %product.8.refs_0_ = f32[512,256]{1,0:T(8,128)S(1)} custom-call(bf16[560,256]{1,0:T(8,128)(2,1)S(1)} %collective-permute-done.5.refs_0_, bf16[544,256]{1,0:T(8,128)(2,1)S(1)} %collective-permute-done.6.refs_1_, bf16[512,64]{1,0:T(8,128)(2,1)S(1)} %get-tuple-element.77.refs_2_, f32[512,256]{1,0:T(8,128)S(1)} %get-tuple-element.107.refs_3_), custom_call_target="tpu_custom_call" | custom-call | flops 1000000000 | tf_op jit(solution)/shard_map/product/pallas_call | solution.py:207
  31.1 1.5 %collective-permute-start.14 = (bf16[16,128]{1,0:T(8,128)(2,1)S(1)}, bf16[16,128]{1,0:T(8,128)(2,1)S(1)}, u32[]{:S(2)}, u32[]{:S(2)}) collective-permute-start(bf16[16,128]{1,0:T(8,128)(2,1)S(1)} %get-tuple-element.120.refs_0_), channel_id=1, source_target_pairs={{0,2},{1,3},{2,0},{3,1},{4,6},{5,7},{6,4},{7,5},{8,10},{9,11},{10,... | collective-permute-start | bytes 12296 | tf_op jit(solution)/shard_map/ppermute | solution.py:558
  32.6 0.0 collective-permute-done.10.refs_1_
  32.6 0.1 add_up.4
  32.7 0.7 %collective-permute-start.13 = (bf16[256,256]{1,0:T(8,128)(2,1)S(1)}, bf16[256,256]{1,0:T(8,128)(2,1)S(1)}, u32[]{:S(2)}, u32[]{:S(2)}) collective-permute-start(bf16[256,256]{1,0:T(8,128)(2,1)S(1)} %get-tuple-element.117.refs_2_), channel_id=1, source_target_pairs={{0,2},{1,3},{2,0},{3,1},{4,6},{5,7},{6,4},{7,5},{8,10},{9,11},{10,... | collective-permute-start | bytes 393224 | tf_op jit(solution)/shard_map/ppermute | solution.py:558
  33.3 2.3 %collective-permute-done.11.refs_1_ = bf16[256,256]{1,0:T(8,128)(2,1)S(1)} collective-permute-done((bf16[256,256]{1,0:T(8,128)(2,1)S(1)}, bf16[256,256]{1,0:T(8,128)(2,1)S(1)}, u32[]{:S(2)}, u32[]{:S(2)}) %collective-permute-start.11) | collective-permute-done | bytes 131104 | tf_op jit(solution)/shard_map/ppermute | solution.py:558
  35.6 2.7 %collective-permute-start.12 = (bf16[256,256]{1,0:T(8,128)(2,1)S(1)}, bf16[256,256]{1,0:T(8,128)(2,1)S(1)}, u32[]{:S(2)}, u32[]{:S(2)}) collective-permute-start(bf16[256,256]{1,0:T(8,128)(2,1)S(1)} %add_up.5), channel_id=1, source_target_pairs={{0,4},{1,5},{2,6},{3,7},{4,0},{5,1},{6,2},{7,3},{8,12},{9,13},{10,... | collective-permute-start | bytes 393224 | tf_op jit(solution)/shard_map/ppermute | solution.py:558
  38.3 0.0 collective-permute-done.14.refs_1_
  38.3 0.9 %top_couplings.1 = (bf16[192,768]{1,0:T(8,128)(2,1)S(1)}, bf16[192,768]{1,0:T(8,128)(2,1)S(1)}) custom-call(bf16[16,128]{1,0:T(8,128)(2,1)S(1)} %get-tuple-element.120.refs_0_, bf16[16,128]{1,0:T(8,128)(2,1)S(1)} %collective-permute-done.14.refs_1_, bf16[6,64,128]{2,1,0:T(8,128)(2,1)S(1)} %get-tuple-element.118.refs_2_.refs_4_.refs_5_), custom_call_target="tpu_custom_call" | custom-call | flops 10000000000 | tf_op jit(solution)/shard_map/top_couplings/pallas_call | solution.py:537
  39.2 4.8 %collective-permute-done.12.refs_1_ = bf16[256,256]{1,0:T(8,128)(2,1)S(1)} collective-permute-done((bf16[256,256]{1,0:T(8,128)(2,1)S(1)}, bf16[256,256]{1,0:T(8,128)(2,1)S(1)}, u32[]{:S(2)}, u32[]{:S(2)}) %collective-permute-start.12) | collective-permute-done | bytes 131104 | tf_op jit(solution)/shard_map/ppermute | solution.py:558
  43.9 0.0 collective-permute-done.13.refs_2_
  43.9 5.6 %leaves.1 = (f32[2,64,128]{2,1,0:T(8,128)}, f32[64,128]{1,0:T(8,128)S(1)}, f32[64,256]{1,0:T(8,128)S(1)}, f32[64,256]{1,0:T(8,128)S(1)}, bf16[192,256]{1,0:T(8,128)(2,1)S(1)}) custom-call(f32[256,256]{1,0:T(8,128)S(1)} %get-tuple-element.114.refs_0_, bf16[256,256]{1,0:T(8,128)(2,1)S(1)} %collective-permute-done.12.refs_1_, ...), custom_call_target="tpu_custom_call" | custom-call | flops 1000000000 | tf_op jit(solution)/shard_map/leaves/pallas_call | solution.py:357
  49.5 0.9 %collective-permute-start.17 = (bf16[192,256]{1,0:T(8,128)(2,1)S(1)}, bf16[192,256]{1,0:T(8,128)(2,1)S(1)}, u32[]{:S(2)}, u32[]{:S(2)}) collective-permute-start(bf16[192,256]{1,0:T(8,128)(2,1)S(1)} %get-tuple-element.126), channel_id=1, source_target_pairs={{0,3},{1,2},{2,1},{3,0},{4,7},{5,6},{6,5},{7,4},{8,11},{9,10},{10,... | collective-permute-start | bytes 294920 | tf_op jit(solution)/shard_map/ppermute | solution.py:558
  50.4 2.2 %collective-permute-start.16 = (bf16[192,256]{1,0:T(8,128)(2,1)S(1)}, bf16[192,256]{1,0:T(8,128)(2,1)S(1)}, u32[]{:S(2)}, u32[]{:S(2)}) collective-permute-start(bf16[192,256]{1,0:T(8,128)(2,1)S(1)} %get-tuple-element.126), channel_id=1, source_target_pairs={{0,2},{1,3},{2,0},{3,1},{4,6},{5,7},{6,4},{7,5},{8,10},{9,11},{10,... | collective-permute-start | bytes 294920 | tf_op jit(solution)/shard_map/ppermute | solution.py:558
  52.6 0.5 collective-permute-start.15
  53.1 2.0 %collective-permute-done.17.refs_4_ = bf16[192,256]{1,0:T(8,128)(2,1)S(1)} collective-permute-done((bf16[192,256]{1,0:T(8,128)(2,1)S(1)}, bf16[192,256]{1,0:T(8,128)(2,1)S(1)}, u32[]{:S(2)}, u32[]{:S(2)}) %collective-permute-start.17) | collective-permute-done | bytes 98336 | tf_op jit(solution)/shard_map/ppermute | solution.py:558
  55.1 1.1 %collective-permute-done.16.refs_3_ = bf16[192,256]{1,0:T(8,128)(2,1)S(1)} collective-permute-done((bf16[192,256]{1,0:T(8,128)(2,1)S(1)}, bf16[192,256]{1,0:T(8,128)(2,1)S(1)}, u32[]{:S(2)}, u32[]{:S(2)}) %collective-permute-start.16) | collective-permute-done | bytes 98336 | tf_op jit(solution)/shard_map/ppermute | solution.py:558
  56.2 1.0 %collective-permute-done.15.refs_2_ = bf16[192,256]{1,0:T(8,128)(2,1)S(1)} collective-permute-done((bf16[192,256]{1,0:T(8,128)(2,1)S(1)}, bf16[192,256]{1,0:T(8,128)(2,1)S(1)}, u32[]{:S(2)}, u32[]{:S(2)}) %collective-permute-start.15) | collective-permute-done | bytes 98336 | tf_op jit(solution)/shard_map/ppermute | solution.py:558
  57.2 5.9 %upper_levels.1 = (f32[3,1,64,128]{3,2,1,0:T(8,128)}, f32[2,1,64,256]{3,2,1,0:T(8,128)}) custom-call(f32[64,256]{1,0:T(8,128)S(1)} %get-tuple-element.124.refs_0_, f32[64,256]{1,0:T(8,128)S(1)} %get-tuple-element.125.refs_1_, bf16[192,256]{1,0:T(8,128)(2,1)S(1)} %collective-permute-done.15.refs_2_, bf16[192,256]{1,0:T(8,128)(2,1)S(1)} %collective-permute-done.16.refs_3_, ...), custom_call_target="tpu_custom_call" | custom-call | flops 1000000000 | tf_op jit(solution)/shard_map/upper_levels/pallas_call | solution.py:433
  (4 shorter events, 0.0 us)
Async XLA Ops:
  1.9 6.1 %collective-permute-start.2 = (bf16[16,256]{1,0:T(8,128)(2,1)S(1)}, bf16[16,256]{1,0:T(8,128)(2,1)S(1)}, u32[]{:S(2)}, u32[]{:S(2)}) collective-permute-start(bf16[16,256]{1,0:T(8,128)(2,1)S(1)} %get-tuple-element.69), channel_id=1, source_target_pairs={{0,2},{1,3},{2,0},{3,1},{4,6},{5,7},{6,4},{7,5},{8,10},{9,11},{10,... | collective-permute-start | bytes 24584 | tf_op jit(solution)/shard_map/ppermute | solution.py:558
  5.0 11.4 %collective-permute-start.1 = (bf16[544,256]{1,0:T(8,128)(2,1)S(1)}, bf16[544,256]{1,0:T(8,128)(2,1)S(1)}, u32[]{:S(2)}, u32[]{:S(2)}) collective-permute-start(bf16[544,256]{1,0:T(8,128)(2,1)S(1)} %get-tuple-element.78.refs_1_), channel_id=1, source_target_pairs={{0,16},{1,17},{2,18},{3,19},{4,20},{5,21},{6,22},{7,23},{8,24},{9,... | collective-permute-start | bytes 835592 | tf_op jit(solution)/shard_map/ppermute | solution.py:558
  6.5 9.9 %collective-permute-start = (bf16[560,256]{1,0:T(8,128)(2,1)S(1)}, bf16[560,256]{1,0:T(8,128)(2,1)S(1)}, u32[]{:S(2)}, u32[]{:S(2)}) collective-permute-start(bf16[560,256]{1,0:T(8,128)(2,1)S(1)} %get-tuple-element.101.refs_0_.refs_3_), channel_id=1, source_target_pairs={{0,1},{1,0},{2,3},{3,2},{4,5},{5,4},{6,7},{7,6},{8,9},{9,8},{10,11... | collective-permute-start | bytes 860168 | tf_op jit(solution)/shard_map/ppermute | solution.py:558
  8.0 4.7 %collective-permute-start.3 = (bf16[16,512]{1,0:T(8,128)(2,1)S(1)}, bf16[16,512]{1,0:T(8,128)(2,1)S(1)}, u32[]{:S(2)}, u32[]{:S(2)}) collective-permute-start(bf16[16,512]{1,0:T(8,128)(2,1)S(1)} %pad_maximum_fusion), channel_id=1, source_target_pairs={{0,4},{1,5},{2,6},{3,7},{4,0},{5,1},{6,2},{7,3},{8,12},{9,13},{10,... | collective-permute-start | bytes 49160 | tf_op jit(solution)/shard_map/ppermute | solution.py:558
  10.6 10.8 %collective-permute-start.7 = (bf16[544,256]{1,0:T(8,128)(2,1)S(1)}, bf16[544,256]{1,0:T(8,128)(2,1)S(1)}, u32[]{:S(2)}, u32[]{:S(2)}) collective-permute-start(bf16[544,256]{1,0:T(8,128)(2,1)S(1)} %get-tuple-element.78.refs_1_), channel_id=1, source_target_pairs={{0,1},{1,0},{2,3},{3,2},{4,5},{5,4},{6,7},{7,6},{8,9},{9,8},{10,11... | collective-permute-start | bytes 835592 | tf_op jit(solution)/shard_map/ppermute | solution.py:558
  11.1 10.2 %collective-permute-start.8 = (bf16[560,256]{1,0:T(8,128)(2,1)S(1)}, bf16[560,256]{1,0:T(8,128)(2,1)S(1)}, u32[]{:S(2)}, u32[]{:S(2)}) collective-permute-start(bf16[560,256]{1,0:T(8,128)(2,1)S(1)} %get-tuple-element.101.refs_0_.refs_3_), channel_id=1, source_target_pairs={{0,16},{1,17},{2,18},{3,19},{4,20},{5,21},{6,22},{7,23},{8,24},{9,... | collective-permute-start | bytes 860168 | tf_op jit(solution)/shard_map/ppermute | solution.py:558
  12.7 1.2 %collective-permute-start.4 = (bf16[16,1024]{1,0:T(8,128)(2,1)S(1)}, bf16[16,1024]{1,0:T(8,128)(2,1)S(1)}, u32[]{:S(2)}, u32[]{:S(2)}) collective-permute-start(bf16[16,1024]{1,0:T(8,128)(2,1)S(1)} %constant_dynamic-update-slice_fusion.refs_2_), channel_id=1, source_target_pairs={{0,8},{1,9},{2,10},{3,11},{4,12},{5,13},{6,14},{7,15},{8,0},{9,1},... | collective-permute-start | bytes 98312 | tf_op jit(solution)/shard_map/ppermute | solution.py:558
  16.4 10.0 %collective-permute-start.5 = (bf16[560,256]{1,0:T(8,128)(2,1)S(1)}, bf16[560,256]{1,0:T(8,128)(2,1)S(1)}, u32[]{:S(2)}, u32[]{:S(2)}) collective-permute-start(bf16[560,256]{1,0:T(8,128)(2,1)S(1)} %collective-permute-done.refs_0_.refs_1_), channel_id=1, source_target_pairs={{0,16},{1,17},{2,18},{3,19},{4,20},{5,21},{6,22},{7,23},{8,24},{9,... | collective-permute-start | bytes 860168 | tf_op jit(solution)/shard_map/ppermute | solution.py:558
  17.1 9.4 %collective-permute-start.6 = (bf16[544,256]{1,0:T(8,128)(2,1)S(1)}, bf16[544,256]{1,0:T(8,128)(2,1)S(1)}, u32[]{:S(2)}, u32[]{:S(2)}) collective-permute-start(bf16[544,256]{1,0:T(8,128)(2,1)S(1)} %collective-permute-done.1.refs_1_), channel_id=1, source_target_pairs={{0,1},{1,0},{2,3},{3,2},{4,5},{5,4},{6,7},{7,6},{8,9},{9,8},{10,11... | collective-permute-start | bytes 835592 | tf_op jit(solution)/shard_map/ppermute | solution.py:558
  27.3 2.0 %collective-permute-start.9 = (f32[512,256]{1,0:T(8,128)S(1)}, f32[512,256]{1,0:T(8,128)S(1)}, u32[]{:S(2)}, u32[]{:S(2)}) collective-permute-start(f32[512,256]{1,0:T(8,128)S(1)} %product.10), channel_id=1, source_target_pairs={{0,8},{1,9},{2,10},{3,11},{4,12},{5,13},{6,14},{7,15},{8,0},{9,1},... | collective-permute-start | bytes 1572872 | tf_op jit(solution)/shard_map/ppermute | solution.py:558
  29.3 3.3 %collective-permute-start.10 = (f32[512,256]{1,0:T(8,128)S(1)}, f32[512,256]{1,0:T(8,128)S(1)}, u32[]{:S(2)}, u32[]{:S(2)}) collective-permute-start(f32[512,256]{1,0:T(8,128)S(1)} %product.11), channel_id=1, source_target_pairs={{0,8},{1,9},{2,10},{3,11},{4,12},{5,13},{6,14},{7,15},{8,0},{9,1},... | collective-permute-start | bytes 1572872 | tf_op jit(solution)/shard_map/ppermute | solution.py:558
  29.7 6.0 %collective-permute-start.11 = (bf16[256,256]{1,0:T(8,128)(2,1)S(1)}, bf16[256,256]{1,0:T(8,128)(2,1)S(1)}, u32[]{:S(2)}, u32[]{:S(2)}) collective-permute-start(bf16[256,256]{1,0:T(8,128)(2,1)S(1)} %get-tuple-element.116), channel_id=1, source_target_pairs={{0,2},{1,3},{2,0},{3,1},{4,6},{5,7},{6,4},{7,5},{8,10},{9,11},{10,... | collective-permute-start | bytes 393224 | tf_op jit(solution)/shard_map/ppermute | solution.py:558
  31.1 7.2 %collective-permute-start.14 = (bf16[16,128]{1,0:T(8,128)(2,1)S(1)}, bf16[16,128]{1,0:T(8,128)(2,1)S(1)}, u32[]{:S(2)}, u32[]{:S(2)}) collective-permute-start(bf16[16,128]{1,0:T(8,128)(2,1)S(1)} %get-tuple-element.120.refs_0_), channel_id=1, source_target_pairs={{0,2},{1,3},{2,0},{3,1},{4,6},{5,7},{6,4},{7,5},{8,10},{9,11},{10,... | collective-permute-start | bytes 12296 | tf_op jit(solution)/shard_map/ppermute | solution.py:558
  32.7 11.3 %collective-permute-start.13 = (bf16[256,256]{1,0:T(8,128)(2,1)S(1)}, bf16[256,256]{1,0:T(8,128)(2,1)S(1)}, u32[]{:S(2)}, u32[]{:S(2)}) collective-permute-start(bf16[256,256]{1,0:T(8,128)(2,1)S(1)} %get-tuple-element.117.refs_2_), channel_id=1, source_target_pairs={{0,2},{1,3},{2,0},{3,1},{4,6},{5,7},{6,4},{7,5},{8,10},{9,11},{10,... | collective-permute-start | bytes 393224 | tf_op jit(solution)/shard_map/ppermute | solution.py:558
  35.6 8.3 %collective-permute-start.12 = (bf16[256,256]{1,0:T(8,128)(2,1)S(1)}, bf16[256,256]{1,0:T(8,128)(2,1)S(1)}, u32[]{:S(2)}, u32[]{:S(2)}) collective-permute-start(bf16[256,256]{1,0:T(8,128)(2,1)S(1)} %add_up.5), channel_id=1, source_target_pairs={{0,4},{1,5},{2,6},{3,7},{4,0},{5,1},{6,2},{7,3},{8,12},{9,13},{10,... | collective-permute-start | bytes 393224 | tf_op jit(solution)/shard_map/ppermute | solution.py:558
  49.5 5.6 %collective-permute-start.17 = (bf16[192,256]{1,0:T(8,128)(2,1)S(1)}, bf16[192,256]{1,0:T(8,128)(2,1)S(1)}, u32[]{:S(2)}, u32[]{:S(2)}) collective-permute-start(bf16[192,256]{1,0:T(8,128)(2,1)S(1)} %get-tuple-element.126), channel_id=1, source_target_pairs={{0,3},{1,2},{2,1},{3,0},{4,7},{5,6},{6,5},{7,4},{8,11},{9,10},{10,... | collective-permute-start | bytes 294920 | tf_op jit(solution)/shard_map/ppermute | solution.py:558
  50.4 5.8 %collective-permute-start.16 = (bf16[192,256]{1,0:T(8,128)(2,1)S(1)}, bf16[192,256]{1,0:T(8,128)(2,1)S(1)}, u32[]{:S(2)}, u32[]{:S(2)}) collective-permute-start(bf16[192,256]{1,0:T(8,128)(2,1)S(1)} %get-tuple-element.126), channel_id=1, source_target_pairs={{0,2},{1,3},{2,0},{3,1},{4,6},{5,7},{6,4},{7,5},{8,10},{9,11},{10,... | collective-permute-start | bytes 294920 | tf_op jit(solution)/shard_map/ppermute | solution.py:558
  52.6 4.6 %collective-permute-start.15 = (bf16[192,256]{1,0:T(8,128)(2,1)S(1)}, bf16[192,256]{1,0:T(8,128)(2,1)S(1)}, u32[]{:S(2)}, u32[]{:S(2)}) collective-permute-start(bf16[192,256]{1,0:T(8,128)(2,1)S(1)} %get-tuple-element.126), channel_id=1, source_target_pairs={{0,1},{1,0},{2,3},{3,2},{4,5},{5,4},{6,7},{7,6},{8,9},{9,8},{10,11... | collective-permute-start | bytes 294920 | tf_op jit(solution)/shard_map/ppermute | solution.py:558
where the time goes:
time: 63.4 us; the launch traced here: 63.3 us
  Pallas kernels  25.8 us (41%)
  starting transfers between devices  22.3 us (35%)
  waiting for transfers between devices  14.3 us (23%)
  between operations  0.91 us (1%)
    ppermute x18, starting transfers between devices, swap(): return lax.ppermute(value, ('row', 'col'), pairs)  22.3 us
    ppermute x18, waiting for transfers between devices, swap(): return lax.ppermute(value, ('row', 'col'), pairs)  14.3 us
    pallas_call x6, Pallas kernels, product(): pl.pallas_call(lambda *refs: product_body(span, len(halves), len(rows), *...  8.27 us
    pallas_call x1, Pallas kernels, upper_levels(): pl.pallas_call(lambda *refs: upper_body(picks.shape[0], *refs), out_shape...  5.94 us
    pallas_call x1, Pallas kernels, leaves(): pl.pallas_call(lambda *refs: leaves_body(len(others), *refs), out_shape=(...  5.59 us
    pallas_call x1, Pallas kernels, first_product(): pl.pallas_call(lambda *refs: first_product_body(gain, span, groups, len(p...  2.53 us
  transfers between devices with their start and end apart: 18, of which 9 were waited for; matrix products, arithmetic and copies ran while one was open for 0% of the time, Pallas kernels for 19%

commit v1 on v0

--- a/solution.py
+++ b/solution.py
@@ -143,8 +143,8 @@
     return jnp.where(row_leaf == col_leaf, 0.0, entries)
 
 
-def add_halves(half_refs, row_refs, cols_ref, put, span, own):
-    for number, half_ref in enumerate(half_refs):
+def add_halves(half_refs, row_refs, cols_ref, put, span, own, ready=False):
+    for number, half_ref in enumerate(() if ready else half_refs):
         for quarter in range(2):
             feats = half_ref[pl.ds(2 * span + 16 * quarter, 16), :]
             cols_ref[:, pl.ds((2 * number + quarter) * span, span)] = col_features(feats)
@@ -189,10 +189,12 @@
     return out[: len(groups)], out[len(groups) :]
 
 
-def product_body(span, half_count, count, *refs):
+def product_body(span, half_count, count, ready, *refs):
     half_refs, refs = refs[:half_count], refs[half_count:]
-    row_refs, old_refs, total_refs = refs[:count], refs[count : 2 * count], refs[2 * count : -1]
-    cols_ref = refs[-1]
+    row_refs, old_refs = refs[:count], refs[count : 2 * count]
+    total_refs, cols_ref = refs[2 * count : 3 * count], refs[-1]
+    if ready:
+        cols_ref, *total_refs = refs[2 * count :]
     for number in range(0, half_count, 2):
 
         def put(group, start, value):
@@ -200,18 +202,21 @@
             base = old_refs if number == 0 else total_refs
             total_refs[group][place, :] = base[group][place, :] + value
 
-        add_halves(half_refs[number : number + 2], row_refs, cols_ref, put, span, False)
-
-
-def product(halves, rows, totals, span, cost=COST):
-    return pl.pallas_call(
-        lambda *refs: product_body(span, len(halves), len(rows), *refs),
-        out_shape=[vmem(total.shape, F32) for total in totals],
-        scratch_shapes=[pltpu.VMEM((64, 4 * span), BF16)],
+        add_halves(half_refs[number : number + 2], row_refs, cols_ref, put, span, False, ready)
+
+
+def product(halves, rows, totals, span, cost=COST, cols=()):
+    out_shape = [vmem(total.shape, F32) for total in totals]
+    if not cols:
+        out_shape.append(vmem((64, 4 * span), BF16))
+    out = pl.pallas_call(
+        lambda *refs: product_body(span, len(halves), len(rows), len(cols) > 0, *refs),
+        out_shape=out_shape,
         cost_estimate=cost,
         compiler_params=PARAMS,
         name="product",
-    )(*halves, *rows, *totals)
+    )(*halves, *rows, *totals, *cols)
+    return out if not cols else [*out, *cols]
 
 
 def add_up_body(span, outs, mine_ref, theirs_ref, *refs):
@@ -233,18 +238,27 @@
     )(mine, theirs, *after)
 
 
-def wide_product(first, second, second_dim):
+def wide_product(first, second):
     high, middle, low = split(first)
     other_high, other_middle, other_low = split(second)
     return over(
         jnp.concatenate([high, high, middle, middle, low, high], axis=1),
         jnp.concatenate(
-            [other_high, other_middle, other_high, other_middle, other_high, other_low],
-            axis=second_dim,
+            [other_high, other_middle, other_high, other_middle, other_high, other_low], axis=1
         ),
         1,
-        second_dim,
-    )
+        1,
+    )
+
+
+def near_product(first, second):
+    high, middle, _ = split(first)
+    return over(jnp.concatenate([high, high, middle], axis=1), near_parts(second), 1, 0)
+
+
+def near_parts(second):
+    high, middle, _ = split(second)
+    return jnp.concatenate([high, middle, high], axis=0)
 
 
 def exact_product(first, second):
@@ -254,11 +268,12 @@
     )
 
 
-def twice_product(twice_parts, parts):
-    high, middle, low = twice_parts
+def twice_product(twice, twice_parts, parts):
+    high, middle, _ = twice_parts
     other_high, other_middle, other_low = parts
     left = lax.broadcasted_iota(jnp.int32, high.shape, 1) < high.shape[1] // 2
-    last = jnp.where(left, low.astype(F32), high.astype(F32)).astype(BF16)
+    low = twice - high.astype(F32) - middle.astype(F32)
+    last = jnp.where(left, low, high.astype(F32)).astype(BF16)
     return over(
         jnp.concatenate([high, middle, last], axis=1),
         jnp.concatenate(
@@ -282,7 +297,7 @@
     eyes = jnp.where((other == place) | (other == place + rank), 1.0, 0.0)
     states = []
     for skeleton, stack in zip(skeletons, stacks):
-        products = wide_product(skeleton, jnp.concatenate([stack, skeleton, skeleton], axis=0), 1)
+        products = wide_product(skeleton, jnp.concatenate([stack, skeleton, skeleton], axis=0))
         ridge = 0.05 * jnp.sum(skeleton * skeleton, keepdims=True) / rank + 1e-05
         inverse = 1.0 / (640.0 * ridge)
         states.append((products[:, :pool], eyes - products[:, pool:] * inverse, inverse))
@@ -294,7 +309,7 @@
             parts = split(solved)
             if not last:
                 parts = [jnp.concatenate(pair, axis=1) for pair in zip(parts, power_parts)]
-            both = twice_product(power_parts, parts)
+            both = twice_product(power, power_parts, parts)
             solved = solved + both[:, :pool] * (1.0 / tau)
             later.append((solved, None if last else 2.0 * both[:, pool:] - eyes, inverse))
         states = later
@@ -305,17 +320,14 @@
     stacks, skeletons = [], []
     for samples, reduced, coupling, picks in nodes:
         pool = samples.shape[0]
-        high, middle, low = split(reduced)
-        coupled = over(
-            coupling, jnp.concatenate([high, middle, high, middle, high, low], axis=0), 1, 0
-        )
+        coupled = over(coupling, near_parts(reduced), 1, 0)
         stacks.append(samples - coupled[:pool])
         skeletons.append(select_rows(picks, samples) - coupled[pool:])
     if early is not None:
         early(skeletons[0])
     interps = interpolate(stacks, skeletons)
     return [
-        (interp, skeleton, wide_product(interp, node[1], 0))
+        (interp, skeleton, near_product(interp, node[1]))
         for interp, skeleton, node in zip(interps, skeletons, nodes)
     ]
 
@@ -461,12 +473,12 @@
     upper = lax.broadcasted_iota(jnp.int32, entries.shape, 0) < rank
     entries = jnp.where(left == upper, 0.0, entries)
     chosen = select_rows(picks.T.astype(BF16), entries)
-    high, middle, low = split(jnp.concatenate([entries, chosen], axis=0))
-    couplings_ref[...] = jnp.concatenate([high, high, middle, middle, low, high], axis=1)
+    high, middle, _ = split(jnp.concatenate([entries, chosen], axis=0))
+    couplings_ref[...] = jnp.concatenate([high, high, middle], axis=1)
 
 
 def coupling_shape(rank):
-    return vmem((3 * rank, 12 * rank), BF16)
+    return vmem((3 * rank, 6 * rank), BF16)
 
 
 def skeletons_body(gain, span, counts, mine_ref, beside_ref, *refs):
@@ -577,11 +589,11 @@
         (beside_first, across_second, *totals)
     )
     diagonal = [swap(beside_first, 2, 0), swap(across_second, 0, 1)]
-    totals = product([beside_first, across_second], feats, totals, span, SHORT)
+    *totals, _ = product([beside_first, across_second], feats, totals, span, SHORT)
     beside_second, across_first, *totals = lax.optimization_barrier(
         (beside_second, across_first, *totals)
     )
-    totals = product([beside_second, across_first], feats, totals, span)
+    *totals, _ = product([beside_second, across_first], feats, totals, span)
     first, *totals = lax.optimization_barrier((first, *totals))
     picks, couplings_one, couplings_two, points_two = skeletons(
         first, beside_first, tables, span, gain
@@ -590,18 +602,18 @@
     pieces = [first, second, beside_first, beside_second, across_first, across_second, *diagonal]
     for bit in range(2, row_count.bit_length() - 1):
         more = [swap(value, 1 << bit, 0) for value in pieces]
-        totals = product(more, feats, totals, span)
+        *totals, _ = product(more, feats, totals, span)
         pieces += more
-    (theirs,) = product(diagonal, feats[3:], totals[3:], span)
+    theirs, *cols = product(diagonal, feats[3:], totals[3:], span)
     from_sibling = swap(theirs, 1, 0)
-    (mine,) = product(diagonal, feats[1:2], totals[1:2], span)
+    mine, _ = product(diagonal, feats[1:2], totals[1:2], span, cols=cols)
     outs = [(range(0, line - 2, 2), F32), (range(1, line - 2, 2), BF16)]
     kept, sent = add_up(mine, from_sibling, outs, span)
-    (theirs,) = product(diagonal, feats[2:3], totals[2:3], span)
+    theirs, _ = product(diagonal, feats[2:3], totals[2:3], span, cols=cols)
     sent, theirs, points_two = lax.optimization_barrier((sent, theirs, points_two))
     arrived = swap(sent, 0, 2)
     from_sibling = swap(theirs, 1, 0)
-    (mine,) = product(diagonal, feats[:1], totals[:1], span)
+    mine, _ = product(diagonal, feats[:1], totals[:1], span, cols=cols)
     own_sum, near_sent = add_up(mine, from_sibling, [([0], F32), ([1], BF16)], span)
     near_sum = swap(near_sent, 0, 2)
     received = []

time: 63.4 us -> 63.1 us (level)
  waiting for transfers between devices: 14.3 us -> 13.3 us
    ppermute x18, waiting for transfers between devices: 14.3 us -> 13.3 us  [swap(): return lax.ppermute(value, ('row', 'col'), pairs)]
    pallas_call x6, Pallas kernels: 8.27 us -> 9.15 us  [product(): pl.pallas_call(lambda *refs: product_body(span, len(halves), len(rows), l...]
  transfers between devices with their start and end apart: 18 -> 18, of which waited for: 9 -> 8; matrix products, arithmetic and copies ran while one was open for 0% -> 0% of each run, Pallas kernels for 19% -> 21%
where the time goes in v1:
time: 63.1 us; the launch traced here: 62.9 us
  Pallas kernels  26.4 us (42%)
  starting transfers between devices  22.4 us (35%)
  waiting for transfers between devices  13.3 us (21%)
  between operations  0.91 us (1%)
    ppermute x18, starting transfers between devices, swap(): return lax.ppermute(value, ('row', 'col'), pairs)  22.4 us
    ppermute x18, waiting for transfers between devices, swap(): return lax.ppermute(value, ('row', 'col'), pairs)  13.3 us
    pallas_call x6, Pallas kernels, product(): pl.pallas_call(lambda *refs: product_body(span, len(halves), len(rows), l...  9.15 us
    pallas_call x1, Pallas kernels, upper_levels(): pl.pallas_call(lambda *refs: upper_body(picks.shape[0], *refs), out_shape...  5.76 us
    pallas_call x1, Pallas kernels, leaves(): pl.pallas_call(lambda *refs: leaves_body(len(others), *refs), out_shape=(...  5.41 us
    pallas_call x1, Pallas kernels, first_product(): pl.pallas_call(lambda *refs: first_product_body(gain, span, groups, len(p...  2.53 us
  transfers between devices with their start and end apart: 18, of which 8 were waited for; matrix products, arithmetic and copies ran while one was open for 0% of the time, Pallas kernels for 21%

profile of v1, /device:TPU:0, one launch (start us, length us, event | category | flops | bytes accessed | tf_op | source)
XLA Modules:
  0.0 62.9 jit_solution(15699551763971462223)
XLA Ops:
  0.6 1.3 %pack.1 = (bf16[560,256]{1,0:T(8,128)(2,1)S(1)}, bf16[544,256]{1,0:T(8,128)(2,1)S(1)}, bf16[16,256]{1,0:T(8,128)(2,1)S(1)}) custom-call(bf16[4,256,256]{2,1,0:T(8,128)(2,1)} %refs_0_.1, bf16[16,4,256]{2,1,0:T(4,128)(2,1)} %refs_1_.1, s32[2,64]{1,0:T(2,128)} %refs_2_.1, s32[1,64]{1,0:T(1,128)} %refs_3_.1, s32[4,64]{1,0:T(4,128)} %refs_4_.1, s32[2,64]{1,0:T(2,128)} %refs_5_.1), custom_call_target="tpu_custom_call" | custom-call | flops 1000000000 | tf_op jit(solution)/shard_map/pack/pallas_call | solution.py:119
  1.9 3.1 %collective-permute-start.2 = (bf16[16,256]{1,0:T(8,128)(2,1)S(1)}, bf16[16,256]{1,0:T(8,128)(2,1)S(1)}, u32[]{:S(2)}, u32[]{:S(2)}) collective-permute-start(bf16[16,256]{1,0:T(8,128)(2,1)S(1)} %get-tuple-element.71), channel_id=1, source_target_pairs={{0,2},{1,3},{2,0},{3,1},{4,6},{5,7},{6,4},{7,5},{8,10},{9,11},{10,... | collective-permute-start | bytes 24584 | tf_op jit(solution)/shard_map/ppermute | solution.py:570
  5.0 1.5 %collective-permute-start.1 = (bf16[544,256]{1,0:T(8,128)(2,1)S(1)}, bf16[544,256]{1,0:T(8,128)(2,1)S(1)}, u32[]{:S(2)}, u32[]{:S(2)}) collective-permute-start(bf16[544,256]{1,0:T(8,128)(2,1)S(1)} %get-tuple-element.80.refs_1_), channel_id=1, source_target_pairs={{0,16},{1,17},{2,18},{3,19},{4,20},{5,21},{6,22},{7,23},{8,24},{9,... | collective-permute-start | bytes 835592 | tf_op jit(solution)/shard_map/ppermute | solution.py:570
  6.5 1.5 %collective-permute-start = (bf16[560,256]{1,0:T(8,128)(2,1)S(1)}, bf16[560,256]{1,0:T(8,128)(2,1)S(1)}, u32[]{:S(2)}, u32[]{:S(2)}) collective-permute-start(bf16[560,256]{1,0:T(8,128)(2,1)S(1)} %get-tuple-element.103.refs_0_.refs_3_), channel_id=1, source_target_pairs={{0,1},{1,0},{2,3},{3,2},{4,5},{5,4},{6,7},{7,6},{8,9},{9,8},{10,11... | collective-permute-start | bytes 860168 | tf_op jit(solution)/shard_map/ppermute | solution.py:570
  8.0 0.0 collective-permute-done.2
  8.0 2.6 %collective-permute-start.3 = (bf16[16,512]{1,0:T(8,128)(2,1)S(1)}, bf16[16,512]{1,0:T(8,128)(2,1)S(1)}, u32[]{:S(2)}, u32[]{:S(2)}) collective-permute-start(bf16[16,512]{1,0:T(8,128)(2,1)S(1)} %pad_maximum_fusion), channel_id=1, source_target_pairs={{0,4},{1,5},{2,6},{3,7},{4,0},{5,1},{6,2},{7,3},{8,12},{9,13},{10,... | collective-permute-start | bytes 49160 | tf_op jit(solution)/shard_map/ppermute | solution.py:570
  10.6 0.6 collective-permute-start.7
  11.1 1.5 %collective-permute-start.8 = (bf16[560,256]{1,0:T(8,128)(2,1)S(1)}, bf16[560,256]{1,0:T(8,128)(2,1)S(1)}, u32[]{:S(2)}, u32[]{:S(2)}) collective-permute-start(bf16[560,256]{1,0:T(8,128)(2,1)S(1)} %get-tuple-element.103.refs_0_.refs_3_), channel_id=1, source_target_pairs={{0,16},{1,17},{2,18},{3,19},{4,20},{5,21},{6,22},{7,23},{8,24},{9,... | collective-permute-start | bytes 860168 | tf_op jit(solution)/shard_map/ppermute | solution.py:570
  12.7 0.0 collective-permute-done.3
  12.7 0.0 collective-permute-start.4
  12.7 1.2 %collective-permute-done.4.refs_3_ = bf16[16,1024]{1,0:T(8,128)(2,1)S(1)} collective-permute-done((bf16[16,1024]{1,0:T(8,128)(2,1)S(1)}, bf16[16,1024]{1,0:T(8,128)(2,1)S(1)}, u32[]{:S(2)}, u32[]{:S(2)}) %collective-permute-start.4) | collective-permute-done | bytes 32800 | tf_op jit(solution)/shard_map/ppermute | solution.py:570
  13.9 2.5 %first_product.1 = (bf16[512,64]{1,0:T(8,128)(2,1)S(1)}, bf16[512,64]{1,0:T(8,128)(2,1)S(1)}, bf16[512,64]{1,0:T(8,128)(2,1)S(1)}, bf16[512,64]{1,0:T(8,128)(2,1...) custom-call(bf16[560,256]{1,0:T(8,128)(2,1)S(1)} %get-tuple-element.10, ...), custom_call_target="tpu_custom_call" | custom-call | flops 1000000000 | tf_op jit(solution)/shard_map/first_product/pallas_call | solution.py:180
  16.4 0.0 collective-permute-done.1.refs_1_
  16.4 0.0 collective-permute-done.refs_0_.refs_1_
  16.4 0.6 collective-permute-start.5
  17.1 1.5 %collective-permute-start.6 = (bf16[544,256]{1,0:T(8,128)(2,1)S(1)}, bf16[544,256]{1,0:T(8,128)(2,1)S(1)}, u32[]{:S(2)}, u32[]{:S(2)}) collective-permute-start(bf16[544,256]{1,0:T(8,128)(2,1)S(1)} %collective-permute-done.1.refs_1_), channel_id=1, source_target_pairs={{0,1},{1,0},{2,3},{3,2},{4,5},{5,4},{6,7},{7,6},{8,9},{9,8},{10,11... | collective-permute-start | bytes 835592 | tf_op jit(solution)/shard_map/ppermute | solution.py:570
  18.5 2.9 %product.6 = (f32[512,256]{1,0:T(8,128)S(1)}, f32[512,256]{1,0:T(8,128)S(1)}, f32[512,256]{1,0:T(8,128)S(1)}, f32[512,256]{1,0:T(8,128)S(1)}, bf16[64,1024]{1,0:T(8,128)(2,1)}) custom-call(bf16[560,256]{1,0:T(8,128)(2,1)S(1)} %collective-permute-done.refs_0_.refs_1_, bf16[544,256]{1,0:T(8,128)(2,1)S(1)} %collective-permute-done.1.refs_1_, ...), custom_call_target="tpu_custom_call" | custom-call | tf_op jit(solution)/shard_map/product/pallas_call | solution.py:212
  21.5 0.0 collective-permute-done.7.refs_0_
  21.5 0.0 collective-permute-done.8.refs_1_
  21.5 2.9 %product.7 = (f32[512,256]{1,0:T(8,128)S(1)}, f32[512,256]{1,0:T(8,128)S(1)}, f32[512,256]{1,0:T(8,128)S(1)}, f32[512,256]{1,0:T(8,128)S(1)}, bf16[64,1024]{1,0:T(8,128)(2,1)}) custom-call(bf16[544,256]{1,0:T(8,128)(2,1)S(1)} %collective-permute-done.7.refs_0_, bf16[560,256]{1,0:T(8,128)(2,1)S(1)} %collective-permute-done.8.refs_1_, ...), custom_call_target="tpu_custom_call" | custom-call | flops 1000000000 | tf_op jit(solution)/shard_map/product/pallas_call | solution.py:212
  24.4 1.2 %skeletons.1 = (bf16[6,64,128]{2,1,0:T(8,128)(2,1)S(1)}, bf16[192,384]{1,0:T(8,128)(2,1)S(1)}, bf16[192,384]{1,0:T(8,128)(2,1)S(1)}, bf16[16,128]{1,0:T(8,128)(2,1)S(1)}) custom-call(bf16[560,256]{1,0:T(8,128)(2,1)S(1)} %get-tuple-element.103.refs_0_.refs_3_, bf16[560,256]{1,0:T(8,128)(2,1)S(1)} %collective-permute-done.refs_0_.refs_1_), custom_call_target="tpu_custom_call" | custom-call | flops 1000000000 | tf_op jit(solution)/shard_map/skeletons/pallas_call | solution.py:522
  25.6 0.9 %collective-permute-done.6.refs_1_ = bf16[544,256]{1,0:T(8,128)(2,1)S(1)} collective-permute-done((bf16[544,256]{1,0:T(8,128)(2,1)S(1)}, bf16[544,256]{1,0:T(8,128)(2,1)S(1)}, u32[]{:S(2)}, u32[]{:S(2)}) %collective-permute-start.6) | collective-permute-done | bytes 278560 | tf_op jit(solution)/shard_map/ppermute | solution.py:570
  26.5 0.0 collective-permute-done.5.refs_0_
  26.5 0.8 %product.8 = (f32[512,256]{1,0:T(8,128)S(1)}, bf16[64,1024]{1,0:T(8,128)(2,1)S(1)}) custom-call(bf16[560,256]{1,0:T(8,128)(2,1)S(1)} %collective-permute-done.5.refs_0_, bf16[544,256]{1,0:T(8,128)(2,1)S(1)} %collective-permute-done.6.refs_1_, bf16[512,64]{1,0:T(8,128)(2,1)S(1)} %get-tuple-element.84.refs_5_.refs_2_, f32[512,256]{1,0:T(8,128)S(1)} %get-tuple-element.110.refs_3_), custom_call_target="tpu_custom_call" | custom-call | flops 1000000000 | tf_op jit(solution)/shard_map/product/pallas_call | solution.py:212
  27.3 0.1 collective-permute-start.9
  27.4 0.8 %product.11 = f32[512,256]{1,0:T(8,128)S(1)} custom-call(bf16[560,256]{1,0:T(8,128)(2,1)S(1)} %collective-permute-done.5.refs_0_, bf16[544,256]{1,0:T(8,128)(2,1)S(1)} %collective-permute-done.6.refs_1_, bf16[512,64]{1,0:T(8,128)(2,1)S(1)} %get-tuple-element.83.refs_4_.refs_2_, f32[512,256]{1,0:T(8,128)S(1)} %get-tuple-element.115.refs_3_, ...), custom_call_target="tpu_custom_call" | custom-call | flops 1000000000 | tf_op jit(solution)/shard_map/product/pallas_call | solution.py:212
  28.2 0.8 %product.10.refs_0_ = f32[512,256]{1,0:T(8,128)S(1)} custom-call(bf16[560,256]{1,0:T(8,128)(2,1)S(1)} %collective-permute-done.5.refs_0_, bf16[544,256]{1,0:T(8,128)(2,1)S(1)} %collective-permute-done.6.refs_1_, bf16[512,64]{1,0:T(8,128)(2,1)S(1)} %get-tuple-element.82.refs_3_.refs_2_, f32[512,256]{1,0:T(8,128)S(1)} %get-tuple-element.112.refs_3_, ...), custom_call_target="tpu_custom_call" | custom-call | flops 1000000000 | tf_op jit(solution)/shard_map/product/pallas_call | solution.py:212
  29.0 0.2 collective-permute-done.9.refs_1_
  29.3 0.1 add_up.3
  29.3 0.3 collective-permute-start.10
  29.7 0.7 %collective-permute-start.11 = (bf16[256,256]{1,0:T(8,128)(2,1)S(1)}, bf16[256,256]{1,0:T(8,128)(2,1)S(1)}, u32[]{:S(2)}, u32[]{:S(2)}) collective-permute-start(bf16[256,256]{1,0:T(8,128)(2,1)S(1)} %get-tuple-element.120), channel_id=1, source_target_pairs={{0,2},{1,3},{2,0},{3,1},{4,6},{5,7},{6,4},{7,5},{8,10},{9,11},{10,... | collective-permute-start | bytes 393224 | tf_op jit(solution)/shard_map/ppermute | solution.py:570
  30.4 0.8 %product.9.refs_0_ = f32[512,256]{1,0:T(8,128)S(1)} custom-call(bf16[560,256]{1,0:T(8,128)(2,1)S(1)} %collective-permute-done.5.refs_0_, bf16[544,256]{1,0:T(8,128)(2,1)S(1)} %collective-permute-done.6.refs_1_, bf16[512,64]{1,0:T(8,128)(2,1)S(1)} %get-tuple-element.79.refs_2_, f32[512,256]{1,0:T(8,128)S(1)} %get-tuple-element.109.refs_3_, ...), custom_call_target="tpu_custom_call" | custom-call | flops 1000000000 | tf_op jit(solution)/shard_map/product/pallas_call | solution.py:212
  31.2 1.4 %collective-permute-start.14 = (bf16[16,128]{1,0:T(8,128)(2,1)S(1)}, bf16[16,128]{1,0:T(8,128)(2,1)S(1)}, u32[]{:S(2)}, u32[]{:S(2)}) collective-permute-start(bf16[16,128]{1,0:T(8,128)(2,1)S(1)} %get-tuple-element.124.refs_0_), channel_id=1, source_target_pairs={{0,2},{1,3},{2,0},{3,1},{4,6},{5,7},{6,4},{7,5},{8,10},{9,11},{10,... | collective-permute-start | bytes 12296 | tf_op jit(solution)/shard_map/ppermute | solution.py:570
  32.6 0.0 collective-permute-done.10.refs_1_
  32.6 0.1 add_up.4
  32.7 0.8 %collective-permute-start.13 = (bf16[256,256]{1,0:T(8,128)(2,1)S(1)}, bf16[256,256]{1,0:T(8,128)(2,1)S(1)}, u32[]{:S(2)}, u32[]{:S(2)}) collective-permute-start(bf16[256,256]{1,0:T(8,128)(2,1)S(1)} %get-tuple-element.121.refs_2_), channel_id=1, source_target_pairs={{0,2},{1,3},{2,0},{3,1},{4,6},{5,7},{6,4},{7,5},{8,10},{9,11},{10,... | collective-permute-start | bytes 393224 | tf_op jit(solution)/shard_map/ppermute | solution.py:570
  33.4 2.2 %collective-permute-done.11.refs_1_ = bf16[256,256]{1,0:T(8,128)(2,1)S(1)} collective-permute-done((bf16[256,256]{1,0:T(8,128)(2,1)S(1)}, bf16[256,256]{1,0:T(8,128)(2,1)S(1)}, u32[]{:S(2)}, u32[]{:S(2)}) %collective-permute-start.11) | collective-permute-done | bytes 131104 | tf_op jit(solution)/shard_map/ppermute | solution.py:570
  35.6 2.6 %collective-permute-start.12 = (bf16[256,256]{1,0:T(8,128)(2,1)S(1)}, bf16[256,256]{1,0:T(8,128)(2,1)S(1)}, u32[]{:S(2)}, u32[]{:S(2)}) collective-permute-start(bf16[256,256]{1,0:T(8,128)(2,1)S(1)} %add_up.5), channel_id=1, source_target_pairs={{0,4},{1,5},{2,6},{3,7},{4,0},{5,1},{6,2},{7,3},{8,12},{9,13},{10,... | collective-permute-start | bytes 393224 | tf_op jit(solution)/shard_map/ppermute | solution.py:570
  38.3 0.0 collective-permute-done.14.refs_1_
  38.3 0.9 %top_couplings.1 = (bf16[192,384]{1,0:T(8,128)(2,1)S(1)}, bf16[192,384]{1,0:T(8,128)(2,1)S(1)}) custom-call(bf16[16,128]{1,0:T(8,128)(2,1)S(1)} %get-tuple-element.124.refs_0_, bf16[16,128]{1,0:T(8,128)(2,1)S(1)} %collective-permute-done.14.refs_1_, bf16[6,64,128]{2,1,0:T(8,128)(2,1)S(1)} %get-tuple-element.122.refs_2_.refs_4_.refs_5_), custom_call_target="tpu_custom_call" | custom-call | flops 10000000000 | tf_op jit(solution)/shard_map/top_couplings/pallas_call | solution.py:549
  39.2 4.7 %collective-permute-done.12.refs_1_ = bf16[256,256]{1,0:T(8,128)(2,1)S(1)} collective-permute-done((bf16[256,256]{1,0:T(8,128)(2,1)S(1)}, bf16[256,256]{1,0:T(8,128)(2,1)S(1)}, u32[]{:S(2)}, u32[]{:S(2)}) %collective-permute-start.12) | collective-permute-done | bytes 131104 | tf_op jit(solution)/shard_map/ppermute | solution.py:570
  43.9 0.0 collective-permute-done.13.refs_2_
  43.9 5.4 %leaves.1 = (f32[2,64,128]{2,1,0:T(8,128)}, f32[64,128]{1,0:T(8,128)S(1)}, f32[64,256]{1,0:T(8,128)S(1)}, f32[64,256]{1,0:T(8,128)S(1)}, bf16[192,256]{1,0:T(8,128)(2,1)S(1)}) custom-call(f32[256,256]{1,0:T(8,128)S(1)} %get-tuple-element.118.refs_0_, bf16[256,256]{1,0:T(8,128)(2,1)S(1)} %collective-permute-done.12.refs_1_, ...), custom_call_target="tpu_custom_call" | custom-call | flops 1000000000 | tf_op jit(solution)/shard_map/leaves/pallas_call | solution.py:369
  49.4 0.9 %collective-permute-start.17 = (bf16[192,256]{1,0:T(8,128)(2,1)S(1)}, bf16[192,256]{1,0:T(8,128)(2,1)S(1)}, u32[]{:S(2)}, u32[]{:S(2)}) collective-permute-start(bf16[192,256]{1,0:T(8,128)(2,1)S(1)} %get-tuple-element.130), channel_id=1, source_target_pairs={{0,3},{1,2},{2,1},{3,0},{4,7},{5,6},{6,5},{7,4},{8,11},{9,10},{10,... | collective-permute-start | bytes 294920 | tf_op jit(solution)/shard_map/ppermute | solution.py:570
  50.2 2.1 %collective-permute-start.16 = (bf16[192,256]{1,0:T(8,128)(2,1)S(1)}, bf16[192,256]{1,0:T(8,128)(2,1)S(1)}, u32[]{:S(2)}, u32[]{:S(2)}) collective-permute-start(bf16[192,256]{1,0:T(8,128)(2,1)S(1)} %get-tuple-element.130), channel_id=1, source_target_pairs={{0,2},{1,3},{2,0},{3,1},{4,6},{5,7},{6,4},{7,5},{8,10},{9,11},{10,... | collective-permute-start | bytes 294920 | tf_op jit(solution)/shard_map/ppermute | solution.py:570
  52.4 0.5 collective-permute-start.15
  52.9 2.0 %collective-permute-done.17.refs_4_ = bf16[192,256]{1,0:T(8,128)(2,1)S(1)} collective-permute-done((bf16[192,256]{1,0:T(8,128)(2,1)S(1)}, bf16[192,256]{1,0:T(8,128)(2,1)S(1)}, u32[]{:S(2)}, u32[]{:S(2)}) %collective-permute-start.17) | collective-permute-done | bytes 98336 | tf_op jit(solution)/shard_map/ppermute | solution.py:570
  54.9 1.1 %collective-permute-done.16.refs_3_ = bf16[192,256]{1,0:T(8,128)(2,1)S(1)} collective-permute-done((bf16[192,256]{1,0:T(8,128)(2,1)S(1)}, bf16[192,256]{1,0:T(8,128)(2,1)S(1)}, u32[]{:S(2)}, u32[]{:S(2)}) %collective-permute-start.16) | collective-permute-done | bytes 98336 | tf_op jit(solution)/shard_map/ppermute | solution.py:570
  56.0 1.0 %collective-permute-done.15.refs_2_ = bf16[192,256]{1,0:T(8,128)(2,1)S(1)} collective-permute-done((bf16[192,256]{1,0:T(8,128)(2,1)S(1)}, bf16[192,256]{1,0:T(8,128)(2,1)S(1)}, u32[]{:S(2)}, u32[]{:S(2)}) %collective-permute-start.15) | collective-permute-done | bytes 98336 | tf_op jit(solution)/shard_map/ppermute | solution.py:570
  57.0 5.8 %upper_levels.1 = (f32[3,1,64,128]{3,2,1,0:T(8,128)}, f32[2,1,64,256]{3,2,1,0:T(8,128)}) custom-call(f32[64,256]{1,0:T(8,128)S(1)} %get-tuple-element.128.refs_0_, f32[64,256]{1,0:T(8,128)S(1)} %get-tuple-element.129.refs_1_, bf16[192,256]{1,0:T(8,128)(2,1)S(1)} %collective-permute-done.15.refs_2_, bf16[192,256]{1,0:T(8,128)(2,1)S(1)} %collective-permute-done.16.refs_3_, ...), custom_call_target="tpu_custom_call" | custom-call | flops 1000000000 | tf_op jit(solution)/shard_map/upper_levels/pallas_call | solution.py:445
  (4 shorter events, 0.0 us)
Async XLA Ops:
  1.9 6.1 %collective-permute-start.2 = (bf16[16,256]{1,0:T(8,128)(2,1)S(1)}, bf16[16,256]{1,0:T(8,128)(2,1)S(1)}, u32[]{:S(2)}, u32[]{:S(2)}) collective-permute-start(bf16[16,256]{1,0:T(8,128)(2,1)S(1)} %get-tuple-element.71), channel_id=1, source_target_pairs={{0,2},{1,3},{2,0},{3,1},{4,6},{5,7},{6,4},{7,5},{8,10},{9,11},{10,... | collective-permute-start | bytes 24584 | tf_op jit(solution)/shard_map/ppermute | solution.py:570
  5.0 11.4 %collective-permute-start.1 = (bf16[544,256]{1,0:T(8,128)(2,1)S(1)}, bf16[544,256]{1,0:T(8,128)(2,1)S(1)}, u32[]{:S(2)}, u32[]{:S(2)}) collective-permute-start(bf16[544,256]{1,0:T(8,128)(2,1)S(1)} %get-tuple-element.80.refs_1_), channel_id=1, source_target_pairs={{0,16},{1,17},{2,18},{3,19},{4,20},{5,21},{6,22},{7,23},{8,24},{9,... | collective-permute-start | bytes 835592 | tf_op jit(solution)/shard_map/ppermute | solution.py:570
  6.5 9.9 %collective-permute-start = (bf16[560,256]{1,0:T(8,128)(2,1)S(1)}, bf16[560,256]{1,0:T(8,128)(2,1)S(1)}, u32[]{:S(2)}, u32[]{:S(2)}) collective-permute-start(bf16[560,256]{1,0:T(8,128)(2,1)S(1)} %get-tuple-element.103.refs_0_.refs_3_), channel_id=1, source_target_pairs={{0,1},{1,0},{2,3},{3,2},{4,5},{5,4},{6,7},{7,6},{8,9},{9,8},{10,11... | collective-permute-start | bytes 860168 | tf_op jit(solution)/shard_map/ppermute | solution.py:570
  8.0 4.7 %collective-permute-start.3 = (bf16[16,512]{1,0:T(8,128)(2,1)S(1)}, bf16[16,512]{1,0:T(8,128)(2,1)S(1)}, u32[]{:S(2)}, u32[]{:S(2)}) collective-permute-start(bf16[16,512]{1,0:T(8,128)(2,1)S(1)} %pad_maximum_fusion), channel_id=1, source_target_pairs={{0,4},{1,5},{2,6},{3,7},{4,0},{5,1},{6,2},{7,3},{8,12},{9,13},{10,... | collective-permute-start | bytes 49160 | tf_op jit(solution)/shard_map/ppermute | solution.py:570
  10.6 10.9 %collective-permute-start.7 = (bf16[544,256]{1,0:T(8,128)(2,1)S(1)}, bf16[544,256]{1,0:T(8,128)(2,1)S(1)}, u32[]{:S(2)}, u32[]{:S(2)}) collective-permute-start(bf16[544,256]{1,0:T(8,128)(2,1)S(1)} %get-tuple-element.80.refs_1_), channel_id=1, source_target_pairs={{0,1},{1,0},{2,3},{3,2},{4,5},{5,4},{6,7},{7,6},{8,9},{9,8},{10,11... | collective-permute-start | bytes 835592 | tf_op jit(solution)/shard_map/ppermute | solution.py:570
  11.1 10.3 %collective-permute-start.8 = (bf16[560,256]{1,0:T(8,128)(2,1)S(1)}, bf16[560,256]{1,0:T(8,128)(2,1)S(1)}, u32[]{:S(2)}, u32[]{:S(2)}) collective-permute-start(bf16[560,256]{1,0:T(8,128)(2,1)S(1)} %get-tuple-element.103.refs_0_.refs_3_), channel_id=1, source_target_pairs={{0,16},{1,17},{2,18},{3,19},{4,20},{5,21},{6,22},{7,23},{8,24},{9,... | collective-permute-start | bytes 860168 | tf_op jit(solution)/shard_map/ppermute | solution.py:570
  12.7 1.2 %collective-permute-start.4 = (bf16[16,1024]{1,0:T(8,128)(2,1)S(1)}, bf16[16,1024]{1,0:T(8,128)(2,1)S(1)}, u32[]{:S(2)}, u32[]{:S(2)}) collective-permute-start(bf16[16,1024]{1,0:T(8,128)(2,1)S(1)} %constant_dynamic-update-slice_fusion.refs_2_), channel_id=1, source_target_pairs={{0,8},{1,9},{2,10},{3,11},{4,12},{5,13},{6,14},{7,15},{8,0},{9,1},... | collective-permute-start | bytes 98312 | tf_op jit(solution)/shard_map/ppermute | solution.py:570
  16.4 10.0 %collective-permute-start.5 = (bf16[560,256]{1,0:T(8,128)(2,1)S(1)}, bf16[560,256]{1,0:T(8,128)(2,1)S(1)}, u32[]{:S(2)}, u32[]{:S(2)}) collective-permute-start(bf16[560,256]{1,0:T(8,128)(2,1)S(1)} %collective-permute-done.refs_0_.refs_1_), channel_id=1, source_target_pairs={{0,16},{1,17},{2,18},{3,19},{4,20},{5,21},{6,22},{7,23},{8,24},{9,... | collective-permute-start | bytes 860168 | tf_op jit(solution)/shard_map/ppermute | solution.py:570
  17.1 9.4 %collective-permute-start.6 = (bf16[544,256]{1,0:T(8,128)(2,1)S(1)}, bf16[544,256]{1,0:T(8,128)(2,1)S(1)}, u32[]{:S(2)}, u32[]{:S(2)}) collective-permute-start(bf16[544,256]{1,0:T(8,128)(2,1)S(1)} %collective-permute-done.1.refs_1_), channel_id=1, source_target_pairs={{0,1},{1,0},{2,3},{3,2},{4,5},{5,4},{6,7},{7,6},{8,9},{9,8},{10,11... | collective-permute-start | bytes 835592 | tf_op jit(solution)/shard_map/ppermute | solution.py:570
  27.3 2.0 %collective-permute-start.9 = (f32[512,256]{1,0:T(8,128)S(1)}, f32[512,256]{1,0:T(8,128)S(1)}, u32[]{:S(2)}, u32[]{:S(2)}) collective-permute-start(f32[512,256]{1,0:T(8,128)S(1)} %get-tuple-element.113), channel_id=1, source_target_pairs={{0,8},{1,9},{2,10},{3,11},{4,12},{5,13},{6,14},{7,15},{8,0},{9,1},... | collective-permute-start | bytes 1572872 | tf_op jit(solution)/shard_map/ppermute | solution.py:570
  29.3 3.3 %collective-permute-start.10 = (f32[512,256]{1,0:T(8,128)S(1)}, f32[512,256]{1,0:T(8,128)S(1)}, u32[]{:S(2)}, u32[]{:S(2)}) collective-permute-start(f32[512,256]{1,0:T(8,128)S(1)} %product.11), channel_id=1, source_target_pairs={{0,8},{1,9},{2,10},{3,11},{4,12},{5,13},{6,14},{7,15},{8,0},{9,1},... | collective-permute-start | bytes 1572872 | tf_op jit(solution)/shard_map/ppermute | solution.py:570
  29.7 5.9 %collective-permute-start.11 = (bf16[256,256]{1,0:T(8,128)(2,1)S(1)}, bf16[256,256]{1,0:T(8,128)(2,1)S(1)}, u32[]{:S(2)}, u32[]{:S(2)}) collective-permute-start(bf16[256,256]{1,0:T(8,128)(2,1)S(1)} %get-tuple-element.120), channel_id=1, source_target_pairs={{0,2},{1,3},{2,0},{3,1},{4,6},{5,7},{6,4},{7,5},{8,10},{9,11},{10,... | collective-permute-start | bytes 393224 | tf_op jit(solution)/shard_map/ppermute | solution.py:570
  31.2 7.1 %collective-permute-start.14 = (bf16[16,128]{1,0:T(8,128)(2,1)S(1)}, bf16[16,128]{1,0:T(8,128)(2,1)S(1)}, u32[]{:S(2)}, u32[]{:S(2)}) collective-permute-start(bf16[16,128]{1,0:T(8,128)(2,1)S(1)} %get-tuple-element.124.refs_0_), channel_id=1, source_target_pairs={{0,2},{1,3},{2,0},{3,1},{4,6},{5,7},{6,4},{7,5},{8,10},{9,11},{10,... | collective-permute-start | bytes 12296 | tf_op jit(solution)/shard_map/ppermute | solution.py:570
  32.7 11.3 %collective-permute-start.13 = (bf16[256,256]{1,0:T(8,128)(2,1)S(1)}, bf16[256,256]{1,0:T(8,128)(2,1)S(1)}, u32[]{:S(2)}, u32[]{:S(2)}) collective-permute-start(bf16[256,256]{1,0:T(8,128)(2,1)S(1)} %get-tuple-element.121.refs_2_), channel_id=1, source_target_pairs={{0,2},{1,3},{2,0},{3,1},{4,6},{5,7},{6,4},{7,5},{8,10},{9,11},{10,... | collective-permute-start | bytes 393224 | tf_op jit(solution)/shard_map/ppermute | solution.py:570
  35.6 8.3 %collective-permute-start.12 = (bf16[256,256]{1,0:T(8,128)(2,1)S(1)}, bf16[256,256]{1,0:T(8,128)(2,1)S(1)}, u32[]{:S(2)}, u32[]{:S(2)}) collective-permute-start(bf16[256,256]{1,0:T(8,128)(2,1)S(1)} %add_up.5), channel_id=1, source_target_pairs={{0,4},{1,5},{2,6},{3,7},{4,0},{5,1},{6,2},{7,3},{8,12},{9,13},{10,... | collective-permute-start | bytes 393224 | tf_op jit(solution)/shard_map/ppermute | solution.py:570
  49.4 5.6 %collective-permute-start.17 = (bf16[192,256]{1,0:T(8,128)(2,1)S(1)}, bf16[192,256]{1,0:T(8,128)(2,1)S(1)}, u32[]{:S(2)}, u32[]{:S(2)}) collective-permute-start(bf16[192,256]{1,0:T(8,128)(2,1)S(1)} %get-tuple-element.130), channel_id=1, source_target_pairs={{0,3},{1,2},{2,1},{3,0},{4,7},{5,6},{6,5},{7,4},{8,11},{9,10},{10,... | collective-permute-start | bytes 294920 | tf_op jit(solution)/shard_map/ppermute | solution.py:570
  50.2 5.8 %collective-permute-start.16 = (bf16[192,256]{1,0:T(8,128)(2,1)S(1)}, bf16[192,256]{1,0:T(8,128)(2,1)S(1)}, u32[]{:S(2)}, u32[]{:S(2)}) collective-permute-start(bf16[192,256]{1,0:T(8,128)(2,1)S(1)} %get-tuple-element.130), channel_id=1, source_target_pairs={{0,2},{1,3},{2,0},{3,1},{4,6},{5,7},{6,4},{7,5},{8,10},{9,11},{10,... | collective-permute-start | bytes 294920 | tf_op jit(solution)/shard_map/ppermute | solution.py:570
  52.4 4.6 %collective-permute-start.15 = (bf16[192,256]{1,0:T(8,128)(2,1)S(1)}, bf16[192,256]{1,0:T(8,128)(2,1)S(1)}, u32[]{:S(2)}, u32[]{:S(2)}) collective-permute-start(bf16[192,256]{1,0:T(8,128)(2,1)S(1)} %get-tuple-element.130), channel_id=1, source_target_pairs={{0,1},{1,0},{2,3},{3,2},{4,5},{5,4},{6,7},{7,6},{8,9},{9,8},{10,11... | collective-permute-start | bytes 294920 | tf_op jit(solution)/shard_map/ppermute | solution.py:570

commit v2 on v0

--- a/solution.py
+++ b/solution.py
@@ -233,18 +233,27 @@
     )(mine, theirs, *after)
 
 
-def wide_product(first, second, second_dim):
+def wide_product(first, second):
     high, middle, low = split(first)
     other_high, other_middle, other_low = split(second)
     return over(
         jnp.concatenate([high, high, middle, middle, low, high], axis=1),
         jnp.concatenate(
-            [other_high, other_middle, other_high, other_middle, other_high, other_low],
-            axis=second_dim,
+            [other_high, other_middle, other_high, other_middle, other_high, other_low], axis=1
         ),
         1,
-        second_dim,
-    )
+        1,
+    )
+
+
+def near_product(first, second):
+    high, middle, _ = split(first)
+    return over(jnp.concatenate([high, high, middle], axis=1), near_parts(second), 1, 0)
+
+
+def near_parts(second):
+    high, middle, _ = split(second)
+    return jnp.concatenate([high, middle, high], axis=0)
 
 
 def exact_product(first, second):
@@ -254,11 +263,12 @@
     )
 
 
-def twice_product(twice_parts, parts):
-    high, middle, low = twice_parts
+def twice_product(twice, twice_parts, parts):
+    high, middle, _ = twice_parts
     other_high, other_middle, other_low = parts
     left = lax.broadcasted_iota(jnp.int32, high.shape, 1) < high.shape[1] // 2
-    last = jnp.where(left, low.astype(F32), high.astype(F32)).astype(BF16)
+    low = twice - high.astype(F32) - middle.astype(F32)
+    last = jnp.where(left, low, high.astype(F32)).astype(BF16)
     return over(
         jnp.concatenate([high, middle, last], axis=1),
         jnp.concatenate(
@@ -282,7 +292,7 @@
     eyes = jnp.where((other == place) | (other == place + rank), 1.0, 0.0)
     states = []
     for skeleton, stack in zip(skeletons, stacks):
-        products = wide_product(skeleton, jnp.concatenate([stack, skeleton, skeleton], axis=0), 1)
+        products = wide_product(skeleton, jnp.concatenate([stack, skeleton, skeleton], axis=0))
         ridge = 0.05 * jnp.sum(skeleton * skeleton, keepdims=True) / rank + 1e-05
         inverse = 1.0 / (640.0 * ridge)
         states.append((products[:, :pool], eyes - products[:, pool:] * inverse, inverse))
@@ -294,7 +304,7 @@
             parts = split(solved)
             if not last:
                 parts = [jnp.concatenate(pair, axis=1) for pair in zip(parts, power_parts)]
-            both = twice_product(power_parts, parts)
+            both = twice_product(power, power_parts, parts)
             solved = solved + both[:, :pool] * (1.0 / tau)
             later.append((solved, None if last else 2.0 * both[:, pool:] - eyes, inverse))
         states = later
@@ -305,17 +315,14 @@
     stacks, skeletons = [], []
     for samples, reduced, coupling, picks in nodes:
         pool = samples.shape[0]
-        high, middle, low = split(reduced)
-        coupled = over(
-            coupling, jnp.concatenate([high, middle, high, middle, high, low], axis=0), 1, 0
-        )
+        coupled = over(coupling, near_parts(reduced), 1, 0)
         stacks.append(samples - coupled[:pool])
         skeletons.append(select_rows(picks, samples) - coupled[pool:])
     if early is not None:
         early(skeletons[0])
     interps = interpolate(stacks, skeletons)
     return [
-        (interp, skeleton, wide_product(interp, node[1], 0))
+        (interp, skeleton, near_product(interp, node[1]))
         for interp, skeleton, node in zip(interps, skeletons, nodes)
     ]
 
@@ -461,12 +468,12 @@
     upper = lax.broadcasted_iota(jnp.int32, entries.shape, 0) < rank
     entries = jnp.where(left == upper, 0.0, entries)
     chosen = select_rows(picks.T.astype(BF16), entries)
-    high, middle, low = split(jnp.concatenate([entries, chosen], axis=0))
-    couplings_ref[...] = jnp.concatenate([high, high, middle, middle, low, high], axis=1)
+    high, middle, _ = split(jnp.concatenate([entries, chosen], axis=0))
+    couplings_ref[...] = jnp.concatenate([high, high, middle], axis=1)
 
 
 def coupling_shape(rank):
-    return vmem((3 * rank, 12 * rank), BF16)
+    return vmem((3 * rank, 6 * rank), BF16)
 
 
 def skeletons_body(gain, span, counts, mine_ref, beside_ref, *refs):
@@ -594,10 +601,9 @@
         pieces += more
     (theirs,) = product(diagonal, feats[3:], totals[3:], span)
     from_sibling = swap(theirs, 1, 0)
-    (mine,) = product(diagonal, feats[1:2], totals[1:2], span)
+    mine, theirs = product(diagonal, feats[1:3], totals[1:3], span)
     outs = [(range(0, line - 2, 2), F32), (range(1, line - 2, 2), BF16)]
     kept, sent = add_up(mine, from_sibling, outs, span)
-    (theirs,) = product(diagonal, feats[2:3], totals[2:3], span)
     sent, theirs, points_two = lax.optimization_barrier((sent, theirs, points_two))
     arrived = swap(sent, 0, 2)
     from_sibling = swap(theirs, 1, 0)

time: 63.4 us -> 63.2 us (level)
    pallas_call x6 -> x5, Pallas kernels: 8.27 us -> 8.01 us  [product(): pl.pallas_call(lambda *refs: product_body(span, len(halves), len(rows), *...]
where the time goes in v2:
time: 63.2 us; the launch traced here: 63 us
  Pallas kernels  25.2 us (40%)
  starting transfers between devices  22.1 us (35%)
  waiting for transfers between devices  14.8 us (23%)
  between operations  0.91 us (1%)
    ppermute x18, starting transfers between devices, swap(): return lax.ppermute(value, ('row', 'col'), pairs)  22.1 us
    ppermute x18, waiting for transfers between devices, swap(): return lax.ppermute(value, ('row', 'col'), pairs)  14.8 us
    pallas_call x5, Pallas kernels, product(): pl.pallas_call(lambda *refs: product_body(span, len(halves), len(rows), *...  8.01 us
    pallas_call x1, Pallas kernels, upper_levels(): pl.pallas_call(lambda *refs: upper_body(picks.shape[0], *refs), out_shape...  5.76 us
    pallas_call x1, Pallas kernels, leaves(): pl.pallas_call(lambda *refs: leaves_body(len(others), *refs), out_shape=(...  5.42 us
    pallas_call x1, Pallas kernels, first_product(): pl.pallas_call(lambda *refs: first_product_body(gain, span, groups, len(p...  2.53 us
  transfers between devices with their start and end apart: 18, of which 9 were waited for; matrix products, arithmetic and copies ran while one was open for 0% of the time, Pallas kernels for 19%

profile of v2, /device:TPU:0, one launch (start us, length us, event | category | flops | bytes accessed | tf_op | source)
XLA Modules:
  0.0 63.0 jit_solution(2132298412576161996)
XLA Ops:
  0.6 1.3 %pack.1 = (bf16[560,256]{1,0:T(8,128)(2,1)S(1)}, bf16[544,256]{1,0:T(8,128)(2,1)S(1)}, bf16[16,256]{1,0:T(8,128)(2,1)S(1)}) custom-call(bf16[4,256,256]{2,1,0:T(8,128)(2,1)} %refs_0_.1, bf16[16,4,256]{2,1,0:T(4,128)(2,1)} %refs_1_.1, s32[2,64]{1,0:T(2,128)} %refs_2_.1, s32[1,64]{1,0:T(1,128)} %refs_3_.1, s32[4,64]{1,0:T(4,128)} %refs_4_.1, s32[2,64]{1,0:T(2,128)} %refs_5_.1), custom_call_target="tpu_custom_call" | custom-call | flops 1000000000 | tf_op jit(solution)/shard_map/pack/pallas_call | solution.py:119
  1.9 3.1 %collective-permute-start.2 = (bf16[16,256]{1,0:T(8,128)(2,1)S(1)}, bf16[16,256]{1,0:T(8,128)(2,1)S(1)}, u32[]{:S(2)}, u32[]{:S(2)}) collective-permute-start(bf16[16,256]{1,0:T(8,128)(2,1)S(1)} %get-tuple-element.71), channel_id=1, source_target_pairs={{0,2},{1,3},{2,0},{3,1},{4,6},{5,7},{6,4},{7,5},{8,10},{9,11},{10,... | collective-permute-start | bytes 24584 | tf_op jit(solution)/shard_map/ppermute | solution.py:565
  5.0 1.5 %collective-permute-start.1 = (bf16[544,256]{1,0:T(8,128)(2,1)S(1)}, bf16[544,256]{1,0:T(8,128)(2,1)S(1)}, u32[]{:S(2)}, u32[]{:S(2)}) collective-permute-start(bf16[544,256]{1,0:T(8,128)(2,1)S(1)} %get-tuple-element.80.refs_1_), channel_id=1, source_target_pairs={{0,16},{1,17},{2,18},{3,19},{4,20},{5,21},{6,22},{7,23},{8,24},{9,... | collective-permute-start | bytes 835592 | tf_op jit(solution)/shard_map/ppermute | solution.py:565
  6.5 1.5 %collective-permute-start = (bf16[560,256]{1,0:T(8,128)(2,1)S(1)}, bf16[560,256]{1,0:T(8,128)(2,1)S(1)}, u32[]{:S(2)}, u32[]{:S(2)}) collective-permute-start(bf16[560,256]{1,0:T(8,128)(2,1)S(1)} %get-tuple-element.103.refs_0_.refs_3_), channel_id=1, source_target_pairs={{0,1},{1,0},{2,3},{3,2},{4,5},{5,4},{6,7},{7,6},{8,9},{9,8},{10,11... | collective-permute-start | bytes 860168 | tf_op jit(solution)/shard_map/ppermute | solution.py:565
  8.0 0.0 collective-permute-done.2
  8.0 2.6 %collective-permute-start.3 = (bf16[16,512]{1,0:T(8,128)(2,1)S(1)}, bf16[16,512]{1,0:T(8,128)(2,1)S(1)}, u32[]{:S(2)}, u32[]{:S(2)}) collective-permute-start(bf16[16,512]{1,0:T(8,128)(2,1)S(1)} %pad_maximum_fusion), channel_id=1, source_target_pairs={{0,4},{1,5},{2,6},{3,7},{4,0},{5,1},{6,2},{7,3},{8,12},{9,13},{10,... | collective-permute-start | bytes 49160 | tf_op jit(solution)/shard_map/ppermute | solution.py:565
  10.6 0.6 collective-permute-start.7
  11.1 1.5 %collective-permute-start.8 = (bf16[560,256]{1,0:T(8,128)(2,1)S(1)}, bf16[560,256]{1,0:T(8,128)(2,1)S(1)}, u32[]{:S(2)}, u32[]{:S(2)}) collective-permute-start(bf16[560,256]{1,0:T(8,128)(2,1)S(1)} %get-tuple-element.103.refs_0_.refs_3_), channel_id=1, source_target_pairs={{0,16},{1,17},{2,18},{3,19},{4,20},{5,21},{6,22},{7,23},{8,24},{9,... | collective-permute-start | bytes 860168 | tf_op jit(solution)/shard_map/ppermute | solution.py:565
  12.7 0.0 collective-permute-done.3
  12.7 0.0 collective-permute-start.4
  12.7 1.2 %collective-permute-done.4.refs_3_ = bf16[16,1024]{1,0:T(8,128)(2,1)S(1)} collective-permute-done((bf16[16,1024]{1,0:T(8,128)(2,1)S(1)}, bf16[16,1024]{1,0:T(8,128)(2,1)S(1)}, u32[]{:S(2)}, u32[]{:S(2)}) %collective-permute-start.4) | collective-permute-done | bytes 32800 | tf_op jit(solution)/shard_map/ppermute | solution.py:565
  13.9 2.5 %first_product.1 = (bf16[512,64]{1,0:T(8,128)(2,1)S(1)}, bf16[512,64]{1,0:T(8,128)(2,1)S(1)}, bf16[512,64]{1,0:T(8,128)(2,1)S(1)}, bf16[512,64]{1,0:T(8,128)(2,1...) custom-call(bf16[560,256]{1,0:T(8,128)(2,1)S(1)} %get-tuple-element.10, ...), custom_call_target="tpu_custom_call" | custom-call | flops 1000000000 | tf_op jit(solution)/shard_map/first_product/pallas_call | solution.py:180
  16.4 0.0 collective-permute-done.1.refs_1_
  16.4 0.0 collective-permute-done.refs_0_.refs_1_
  16.4 0.6 collective-permute-start.5
  17.1 1.5 %collective-permute-start.6 = (bf16[544,256]{1,0:T(8,128)(2,1)S(1)}, bf16[544,256]{1,0:T(8,128)(2,1)S(1)}, u32[]{:S(2)}, u32[]{:S(2)}) collective-permute-start(bf16[544,256]{1,0:T(8,128)(2,1)S(1)} %collective-permute-done.1.refs_1_), channel_id=1, source_target_pairs={{0,1},{1,0},{2,3},{3,2},{4,5},{5,4},{6,7},{7,6},{8,9},{9,8},{10,11... | collective-permute-start | bytes 835592 | tf_op jit(solution)/shard_map/ppermute | solution.py:565
  18.5 2.5 %product.5 = (f32[512,256]{1,0:T(8,128)S(1)}, f32[512,256]{1,0:T(8,128)S(1)}, f32[512,256]{1,0:T(8,128)S(1)}, f32[512,256]{1,0:T(8,128)S(1)}) custom-call(bf16[560,256]{1,0:T(8,128)(2,1)S(1)} %collective-permute-done.refs_0_.refs_1_, bf16[544,256]{1,0:T(8,128)(2,1)S(1)} %collective-permute-done.1.refs_1_, bf16[512,64]{1,0:T(8,128)(2,1)S(1)} %get-tuple-element.79.refs_2_, ...), custom_call_target="tpu_custom_call" | custom-call | tf_op jit(solution)/shard_map/product/pallas_call | solution.py:207
  21.0 0.3 collective-permute-done.7.refs_0_
  21.4 0.0 collective-permute-done.8.refs_1_
  21.4 2.5 %product.6 = (f32[512,256]{1,0:T(8,128)S(1)}, f32[512,256]{1,0:T(8,128)S(1)}, f32[512,256]{1,0:T(8,128)S(1)}, f32[512,256]{1,0:T(8,128)S(1)}) custom-call(bf16[544,256]{1,0:T(8,128)(2,1)S(1)} %collective-permute-done.7.refs_0_, bf16[560,256]{1,0:T(8,128)(2,1)S(1)} %collective-permute-done.8.refs_1_, bf16[512,64]{1,0:T(8,128)(2,1)S(1)} %get-tuple-element.79.refs_2_, ...), custom_call_target="tpu_custom_call" | custom-call | flops 1000000000 | tf_op jit(solution)/shard_map/product/pallas_call | solution.py:207
  23.9 1.2 %skeletons.1 = (bf16[6,64,128]{2,1,0:T(8,128)(2,1)S(1)}, bf16[192,384]{1,0:T(8,128)(2,1)S(1)}, bf16[192,384]{1,0:T(8,128)(2,1)S(1)}, bf16[16,128]{1,0:T(8,128)(2,1)S(1)}) custom-call(bf16[560,256]{1,0:T(8,128)(2,1)S(1)} %get-tuple-element.103.refs_0_.refs_3_, bf16[560,256]{1,0:T(8,128)(2,1)S(1)} %collective-permute-done.refs_0_.refs_1_), custom_call_target="tpu_custom_call" | custom-call | flops 1000000000 | tf_op jit(solution)/shard_map/skeletons/pallas_call | solution.py:517
  25.0 1.4 %collective-permute-done.6.refs_1_ = bf16[544,256]{1,0:T(8,128)(2,1)S(1)} collective-permute-done((bf16[544,256]{1,0:T(8,128)(2,1)S(1)}, bf16[544,256]{1,0:T(8,128)(2,1)S(1)}, u32[]{:S(2)}, u32[]{:S(2)}) %collective-permute-start.6) | collective-permute-done | bytes 278560 | tf_op jit(solution)/shard_map/ppermute | solution.py:565
  26.5 0.0 collective-permute-done.5.refs_0_
  26.5 0.8 %product.9 = f32[512,256]{1,0:T(8,128)S(1)} custom-call(bf16[560,256]{1,0:T(8,128)(2,1)S(1)} %collective-permute-done.5.refs_0_, bf16[544,256]{1,0:T(8,128)(2,1)S(1)} %collective-permute-done.6.refs_1_, bf16[512,64]{1,0:T(8,128)(2,1)S(1)} %get-tuple-element.84.refs_5_.refs_2_, f32[512,256]{1,0:T(8,128)S(1)} %get-tuple-element.113.refs_3_), custom_call_target="tpu_custom_call" | custom-call | flops 1000000000 | tf_op jit(solution)/shard_map/product/pallas_call | solution.py:207
  27.3 0.1 collective-permute-start.9
  27.4 1.4 %product.8 = (f32[512,256]{1,0:T(8,128)S(1)}, f32[512,256]{1,0:T(8,128)S(1)}) custom-call(bf16[560,256]{1,0:T(8,128)(2,1)S(1)} %collective-permute-done.5.refs_0_, bf16[544,256]{1,0:T(8,128)(2,1)S(1)} %collective-permute-done.6.refs_1_, bf16[512,64]{1,0:T(8,128)(2,1)S(1)} %get-tuple-element.82.refs_3_.refs_2_, ...), custom_call_target="tpu_custom_call" | custom-call | flops 1000000000 | tf_op jit(solution)/shard_map/product/pallas_call | solution.py:207
  28.8 0.5 collective-permute-done.9.refs_1_
  29.3 0.1 add_up.3
  29.3 0.2 collective-permute-start.10
  29.5 0.6 collective-permute-start.11
  30.2 0.8 %product.7.refs_0_ = f32[512,256]{1,0:T(8,128)S(1)} custom-call(bf16[560,256]{1,0:T(8,128)(2,1)S(1)} %collective-permute-done.5.refs_0_, bf16[544,256]{1,0:T(8,128)(2,1)S(1)} %collective-permute-done.6.refs_1_, bf16[512,64]{1,0:T(8,128)(2,1)S(1)} %get-tuple-element.79.refs_2_, f32[512,256]{1,0:T(8,128)S(1)} %get-tuple-element.109.refs_3_), custom_call_target="tpu_custom_call" | custom-call | flops 1000000000 | tf_op jit(solution)/shard_map/product/pallas_call | solution.py:207
  31.0 1.5 %collective-permute-start.14 = (bf16[16,128]{1,0:T(8,128)(2,1)S(1)}, bf16[16,128]{1,0:T(8,128)(2,1)S(1)}, u32[]{:S(2)}, u32[]{:S(2)}) collective-permute-start(bf16[16,128]{1,0:T(8,128)(2,1)S(1)} %get-tuple-element.124.refs_0_), channel_id=1, source_target_pairs={{0,2},{1,3},{2,0},{3,1},{4,6},{5,7},{6,4},{7,5},{8,10},{9,11},{10,... | collective-permute-start | bytes 12296 | tf_op jit(solution)/shard_map/ppermute | solution.py:565
  32.5 0.0 collective-permute-done.10.refs_1_
  32.5 0.1 add_up.4
  32.5 0.7 %collective-permute-start.13 = (bf16[256,256]{1,0:T(8,128)(2,1)S(1)}, bf16[256,256]{1,0:T(8,128)(2,1)S(1)}, u32[]{:S(2)}, u32[]{:S(2)}) collective-permute-start(bf16[256,256]{1,0:T(8,128)(2,1)S(1)} %get-tuple-element.121.refs_2_), channel_id=1, source_target_pairs={{0,2},{1,3},{2,0},{3,1},{4,6},{5,7},{6,4},{7,5},{8,10},{9,11},{10,... | collective-permute-start | bytes 393224 | tf_op jit(solution)/shard_map/ppermute | solution.py:565
  33.2 2.4 %collective-permute-done.11.refs_1_ = bf16[256,256]{1,0:T(8,128)(2,1)S(1)} collective-permute-done((bf16[256,256]{1,0:T(8,128)(2,1)S(1)}, bf16[256,256]{1,0:T(8,128)(2,1)S(1)}, u32[]{:S(2)}, u32[]{:S(2)}) %collective-permute-start.11) | collective-permute-done | bytes 131104 | tf_op jit(solution)/shard_map/ppermute | solution.py:565
  35.6 2.7 %collective-permute-start.12 = (bf16[256,256]{1,0:T(8,128)(2,1)S(1)}, bf16[256,256]{1,0:T(8,128)(2,1)S(1)}, u32[]{:S(2)}, u32[]{:S(2)}) collective-permute-start(bf16[256,256]{1,0:T(8,128)(2,1)S(1)} %add_up.5), channel_id=1, source_target_pairs={{0,4},{1,5},{2,6},{3,7},{4,0},{5,1},{6,2},{7,3},{8,12},{9,13},{10,... | collective-permute-start | bytes 393224 | tf_op jit(solution)/shard_map/ppermute | solution.py:565
  38.3 0.0 collective-permute-done.14.refs_1_
  38.3 1.0 %top_couplings.1 = (bf16[192,384]{1,0:T(8,128)(2,1)S(1)}, bf16[192,384]{1,0:T(8,128)(2,1)S(1)}) custom-call(bf16[16,128]{1,0:T(8,128)(2,1)S(1)} %get-tuple-element.124.refs_0_, bf16[16,128]{1,0:T(8,128)(2,1)S(1)} %collective-permute-done.14.refs_1_, bf16[6,64,128]{2,1,0:T(8,128)(2,1)S(1)} %get-tuple-element.122.refs_2_.refs_4_.refs_5_), custom_call_target="tpu_custom_call" | custom-call | flops 10000000000 | tf_op jit(solution)/shard_map/top_couplings/pallas_call | solution.py:544
  39.3 4.8 %collective-permute-done.12.refs_1_ = bf16[256,256]{1,0:T(8,128)(2,1)S(1)} collective-permute-done((bf16[256,256]{1,0:T(8,128)(2,1)S(1)}, bf16[256,256]{1,0:T(8,128)(2,1)S(1)}, u32[]{:S(2)}, u32[]{:S(2)}) %collective-permute-start.12) | collective-permute-done | bytes 131104 | tf_op jit(solution)/shard_map/ppermute | solution.py:565
  44.1 0.0 collective-permute-done.13.refs_2_
  44.1 5.4 %leaves.1 = (f32[2,64,128]{2,1,0:T(8,128)}, f32[64,128]{1,0:T(8,128)S(1)}, f32[64,256]{1,0:T(8,128)S(1)}, f32[64,256]{1,0:T(8,128)S(1)}, bf16[192,256]{1,0:T(8,128)(2,1)S(1)}) custom-call(f32[256,256]{1,0:T(8,128)S(1)} %get-tuple-element.118.refs_0_, bf16[256,256]{1,0:T(8,128)(2,1)S(1)} %collective-permute-done.12.refs_1_, ...), custom_call_target="tpu_custom_call" | custom-call | flops 1000000000 | tf_op jit(solution)/shard_map/leaves/pallas_call | solution.py:364
  49.5 0.9 %collective-permute-start.17 = (bf16[192,256]{1,0:T(8,128)(2,1)S(1)}, bf16[192,256]{1,0:T(8,128)(2,1)S(1)}, u32[]{:S(2)}, u32[]{:S(2)}) collective-permute-start(bf16[192,256]{1,0:T(8,128)(2,1)S(1)} %get-tuple-element.130), channel_id=1, source_target_pairs={{0,3},{1,2},{2,1},{3,0},{4,7},{5,6},{6,5},{7,4},{8,11},{9,10},{10,... | collective-permute-start | bytes 294920 | tf_op jit(solution)/shard_map/ppermute | solution.py:565
  50.4 2.1 %collective-permute-start.16 = (bf16[192,256]{1,0:T(8,128)(2,1)S(1)}, bf16[192,256]{1,0:T(8,128)(2,1)S(1)}, u32[]{:S(2)}, u32[]{:S(2)}) collective-permute-start(bf16[192,256]{1,0:T(8,128)(2,1)S(1)} %get-tuple-element.130), channel_id=1, source_target_pairs={{0,2},{1,3},{2,0},{3,1},{4,6},{5,7},{6,4},{7,5},{8,10},{9,11},{10,... | collective-permute-start | bytes 294920 | tf_op jit(solution)/shard_map/ppermute | solution.py:565
  52.5 0.5 collective-permute-start.15
  53.0 2.0 %collective-permute-done.17.refs_4_ = bf16[192,256]{1,0:T(8,128)(2,1)S(1)} collective-permute-done((bf16[192,256]{1,0:T(8,128)(2,1)S(1)}, bf16[192,256]{1,0:T(8,128)(2,1)S(1)}, u32[]{:S(2)}, u32[]{:S(2)}) %collective-permute-start.17) | collective-permute-done | bytes 98336 | tf_op jit(solution)/shard_map/ppermute | solution.py:565
  55.1 1.1 %collective-permute-done.16.refs_3_ = bf16[192,256]{1,0:T(8,128)(2,1)S(1)} collective-permute-done((bf16[192,256]{1,0:T(8,128)(2,1)S(1)}, bf16[192,256]{1,0:T(8,128)(2,1)S(1)}, u32[]{:S(2)}, u32[]{:S(2)}) %collective-permute-start.16) | collective-permute-done | bytes 98336 | tf_op jit(solution)/shard_map/ppermute | solution.py:565
  56.1 1.0 %collective-permute-done.15.refs_2_ = bf16[192,256]{1,0:T(8,128)(2,1)S(1)} collective-permute-done((bf16[192,256]{1,0:T(8,128)(2,1)S(1)}, bf16[192,256]{1,0:T(8,128)(2,1)S(1)}, u32[]{:S(2)}, u32[]{:S(2)}) %collective-permute-start.15) | collective-permute-done | bytes 98336 | tf_op jit(solution)/shard_map/ppermute | solution.py:565
  57.1 5.8 %upper_levels.1 = (f32[3,1,64,128]{3,2,1,0:T(8,128)}, f32[2,1,64,256]{3,2,1,0:T(8,128)}) custom-call(f32[64,256]{1,0:T(8,128)S(1)} %get-tuple-element.128.refs_0_, f32[64,256]{1,0:T(8,128)S(1)} %get-tuple-element.129.refs_1_, bf16[192,256]{1,0:T(8,128)(2,1)S(1)} %collective-permute-done.15.refs_2_, bf16[192,256]{1,0:T(8,128)(2,1)S(1)} %collective-permute-done.16.refs_3_, ...), custom_call_target="tpu_custom_call" | custom-call | flops 1000000000 | tf_op jit(solution)/shard_map/upper_levels/pallas_call | solution.py:440
  (4 shorter events, 0.0 us)
Async XLA Ops:
  1.9 6.1 %collective-permute-start.2 = (bf16[16,256]{1,0:T(8,128)(2,1)S(1)}, bf16[16,256]{1,0:T(8,128)(2,1)S(1)}, u32[]{:S(2)}, u32[]{:S(2)}) collective-permute-start(bf16[16,256]{1,0:T(8,128)(2,1)S(1)} %get-tuple-element.71), channel_id=1, source_target_pairs={{0,2},{1,3},{2,0},{3,1},{4,6},{5,7},{6,4},{7,5},{8,10},{9,11},{10,... | collective-permute-start | bytes 24584 | tf_op jit(solution)/shard_map/ppermute | solution.py:565
  5.0 11.4 %collective-permute-start.1 = (bf16[544,256]{1,0:T(8,128)(2,1)S(1)}, bf16[544,256]{1,0:T(8,128)(2,1)S(1)}, u32[]{:S(2)}, u32[]{:S(2)}) collective-permute-start(bf16[544,256]{1,0:T(8,128)(2,1)S(1)} %get-tuple-element.80.refs_1_), channel_id=1, source_target_pairs={{0,16},{1,17},{2,18},{3,19},{4,20},{5,21},{6,22},{7,23},{8,24},{9,... | collective-permute-start | bytes 835592 | tf_op jit(solution)/shard_map/ppermute | solution.py:565
  6.5 9.9 %collective-permute-start = (bf16[560,256]{1,0:T(8,128)(2,1)S(1)}, bf16[560,256]{1,0:T(8,128)(2,1)S(1)}, u32[]{:S(2)}, u32[]{:S(2)}) collective-permute-start(bf16[560,256]{1,0:T(8,128)(2,1)S(1)} %get-tuple-element.103.refs_0_.refs_3_), channel_id=1, source_target_pairs={{0,1},{1,0},{2,3},{3,2},{4,5},{5,4},{6,7},{7,6},{8,9},{9,8},{10,11... | collective-permute-start | bytes 860168 | tf_op jit(solution)/shard_map/ppermute | solution.py:565
  8.0 4.7 %collective-permute-start.3 = (bf16[16,512]{1,0:T(8,128)(2,1)S(1)}, bf16[16,512]{1,0:T(8,128)(2,1)S(1)}, u32[]{:S(2)}, u32[]{:S(2)}) collective-permute-start(bf16[16,512]{1,0:T(8,128)(2,1)S(1)} %pad_maximum_fusion), channel_id=1, source_target_pairs={{0,4},{1,5},{2,6},{3,7},{4,0},{5,1},{6,2},{7,3},{8,12},{9,13},{10,... | collective-permute-start | bytes 49160 | tf_op jit(solution)/shard_map/ppermute | solution.py:565
  10.6 10.8 %collective-permute-start.7 = (bf16[544,256]{1,0:T(8,128)(2,1)S(1)}, bf16[544,256]{1,0:T(8,128)(2,1)S(1)}, u32[]{:S(2)}, u32[]{:S(2)}) collective-permute-start(bf16[544,256]{1,0:T(8,128)(2,1)S(1)} %get-tuple-element.80.refs_1_), channel_id=1, source_target_pairs={{0,1},{1,0},{2,3},{3,2},{4,5},{5,4},{6,7},{7,6},{8,9},{9,8},{10,11... | collective-permute-start | bytes 835592 | tf_op jit(solution)/shard_map/ppermute | solution.py:565
  11.1 10.2 %collective-permute-start.8 = (bf16[560,256]{1,0:T(8,128)(2,1)S(1)}, bf16[560,256]{1,0:T(8,128)(2,1)S(1)}, u32[]{:S(2)}, u32[]{:S(2)}) collective-permute-start(bf16[560,256]{1,0:T(8,128)(2,1)S(1)} %get-tuple-element.103.refs_0_.refs_3_), channel_id=1, source_target_pairs={{0,16},{1,17},{2,18},{3,19},{4,20},{5,21},{6,22},{7,23},{8,24},{9,... | collective-permute-start | bytes 860168 | tf_op jit(solution)/shard_map/ppermute | solution.py:565
  12.7 1.2 %collective-permute-start.4 = (bf16[16,1024]{1,0:T(8,128)(2,1)S(1)}, bf16[16,1024]{1,0:T(8,128)(2,1)S(1)}, u32[]{:S(2)}, u32[]{:S(2)}) collective-permute-start(bf16[16,1024]{1,0:T(8,128)(2,1)S(1)} %constant_dynamic-update-slice_fusion.refs_2_), channel_id=1, source_target_pairs={{0,8},{1,9},{2,10},{3,11},{4,12},{5,13},{6,14},{7,15},{8,0},{9,1},... | collective-permute-start | bytes 98312 | tf_op jit(solution)/shard_map/ppermute | solution.py:565
  16.4 10.0 %collective-permute-start.5 = (bf16[560,256]{1,0:T(8,128)(2,1)S(1)}, bf16[560,256]{1,0:T(8,128)(2,1)S(1)}, u32[]{:S(2)}, u32[]{:S(2)}) collective-permute-start(bf16[560,256]{1,0:T(8,128)(2,1)S(1)} %collective-permute-done.refs_0_.refs_1_), channel_id=1, source_target_pairs={{0,16},{1,17},{2,18},{3,19},{4,20},{5,21},{6,22},{7,23},{8,24},{9,... | collective-permute-start | bytes 860168 | tf_op jit(solution)/shard_map/ppermute | solution.py:565
  17.1 9.4 %collective-permute-start.6 = (bf16[544,256]{1,0:T(8,128)(2,1)S(1)}, bf16[544,256]{1,0:T(8,128)(2,1)S(1)}, u32[]{:S(2)}, u32[]{:S(2)}) collective-permute-start(bf16[544,256]{1,0:T(8,128)(2,1)S(1)} %collective-permute-done.1.refs_1_), channel_id=1, source_target_pairs={{0,1},{1,0},{2,3},{3,2},{4,5},{5,4},{6,7},{7,6},{8,9},{9,8},{10,11... | collective-permute-start | bytes 835592 | tf_op jit(solution)/shard_map/ppermute | solution.py:565
  27.3 2.0 %collective-permute-start.9 = (f32[512,256]{1,0:T(8,128)S(1)}, f32[512,256]{1,0:T(8,128)S(1)}, u32[]{:S(2)}, u32[]{:S(2)}) collective-permute-start(f32[512,256]{1,0:T(8,128)S(1)} %product.9), channel_id=1, source_target_pairs={{0,8},{1,9},{2,10},{3,11},{4,12},{5,13},{6,14},{7,15},{8,0},{9,1},... | collective-permute-start | bytes 1572872 | tf_op jit(solution)/shard_map/ppermute | solution.py:565
  29.3 3.1 %collective-permute-start.10 = (f32[512,256]{1,0:T(8,128)S(1)}, f32[512,256]{1,0:T(8,128)S(1)}, u32[]{:S(2)}, u32[]{:S(2)}) collective-permute-start(f32[512,256]{1,0:T(8,128)S(1)} %get-tuple-element.117), channel_id=1, source_target_pairs={{0,8},{1,9},{2,10},{3,11},{4,12},{5,13},{6,14},{7,15},{8,0},{9,1},... | collective-permute-start | bytes 1572872 | tf_op jit(solution)/shard_map/ppermute | solution.py:565
  29.5 6.1 %collective-permute-start.11 = (bf16[256,256]{1,0:T(8,128)(2,1)S(1)}, bf16[256,256]{1,0:T(8,128)(2,1)S(1)}, u32[]{:S(2)}, u32[]{:S(2)}) collective-permute-start(bf16[256,256]{1,0:T(8,128)(2,1)S(1)} %get-tuple-element.120), channel_id=1, source_target_pairs={{0,2},{1,3},{2,0},{3,1},{4,6},{5,7},{6,4},{7,5},{8,10},{9,11},{10,... | collective-permute-start | bytes 393224 | tf_op jit(solution)/shard_map/ppermute | solution.py:565
  31.0 7.3 %collective-permute-start.14 = (bf16[16,128]{1,0:T(8,128)(2,1)S(1)}, bf16[16,128]{1,0:T(8,128)(2,1)S(1)}, u32[]{:S(2)}, u32[]{:S(2)}) collective-permute-start(bf16[16,128]{1,0:T(8,128)(2,1)S(1)} %get-tuple-element.124.refs_0_), channel_id=1, source_target_pairs={{0,2},{1,3},{2,0},{3,1},{4,6},{5,7},{6,4},{7,5},{8,10},{9,11},{10,... | collective-permute-start | bytes 12296 | tf_op jit(solution)/shard_map/ppermute | solution.py:565
  32.5 11.5 %collective-permute-start.13 = (bf16[256,256]{1,0:T(8,128)(2,1)S(1)}, bf16[256,256]{1,0:T(8,128)(2,1)S(1)}, u32[]{:S(2)}, u32[]{:S(2)}) collective-permute-start(bf16[256,256]{1,0:T(8,128)(2,1)S(1)} %get-tuple-element.121.refs_2_), channel_id=1, source_target_pairs={{0,2},{1,3},{2,0},{3,1},{4,6},{5,7},{6,4},{7,5},{8,10},{9,11},{10,... | collective-permute-start | bytes 393224 | tf_op jit(solution)/shard_map/ppermute | solution.py:565
  35.6 8.4 %collective-permute-start.12 = (bf16[256,256]{1,0:T(8,128)(2,1)S(1)}, bf16[256,256]{1,0:T(8,128)(2,1)S(1)}, u32[]{:S(2)}, u32[]{:S(2)}) collective-permute-start(bf16[256,256]{1,0:T(8,128)(2,1)S(1)} %add_up.5), channel_id=1, source_target_pairs={{0,4},{1,5},{2,6},{3,7},{4,0},{5,1},{6,2},{7,3},{8,12},{9,13},{10,... | collective-permute-start | bytes 393224 | tf_op jit(solution)/shard_map/ppermute | solution.py:565
  49.5 5.6 %collective-permute-start.17 = (bf16[192,256]{1,0:T(8,128)(2,1)S(1)}, bf16[192,256]{1,0:T(8,128)(2,1)S(1)}, u32[]{:S(2)}, u32[]{:S(2)}) collective-permute-start(bf16[192,256]{1,0:T(8,128)(2,1)S(1)} %get-tuple-element.130), channel_id=1, source_target_pairs={{0,3},{1,2},{2,1},{3,0},{4,7},{5,6},{6,5},{7,4},{8,11},{9,10},{10,... | collective-permute-start | bytes 294920 | tf_op jit(solution)/shard_map/ppermute | solution.py:565
  50.4 5.8 %collective-permute-start.16 = (bf16[192,256]{1,0:T(8,128)(2,1)S(1)}, bf16[192,256]{1,0:T(8,128)(2,1)S(1)}, u32[]{:S(2)}, u32[]{:S(2)}) collective-permute-start(bf16[192,256]{1,0:T(8,128)(2,1)S(1)} %get-tuple-element.130), channel_id=1, source_target_pairs={{0,2},{1,3},{2,0},{3,1},{4,6},{5,7},{6,4},{7,5},{8,10},{9,11},{10,... | collective-permute-start | bytes 294920 | tf_op jit(solution)/shard_map/ppermute | solution.py:565
  52.5 4.6 %collective-permute-start.15 = (bf16[192,256]{1,0:T(8,128)(2,1)S(1)}, bf16[192,256]{1,0:T(8,128)(2,1)S(1)}, u32[]{:S(2)}, u32[]{:S(2)}) collective-permute-start(bf16[192,256]{1,0:T(8,128)(2,1)S(1)} %get-tuple-element.130), channel_id=1, source_target_pairs={{0,1},{1,0},{2,3},{3,2},{4,5},{5,4},{6,7},{7,6},{8,9},{9,8},{10,11... | collective-permute-start | bytes 294920 | tf_op jit(solution)/shard_map/ppermute | solution.py:565

commit v3 on v2

--- a/solution.py
+++ b/solution.py
@@ -198,15 +198,16 @@
         def put(group, start, value):
             place = pl.ds(start, span)
             base = old_refs if number == 0 else total_refs
-            total_refs[group][place, :] = base[group][place, :] + value
+            value = base[group][place, :] + value
+            total_refs[group][place, :] = value.astype(total_refs[group].dtype)
 
         add_halves(half_refs[number : number + 2], row_refs, cols_ref, put, span, False)
 
 
-def product(halves, rows, totals, span, cost=COST):
+def product(halves, rows, totals, span, cost=COST, kind=F32):
     return pl.pallas_call(
         lambda *refs: product_body(span, len(halves), len(rows), *refs),
-        out_shape=[vmem(total.shape, F32) for total in totals],
+        out_shape=[vmem(total.shape, kind) for total in totals],
         scratch_shapes=[pltpu.VMEM((64, 4 * span), BF16)],
         cost_estimate=cost,
         compiler_params=PARAMS,
@@ -599,7 +600,7 @@
         more = [swap(value, 1 << bit, 0) for value in pieces]
         totals = product(more, feats, totals, span)
         pieces += more
-    (theirs,) = product(diagonal, feats[3:], totals[3:], span)
+    (theirs,) = product(diagonal, feats[3:], totals[3:], span, kind=BF16)
     from_sibling = swap(theirs, 1, 0)
     mine, theirs = product(diagonal, feats[1:3], totals[1:3], span)
     outs = [(range(0, line - 2, 2), F32), (range(1, line - 2, 2), BF16)]

time: 63.2 us -> 62.6 us (level)
  no operation moved by 1% of the time
where the time goes in v3:
time: 62.6 us; the launch traced here: 62.5 us
  Pallas kernels  25 us (40%)
  starting transfers between devices  22.3 us (36%)
  waiting for transfers between devices  14.2 us (23%)
  between operations  0.91 us (1%)
    ppermute x18, starting transfers between devices, swap(): return lax.ppermute(value, ('row', 'col'), pairs)  22.3 us
    ppermute x18, waiting for transfers between devices, swap(): return lax.ppermute(value, ('row', 'col'), pairs)  14.2 us
    pallas_call x5, Pallas kernels, product(): pl.pallas_call(lambda *refs: product_body(span, len(halves), len(rows), *...  7.99 us
    pallas_call x1, Pallas kernels, upper_levels(): pl.pallas_call(lambda *refs: upper_body(picks.shape[0], *refs), out_shape...  5.76 us
    pallas_call x1, Pallas kernels, leaves(): pl.pallas_call(lambda *refs: leaves_body(len(others), *refs), out_shape=(...  5.42 us
    pallas_call x1, Pallas kernels, first_product(): pl.pallas_call(lambda *refs: first_product_body(gain, span, groups, len(p...  2.53 us
    pallas_call x1, Pallas kernels, pack(): pl.pallas_call(pack_body, out_shape=(vmem((2 * (span + 16) + table_rows,...  1.26 us
  transfers between devices with their start and end apart: 18, of which 9 were waited for; matrix products, arithmetic and copies ran while one was open for 0% of the time, Pallas kernels for 19%

profile of v3, /device:TPU:0, one launch (start us, length us, event | category | flops | bytes accessed | tf_op | source)
XLA Modules:
  0.0 62.5 jit_solution(2706743915796942476)
XLA Ops:
  0.6 1.3 %pack.1 = (bf16[560,256]{1,0:T(8,128)(2,1)S(1)}, bf16[544,256]{1,0:T(8,128)(2,1)S(1)}, bf16[16,256]{1,0:T(8,128)(2,1)S(1)}) custom-call(bf16[4,256,256]{2,1,0:T(8,128)(2,1)} %refs_0_.1, bf16[16,4,256]{2,1,0:T(4,128)(2,1)} %refs_1_.1, s32[2,64]{1,0:T(2,128)} %refs_2_.1, s32[1,64]{1,0:T(1,128)} %refs_3_.1, s32[4,64]{1,0:T(4,128)} %refs_4_.1, s32[2,64]{1,0:T(2,128)} %refs_5_.1), custom_call_target="tpu_custom_call" | custom-call | flops 1000000000 | tf_op jit(solution)/shard_map/pack/pallas_call | solution.py:119
  1.9 3.1 %collective-permute-start.2 = (bf16[16,256]{1,0:T(8,128)(2,1)S(1)}, bf16[16,256]{1,0:T(8,128)(2,1)S(1)}, u32[]{:S(2)}, u32[]{:S(2)}) collective-permute-start(bf16[16,256]{1,0:T(8,128)(2,1)S(1)} %get-tuple-element.71), channel_id=1, source_target_pairs={{0,2},{1,3},{2,0},{3,1},{4,6},{5,7},{6,4},{7,5},{8,10},{9,11},{10,... | collective-permute-start | bytes 24584 | tf_op jit(solution)/shard_map/ppermute | solution.py:566
  5.0 1.5 %collective-permute-start.1 = (bf16[544,256]{1,0:T(8,128)(2,1)S(1)}, bf16[544,256]{1,0:T(8,128)(2,1)S(1)}, u32[]{:S(2)}, u32[]{:S(2)}) collective-permute-start(bf16[544,256]{1,0:T(8,128)(2,1)S(1)} %get-tuple-element.80.refs_1_), channel_id=1, source_target_pairs={{0,16},{1,17},{2,18},{3,19},{4,20},{5,21},{6,22},{7,23},{8,24},{9,... | collective-permute-start | bytes 835592 | tf_op jit(solution)/shard_map/ppermute | solution.py:566
  6.5 1.5 %collective-permute-start = (bf16[560,256]{1,0:T(8,128)(2,1)S(1)}, bf16[560,256]{1,0:T(8,128)(2,1)S(1)}, u32[]{:S(2)}, u32[]{:S(2)}) collective-permute-start(bf16[560,256]{1,0:T(8,128)(2,1)S(1)} %get-tuple-element.103.refs_0_.refs_3_), channel_id=1, source_target_pairs={{0,1},{1,0},{2,3},{3,2},{4,5},{5,4},{6,7},{7,6},{8,9},{9,8},{10,11... | collective-permute-start | bytes 860168 | tf_op jit(solution)/shard_map/ppermute | solution.py:566
  8.0 0.0 collective-permute-done.2
  8.0 2.6 %collective-permute-start.3 = (bf16[16,512]{1,0:T(8,128)(2,1)S(1)}, bf16[16,512]{1,0:T(8,128)(2,1)S(1)}, u32[]{:S(2)}, u32[]{:S(2)}) collective-permute-start(bf16[16,512]{1,0:T(8,128)(2,1)S(1)} %pad_maximum_fusion), channel_id=1, source_target_pairs={{0,4},{1,5},{2,6},{3,7},{4,0},{5,1},{6,2},{7,3},{8,12},{9,13},{10,... | collective-permute-start | bytes 49160 | tf_op jit(solution)/shard_map/ppermute | solution.py:566
  10.6 0.6 collective-permute-start.7
  11.1 1.5 %collective-permute-start.8 = (bf16[560,256]{1,0:T(8,128)(2,1)S(1)}, bf16[560,256]{1,0:T(8,128)(2,1)S(1)}, u32[]{:S(2)}, u32[]{:S(2)}) collective-permute-start(bf16[560,256]{1,0:T(8,128)(2,1)S(1)} %get-tuple-element.103.refs_0_.refs_3_), channel_id=1, source_target_pairs={{0,16},{1,17},{2,18},{3,19},{4,20},{5,21},{6,22},{7,23},{8,24},{9,... | collective-permute-start | bytes 860168 | tf_op jit(solution)/shard_map/ppermute | solution.py:566
  12.7 0.0 collective-permute-done.3
  12.7 0.0 collective-permute-start.4
  12.7 1.2 %collective-permute-done.4.refs_3_ = bf16[16,1024]{1,0:T(8,128)(2,1)S(1)} collective-permute-done((bf16[16,1024]{1,0:T(8,128)(2,1)S(1)}, bf16[16,1024]{1,0:T(8,128)(2,1)S(1)}, u32[]{:S(2)}, u32[]{:S(2)}) %collective-permute-start.4) | collective-permute-done | bytes 32800 | tf_op jit(solution)/shard_map/ppermute | solution.py:566
  13.9 2.5 %first_product.1 = (bf16[512,64]{1,0:T(8,128)(2,1)S(1)}, bf16[512,64]{1,0:T(8,128)(2,1)S(1)}, bf16[512,64]{1,0:T(8,128)(2,1)S(1)}, bf16[512,64]{1,0:T(8,128)(2,1...) custom-call(bf16[560,256]{1,0:T(8,128)(2,1)S(1)} %get-tuple-element.10, ...), custom_call_target="tpu_custom_call" | custom-call | flops 1000000000 | tf_op jit(solution)/shard_map/first_product/pallas_call | solution.py:180
  16.4 0.0 collective-permute-done.1.refs_1_
  16.4 0.0 collective-permute-done.refs_0_.refs_1_
  16.4 0.6 collective-permute-start.5
  17.1 1.5 %collective-permute-start.6 = (bf16[544,256]{1,0:T(8,128)(2,1)S(1)}, bf16[544,256]{1,0:T(8,128)(2,1)S(1)}, u32[]{:S(2)}, u32[]{:S(2)}) collective-permute-start(bf16[544,256]{1,0:T(8,128)(2,1)S(1)} %collective-permute-done.1.refs_1_), channel_id=1, source_target_pairs={{0,1},{1,0},{2,3},{3,2},{4,5},{5,4},{6,7},{7,6},{8,9},{9,8},{10,11... | collective-permute-start | bytes 835592 | tf_op jit(solution)/shard_map/ppermute | solution.py:566
  18.5 2.5 %product.5 = (f32[512,256]{1,0:T(8,128)S(1)}, f32[512,256]{1,0:T(8,128)S(1)}, f32[512,256]{1,0:T(8,128)S(1)}, f32[512,256]{1,0:T(8,128)S(1)}) custom-call(bf16[560,256]{1,0:T(8,128)(2,1)S(1)} %collective-permute-done.refs_0_.refs_1_, bf16[544,256]{1,0:T(8,128)(2,1)S(1)} %collective-permute-done.1.refs_1_, bf16[512,64]{1,0:T(8,128)(2,1)S(1)} %get-tuple-element.79.refs_2_, ...), custom_call_target="tpu_custom_call" | custom-call | tf_op jit(solution)/shard_map/product/pallas_call | solution.py:208
  21.0 0.3 collective-permute-done.7.refs_0_
  21.4 0.0 collective-permute-done.8.refs_1_
  21.4 2.5 %product.6 = (f32[512,256]{1,0:T(8,128)S(1)}, f32[512,256]{1,0:T(8,128)S(1)}, f32[512,256]{1,0:T(8,128)S(1)}, f32[512,256]{1,0:T(8,128)S(1)}) custom-call(bf16[544,256]{1,0:T(8,128)(2,1)S(1)} %collective-permute-done.7.refs_0_, bf16[560,256]{1,0:T(8,128)(2,1)S(1)} %collective-permute-done.8.refs_1_, bf16[512,64]{1,0:T(8,128)(2,1)S(1)} %get-tuple-element.79.refs_2_, ...), custom_call_target="tpu_custom_call" | custom-call | flops 1000000000 | tf_op jit(solution)/shard_map/product/pallas_call | solution.py:208
  23.9 1.2 %skeletons.1 = (bf16[6,64,128]{2,1,0:T(8,128)(2,1)S(1)}, bf16[192,384]{1,0:T(8,128)(2,1)S(1)}, bf16[192,384]{1,0:T(8,128)(2,1)S(1)}, bf16[16,128]{1,0:T(8,128)(2,1)S(1)}) custom-call(bf16[560,256]{1,0:T(8,128)(2,1)S(1)} %get-tuple-element.103.refs_0_.refs_3_, bf16[560,256]{1,0:T(8,128)(2,1)S(1)} %collective-permute-done.refs_0_.refs_1_), custom_call_target="tpu_custom_call" | custom-call | flops 1000000000 | tf_op jit(solution)/shard_map/skeletons/pallas_call | solution.py:518
  25.0 1.4 %collective-permute-done.6.refs_1_ = bf16[544,256]{1,0:T(8,128)(2,1)S(1)} collective-permute-done((bf16[544,256]{1,0:T(8,128)(2,1)S(1)}, bf16[544,256]{1,0:T(8,128)(2,1)S(1)}, u32[]{:S(2)}, u32[]{:S(2)}) %collective-permute-start.6) | collective-permute-done | bytes 278560 | tf_op jit(solution)/shard_map/ppermute | solution.py:566
  26.5 0.0 collective-permute-done.5.refs_0_
  26.5 0.8 %product.9 = bf16[512,256]{1,0:T(8,128)(2,1)S(1)} custom-call(bf16[560,256]{1,0:T(8,128)(2,1)S(1)} %collective-permute-done.5.refs_0_, bf16[544,256]{1,0:T(8,128)(2,1)S(1)} %collective-permute-done.6.refs_1_, bf16[512,64]{1,0:T(8,128)(2,1)S(1)} %get-tuple-element.84.refs_5_.refs_2_, f32[512,256]{1,0:T(8,128)S(1)} %get-tuple-element.113.refs_3_), custom_call_target="tpu_custom_call" | custom-call | flops 1000000000 | tf_op jit(solution)/shard_map/product/pallas_call | solution.py:208
  27.3 0.1 collective-permute-start.9
  27.4 1.4 %product.8 = (f32[512,256]{1,0:T(8,128)S(1)}, f32[512,256]{1,0:T(8,128)S(1)}) custom-call(bf16[560,256]{1,0:T(8,128)(2,1)S(1)} %collective-permute-done.5.refs_0_, bf16[544,256]{1,0:T(8,128)(2,1)S(1)} %collective-permute-done.6.refs_1_, bf16[512,64]{1,0:T(8,128)(2,1)S(1)} %get-tuple-element.82.refs_3_.refs_2_, ...), custom_call_target="tpu_custom_call" | custom-call | flops 1000000000 | tf_op jit(solution)/shard_map/product/pallas_call | solution.py:208
  28.7 0.2 collective-permute-done.9.refs_1_
  28.9 0.4 collective-permute-start.10
  29.4 0.6 collective-permute-start.11
  30.0 0.8 %product.7.refs_0_ = f32[512,256]{1,0:T(8,128)S(1)} custom-call(bf16[560,256]{1,0:T(8,128)(2,1)S(1)} %collective-permute-done.5.refs_0_, bf16[544,256]{1,0:T(8,128)(2,1)S(1)} %collective-permute-done.6.refs_1_, bf16[512,64]{1,0:T(8,128)(2,1)S(1)} %get-tuple-element.79.refs_2_, f32[512,256]{1,0:T(8,128)S(1)} %get-tuple-element.109.refs_3_), custom_call_target="tpu_custom_call" | custom-call | flops 1000000000 | tf_op jit(solution)/shard_map/product/pallas_call | solution.py:208
  30.8 1.5 %collective-permute-start.14 = (bf16[16,128]{1,0:T(8,128)(2,1)S(1)}, bf16[16,128]{1,0:T(8,128)(2,1)S(1)}, u32[]{:S(2)}, u32[]{:S(2)}) collective-permute-start(bf16[16,128]{1,0:T(8,128)(2,1)S(1)} %get-tuple-element.124.refs_0_), channel_id=1, source_target_pairs={{0,2},{1,3},{2,0},{3,1},{4,6},{5,7},{6,4},{7,5},{8,10},{9,11},{10,... | collective-permute-start | bytes 12296 | tf_op jit(solution)/shard_map/ppermute | solution.py:566
  32.3 0.0 collective-permute-done.10.refs_1_
  32.3 0.1 add_up.4
  32.4 0.7 %collective-permute-start.13 = (bf16[256,256]{1,0:T(8,128)(2,1)S(1)}, bf16[256,256]{1,0:T(8,128)(2,1)S(1)}, u32[]{:S(2)}, u32[]{:S(2)}) collective-permute-start(bf16[256,256]{1,0:T(8,128)(2,1)S(1)} %get-tuple-element.121.refs_2_), channel_id=1, source_target_pairs={{0,2},{1,3},{2,0},{3,1},{4,6},{5,7},{6,4},{7,5},{8,10},{9,11},{10,... | collective-permute-start | bytes 393224 | tf_op jit(solution)/shard_map/ppermute | solution.py:566
  33.0 2.2 %collective-permute-done.11.refs_1_ = bf16[256,256]{1,0:T(8,128)(2,1)S(1)} collective-permute-done((bf16[256,256]{1,0:T(8,128)(2,1)S(1)}, bf16[256,256]{1,0:T(8,128)(2,1)S(1)}, u32[]{:S(2)}, u32[]{:S(2)}) %collective-permute-start.11) | collective-permute-done | bytes 131104 | tf_op jit(solution)/shard_map/ppermute | solution.py:566
  35.3 2.7 %collective-permute-start.12 = (bf16[256,256]{1,0:T(8,128)(2,1)S(1)}, bf16[256,256]{1,0:T(8,128)(2,1)S(1)}, u32[]{:S(2)}, u32[]{:S(2)}) collective-permute-start(bf16[256,256]{1,0:T(8,128)(2,1)S(1)} %add_up.5), channel_id=1, source_target_pairs={{0,4},{1,5},{2,6},{3,7},{4,0},{5,1},{6,2},{7,3},{8,12},{9,13},{10,... | collective-permute-start | bytes 393224 | tf_op jit(solution)/shard_map/ppermute | solution.py:566
  37.9 0.0 collective-permute-done.14.refs_1_
  37.9 0.8 %top_couplings.1 = (bf16[192,384]{1,0:T(8,128)(2,1)S(1)}, bf16[192,384]{1,0:T(8,128)(2,1)S(1)}) custom-call(bf16[16,128]{1,0:T(8,128)(2,1)S(1)} %get-tuple-element.124.refs_0_, bf16[16,128]{1,0:T(8,128)(2,1)S(1)} %collective-permute-done.14.refs_1_, bf16[6,64,128]{2,1,0:T(8,128)(2,1)S(1)} %get-tuple-element.122.refs_2_.refs_4_.refs_5_), custom_call_target="tpu_custom_call" | custom-call | flops 10000000000 | tf_op jit(solution)/shard_map/top_couplings/pallas_call | solution.py:545
  38.7 4.8 %collective-permute-done.12.refs_1_ = bf16[256,256]{1,0:T(8,128)(2,1)S(1)} collective-permute-done((bf16[256,256]{1,0:T(8,128)(2,1)S(1)}, bf16[256,256]{1,0:T(8,128)(2,1)S(1)}, u32[]{:S(2)}, u32[]{:S(2)}) %collective-permute-start.12) | collective-permute-done | bytes 131104 | tf_op jit(solution)/shard_map/ppermute | solution.py:566
  43.5 0.0 collective-permute-done.13.refs_2_
  43.5 5.4 %leaves.1 = (f32[2,64,128]{2,1,0:T(8,128)}, f32[64,128]{1,0:T(8,128)S(1)}, f32[64,256]{1,0:T(8,128)S(1)}, f32[64,256]{1,0:T(8,128)S(1)}, bf16[192,256]{1,0:T(8,128)(2,1)S(1)}) custom-call(f32[256,256]{1,0:T(8,128)S(1)} %get-tuple-element.118.refs_0_, bf16[256,256]{1,0:T(8,128)(2,1)S(1)} %collective-permute-done.12.refs_1_, ...), custom_call_target="tpu_custom_call" | custom-call | flops 1000000000 | tf_op jit(solution)/shard_map/leaves/pallas_call | solution.py:365
  48.9 0.8 %collective-permute-start.17 = (bf16[192,256]{1,0:T(8,128)(2,1)S(1)}, bf16[192,256]{1,0:T(8,128)(2,1)S(1)}, u32[]{:S(2)}, u32[]{:S(2)}) collective-permute-start(bf16[192,256]{1,0:T(8,128)(2,1)S(1)} %get-tuple-element.130), channel_id=1, source_target_pairs={{0,3},{1,2},{2,1},{3,0},{4,7},{5,6},{6,5},{7,4},{8,11},{9,10},{10,... | collective-permute-start | bytes 294920 | tf_op jit(solution)/shard_map/ppermute | solution.py:566
  49.8 2.2 %collective-permute-start.16 = (bf16[192,256]{1,0:T(8,128)(2,1)S(1)}, bf16[192,256]{1,0:T(8,128)(2,1)S(1)}, u32[]{:S(2)}, u32[]{:S(2)}) collective-permute-start(bf16[192,256]{1,0:T(8,128)(2,1)S(1)} %get-tuple-element.130), channel_id=1, source_target_pairs={{0,2},{1,3},{2,0},{3,1},{4,6},{5,7},{6,4},{7,5},{8,10},{9,11},{10,... | collective-permute-start | bytes 294920 | tf_op jit(solution)/shard_map/ppermute | solution.py:566
  52.0 0.5 collective-permute-start.15
  52.5 2.0 %collective-permute-done.17.refs_4_ = bf16[192,256]{1,0:T(8,128)(2,1)S(1)} collective-permute-done((bf16[192,256]{1,0:T(8,128)(2,1)S(1)}, bf16[192,256]{1,0:T(8,128)(2,1)S(1)}, u32[]{:S(2)}, u32[]{:S(2)}) %collective-permute-start.17) | collective-permute-done | bytes 98336 | tf_op jit(solution)/shard_map/ppermute | solution.py:566
  54.5 1.1 %collective-permute-done.16.refs_3_ = bf16[192,256]{1,0:T(8,128)(2,1)S(1)} collective-permute-done((bf16[192,256]{1,0:T(8,128)(2,1)S(1)}, bf16[192,256]{1,0:T(8,128)(2,1)S(1)}, u32[]{:S(2)}, u32[]{:S(2)}) %collective-permute-start.16) | collective-permute-done | bytes 98336 | tf_op jit(solution)/shard_map/ppermute | solution.py:566
  55.6 1.0 %collective-permute-done.15.refs_2_ = bf16[192,256]{1,0:T(8,128)(2,1)S(1)} collective-permute-done((bf16[192,256]{1,0:T(8,128)(2,1)S(1)}, bf16[192,256]{1,0:T(8,128)(2,1)S(1)}, u32[]{:S(2)}, u32[]{:S(2)}) %collective-permute-start.15) | collective-permute-done | bytes 98336 | tf_op jit(solution)/shard_map/ppermute | solution.py:566
  56.6 5.8 %upper_levels.1 = (f32[3,1,64,128]{3,2,1,0:T(8,128)}, f32[2,1,64,256]{3,2,1,0:T(8,128)}) custom-call(f32[64,256]{1,0:T(8,128)S(1)} %get-tuple-element.128.refs_0_, f32[64,256]{1,0:T(8,128)S(1)} %get-tuple-element.129.refs_1_, bf16[192,256]{1,0:T(8,128)(2,1)S(1)} %collective-permute-done.15.refs_2_, bf16[192,256]{1,0:T(8,128)(2,1)S(1)} %collective-permute-done.16.refs_3_, ...), custom_call_target="tpu_custom_call" | custom-call | flops 1000000000 | tf_op jit(solution)/shard_map/upper_levels/pallas_call | solution.py:441
  (5 shorter events, 0.1 us)
Async XLA Ops:
  1.9 6.1 %collective-permute-start.2 = (bf16[16,256]{1,0:T(8,128)(2,1)S(1)}, bf16[16,256]{1,0:T(8,128)(2,1)S(1)}, u32[]{:S(2)}, u32[]{:S(2)}) collective-permute-start(bf16[16,256]{1,0:T(8,128)(2,1)S(1)} %get-tuple-element.71), channel_id=1, source_target_pairs={{0,2},{1,3},{2,0},{3,1},{4,6},{5,7},{6,4},{7,5},{8,10},{9,11},{10,... | collective-permute-start | bytes 24584 | tf_op jit(solution)/shard_map/ppermute | solution.py:566
  5.0 11.4 %collective-permute-start.1 = (bf16[544,256]{1,0:T(8,128)(2,1)S(1)}, bf16[544,256]{1,0:T(8,128)(2,1)S(1)}, u32[]{:S(2)}, u32[]{:S(2)}) collective-permute-start(bf16[544,256]{1,0:T(8,128)(2,1)S(1)} %get-tuple-element.80.refs_1_), channel_id=1, source_target_pairs={{0,16},{1,17},{2,18},{3,19},{4,20},{5,21},{6,22},{7,23},{8,24},{9,... | collective-permute-start | bytes 835592 | tf_op jit(solution)/shard_map/ppermute | solution.py:566
  6.5 9.9 %collective-permute-start = (bf16[560,256]{1,0:T(8,128)(2,1)S(1)}, bf16[560,256]{1,0:T(8,128)(2,1)S(1)}, u32[]{:S(2)}, u32[]{:S(2)}) collective-permute-start(bf16[560,256]{1,0:T(8,128)(2,1)S(1)} %get-tuple-element.103.refs_0_.refs_3_), channel_id=1, source_target_pairs={{0,1},{1,0},{2,3},{3,2},{4,5},{5,4},{6,7},{7,6},{8,9},{9,8},{10,11... | collective-permute-start | bytes 860168 | tf_op jit(solution)/shard_map/ppermute | solution.py:566
  8.0 4.7 %collective-permute-start.3 = (bf16[16,512]{1,0:T(8,128)(2,1)S(1)}, bf16[16,512]{1,0:T(8,128)(2,1)S(1)}, u32[]{:S(2)}, u32[]{:S(2)}) collective-permute-start(bf16[16,512]{1,0:T(8,128)(2,1)S(1)} %pad_maximum_fusion), channel_id=1, source_target_pairs={{0,4},{1,5},{2,6},{3,7},{4,0},{5,1},{6,2},{7,3},{8,12},{9,13},{10,... | collective-permute-start | bytes 49160 | tf_op jit(solution)/shard_map/ppermute | solution.py:566
  10.6 10.8 %collective-permute-start.7 = (bf16[544,256]{1,0:T(8,128)(2,1)S(1)}, bf16[544,256]{1,0:T(8,128)(2,1)S(1)}, u32[]{:S(2)}, u32[]{:S(2)}) collective-permute-start(bf16[544,256]{1,0:T(8,128)(2,1)S(1)} %get-tuple-element.80.refs_1_), channel_id=1, source_target_pairs={{0,1},{1,0},{2,3},{3,2},{4,5},{5,4},{6,7},{7,6},{8,9},{9,8},{10,11... | collective-permute-start | bytes 835592 | tf_op jit(solution)/shard_map/ppermute | solution.py:566
  11.1 10.2 %collective-permute-start.8 = (bf16[560,256]{1,0:T(8,128)(2,1)S(1)}, bf16[560,256]{1,0:T(8,128)(2,1)S(1)}, u32[]{:S(2)}, u32[]{:S(2)}) collective-permute-start(bf16[560,256]{1,0:T(8,128)(2,1)S(1)} %get-tuple-element.103.refs_0_.refs_3_), channel_id=1, source_target_pairs={{0,16},{1,17},{2,18},{3,19},{4,20},{5,21},{6,22},{7,23},{8,24},{9,... | collective-permute-start | bytes 860168 | tf_op jit(solution)/shard_map/ppermute | solution.py:566
  12.7 1.2 %collective-permute-start.4 = (bf16[16,1024]{1,0:T(8,128)(2,1)S(1)}, bf16[16,1024]{1,0:T(8,128)(2,1)S(1)}, u32[]{:S(2)}, u32[]{:S(2)}) collective-permute-start(bf16[16,1024]{1,0:T(8,128)(2,1)S(1)} %constant_dynamic-update-slice_fusion.refs_2_), channel_id=1, source_target_pairs={{0,8},{1,9},{2,10},{3,11},{4,12},{5,13},{6,14},{7,15},{8,0},{9,1},... | collective-permute-start | bytes 98312 | tf_op jit(solution)/shard_map/ppermute | solution.py:566
  16.4 10.0 %collective-permute-start.5 = (bf16[560,256]{1,0:T(8,128)(2,1)S(1)}, bf16[560,256]{1,0:T(8,128)(2,1)S(1)}, u32[]{:S(2)}, u32[]{:S(2)}) collective-permute-start(bf16[560,256]{1,0:T(8,128)(2,1)S(1)} %collective-permute-done.refs_0_.refs_1_), channel_id=1, source_target_pairs={{0,16},{1,17},{2,18},{3,19},{4,20},{5,21},{6,22},{7,23},{8,24},{9,... | collective-permute-start | bytes 860168 | tf_op jit(solution)/shard_map/ppermute | solution.py:566
  17.1 9.4 %collective-permute-start.6 = (bf16[544,256]{1,0:T(8,128)(2,1)S(1)}, bf16[544,256]{1,0:T(8,128)(2,1)S(1)}, u32[]{:S(2)}, u32[]{:S(2)}) collective-permute-start(bf16[544,256]{1,0:T(8,128)(2,1)S(1)} %collective-permute-done.1.refs_1_), channel_id=1, source_target_pairs={{0,1},{1,0},{2,3},{3,2},{4,5},{5,4},{6,7},{7,6},{8,9},{9,8},{10,11... | collective-permute-start | bytes 835592 | tf_op jit(solution)/shard_map/ppermute | solution.py:566
  27.3 1.6 %collective-permute-start.9 = (bf16[512,256]{1,0:T(8,128)(2,1)S(1)}, bf16[512,256]{1,0:T(8,128)(2,1)S(1)}, u32[]{:S(2)}, u32[]{:S(2)}) collective-permute-start(bf16[512,256]{1,0:T(8,128)(2,1)S(1)} %product.9), channel_id=1, source_target_pairs={{0,8},{1,9},{2,10},{3,11},{4,12},{5,13},{6,14},{7,15},{8,0},{9,1},... | collective-permute-start | bytes 786440 | tf_op jit(solution)/shard_map/ppermute | solution.py:566
  28.9 3.4 %collective-permute-start.10 = (f32[512,256]{1,0:T(8,128)S(1)}, f32[512,256]{1,0:T(8,128)S(1)}, u32[]{:S(2)}, u32[]{:S(2)}) collective-permute-start(f32[512,256]{1,0:T(8,128)S(1)} %get-tuple-element.117), channel_id=1, source_target_pairs={{0,8},{1,9},{2,10},{3,11},{4,12},{5,13},{6,14},{7,15},{8,0},{9,1},... | collective-permute-start | bytes 1572872 | tf_op jit(solution)/shard_map/ppermute | solution.py:566
  29.4 5.9 %collective-permute-start.11 = (bf16[256,256]{1,0:T(8,128)(2,1)S(1)}, bf16[256,256]{1,0:T(8,128)(2,1)S(1)}, u32[]{:S(2)}, u32[]{:S(2)}) collective-permute-start(bf16[256,256]{1,0:T(8,128)(2,1)S(1)} %get-tuple-element.120), channel_id=1, source_target_pairs={{0,2},{1,3},{2,0},{3,1},{4,6},{5,7},{6,4},{7,5},{8,10},{9,11},{10,... | collective-permute-start | bytes 393224 | tf_op jit(solution)/shard_map/ppermute | solution.py:566
  30.8 7.1 %collective-permute-start.14 = (bf16[16,128]{1,0:T(8,128)(2,1)S(1)}, bf16[16,128]{1,0:T(8,128)(2,1)S(1)}, u32[]{:S(2)}, u32[]{:S(2)}) collective-permute-start(bf16[16,128]{1,0:T(8,128)(2,1)S(1)} %get-tuple-element.124.refs_0_), channel_id=1, source_target_pairs={{0,2},{1,3},{2,0},{3,1},{4,6},{5,7},{6,4},{7,5},{8,10},{9,11},{10,... | collective-permute-start | bytes 12296 | tf_op jit(solution)/shard_map/ppermute | solution.py:566
  32.4 11.2 %collective-permute-start.13 = (bf16[256,256]{1,0:T(8,128)(2,1)S(1)}, bf16[256,256]{1,0:T(8,128)(2,1)S(1)}, u32[]{:S(2)}, u32[]{:S(2)}) collective-permute-start(bf16[256,256]{1,0:T(8,128)(2,1)S(1)} %get-tuple-element.121.refs_2_), channel_id=1, source_target_pairs={{0,2},{1,3},{2,0},{3,1},{4,6},{5,7},{6,4},{7,5},{8,10},{9,11},{10,... | collective-permute-start | bytes 393224 | tf_op jit(solution)/shard_map/ppermute | solution.py:566
  35.3 8.2 %collective-permute-start.12 = (bf16[256,256]{1,0:T(8,128)(2,1)S(1)}, bf16[256,256]{1,0:T(8,128)(2,1)S(1)}, u32[]{:S(2)}, u32[]{:S(2)}) collective-permute-start(bf16[256,256]{1,0:T(8,128)(2,1)S(1)} %add_up.5), channel_id=1, source_target_pairs={{0,4},{1,5},{2,6},{3,7},{4,0},{5,1},{6,2},{7,3},{8,12},{9,13},{10,... | collective-permute-start | bytes 393224 | tf_op jit(solution)/shard_map/ppermute | solution.py:566
  48.9 5.6 %collective-permute-start.17 = (bf16[192,256]{1,0:T(8,128)(2,1)S(1)}, bf16[192,256]{1,0:T(8,128)(2,1)S(1)}, u32[]{:S(2)}, u32[]{:S(2)}) collective-permute-start(bf16[192,256]{1,0:T(8,128)(2,1)S(1)} %get-tuple-element.130), channel_id=1, source_target_pairs={{0,3},{1,2},{2,1},{3,0},{4,7},{5,6},{6,5},{7,4},{8,11},{9,10},{10,... | collective-permute-start | bytes 294920 | tf_op jit(solution)/shard_map/ppermute | solution.py:566
  49.8 5.9 %collective-permute-start.16 = (bf16[192,256]{1,0:T(8,128)(2,1)S(1)}, bf16[192,256]{1,0:T(8,128)(2,1)S(1)}, u32[]{:S(2)}, u32[]{:S(2)}) collective-permute-start(bf16[192,256]{1,0:T(8,128)(2,1)S(1)} %get-tuple-element.130), channel_id=1, source_target_pairs={{0,2},{1,3},{2,0},{3,1},{4,6},{5,7},{6,4},{7,5},{8,10},{9,11},{10,... | collective-permute-start | bytes 294920 | tf_op jit(solution)/shard_map/ppermute | solution.py:566
  52.0 4.6 %collective-permute-start.15 = (bf16[192,256]{1,0:T(8,128)(2,1)S(1)}, bf16[192,256]{1,0:T(8,128)(2,1)S(1)}, u32[]{:S(2)}, u32[]{:S(2)}) collective-permute-start(bf16[192,256]{1,0:T(8,128)(2,1)S(1)} %get-tuple-element.130), channel_id=1, source_target_pairs={{0,1},{1,0},{2,3},{3,2},{4,5},{5,4},{6,7},{7,6},{8,9},{9,8},{10,11... | collective-permute-start | bytes 294920 | tf_op jit(solution)/shard_map/ppermute | solution.py:566

commit v4 on v3

--- a/solution.py
+++ b/solution.py
@@ -80,12 +80,12 @@
 def pack_body(*refs):
     probes_ref, points_ref, *table_refs = refs[:6]
     first_ref, second_ref, own_ref, held_ref, rows_ref, *held_tables, sem = refs[6:]
-    span = probes_ref.shape[1]
-    pairs = [(points_ref, held_ref), *zip(table_refs, held_tables)]
-    small = len(pairs)
-    for quarter in range(4):
-        target = (first_ref, second_ref)[quarter // 2].at[pl.ds(quarter % 2 * span, span)]
-        pairs.append((probes_ref.at[quarter], target))
+    span = own_ref.shape[1]
+    pairs = [(points_ref, held_ref)]
+    for number, half_ref in enumerate((first_ref, second_ref)):
+        source = probes_ref.at[pl.ds(2 * span * number, 2 * span)]
+        pairs.append((source, half_ref.at[pl.ds(0, 2 * span)]))
+    pairs += zip(table_refs, held_tables)
     copies = [
         pltpu.make_async_copy(source, target, sem.at[pos])
         for pos, (source, target) in enumerate(pairs)
@@ -93,8 +93,7 @@
     for copy in copies:
         copy.start()
     rows_ref[...] = jnp.zeros_like(rows_ref)
-    for copy in copies[:small]:
-        copy.wait()
+    copies[0].wait()
     points = held_ref[...].astype(F32)
     for quarter in range(4):
         feats = points[:, quarter, :].astype(BF16)
@@ -102,20 +101,22 @@
         half_ref[pl.ds(2 * span + quarter % 2 * 16, 16), :] = feats
         if quarter == 0:
             own_ref[...] = feats
+    for copy in copies[3:]:
+        copy.wait()
     start = 0
     for table in held_tables:
         count, rank = table.shape
         rows_ref[pl.ds(start, count), pl.ds(0, rank)] = table[...].astype(F32)
         start += count
     first_ref[pl.ds(second_ref.shape[0], rows_ref.shape[0]), :] = rows_ref[...].astype(BF16)
-    for copy in copies[small:]:
+    for copy in copies[1:3]:
         copy.wait()
 
 
 def pack(probes, points, tables):
-    _, span, samples = probes.shape
+    quarters, span, samples = probes.shape
     table_rows = -(-sum(table.shape[0] for table in tables) // 16) * 16
-    inputs = (probes, points, *tables)
+    inputs = (probes.reshape(quarters * span, samples), points, *tables)
     return pl.pallas_call(
         pack_body,
         out_shape=(
@@ -128,7 +129,7 @@
             pltpu.VMEM(points.shape, BF16),
             pltpu.VMEM((table_rows, samples), F32),
             *[pltpu.VMEM(table.shape, jnp.int32) for table in tables],
-            pltpu.SemaphoreType.DMA((5 + len(tables),)),
+            pltpu.SemaphoreType.DMA((3 + len(tables),)),
         ],
         cost_estimate=COST,
         compiler_params=PARAMS,

time: 62.6 us -> 62.5 us (level)
  no operation moved by 1% of the time
where the time goes in v4:
time: 62.5 us; the launch traced here: 62.4 us
  Pallas kernels  24.9 us (40%)
  starting transfers between devices  22.3 us (36%)
  waiting for transfers between devices  14.2 us (23%)
  between operations  0.91 us (1%)
    ppermute x18, starting transfers between devices, swap(): return lax.ppermute(value, ('row', 'col'), pairs)  22.3 us
    ppermute x18, waiting for transfers between devices, swap(): return lax.ppermute(value, ('row', 'col'), pairs)  14.2 us
    pallas_call x5, Pallas kernels, product(): pl.pallas_call(lambda *refs: product_body(span, len(halves), len(rows), *...  7.98 us
    pallas_call x1, Pallas kernels, upper_levels(): pl.pallas_call(lambda *refs: upper_body(picks.shape[0], *refs), out_shape...  5.76 us
    pallas_call x1, Pallas kernels, leaves(): pl.pallas_call(lambda *refs: leaves_body(len(others), *refs), out_shape=(...  5.42 us
    pallas_call x1, Pallas kernels, first_product(): pl.pallas_call(lambda *refs: first_product_body(gain, span, groups, len(p...  2.53 us
  transfers between devices with their start and end apart: 18, of which 9 were waited for; matrix products, arithmetic and copies ran while one was open for 0% of the time, Pallas kernels for 19%

profile of v4, /device:TPU:0, one launch (start us, length us, event | category | flops | bytes accessed | tf_op | source)
XLA Modules:
  0.0 62.4 jit_solution(4490013174193299810)
XLA Ops:
  0.6 1.1 %pack.1 = (bf16[560,256]{1,0:T(8,128)(2,1)S(1)}, bf16[544,256]{1,0:T(8,128)(2,1)S(1)}, bf16[16,256]{1,0:T(8,128)(2,1)S(1)}) custom-call(bf16[1024,256]{1,0:T(8,128)(2,1)} %bitcast.3, bf16[16,4,256]{2,1,0:T(4,128)(2,1)} %refs_1_.1, s32[2,64]{1,0:T(2,128)} %refs_2_.1, s32[1,64]{1,0:T(1,128)} %refs_3_.1, s32[4,64]{1,0:T(4,128)} %refs_4_.1, s32[2,64]{1,0:T(2,128)} %refs_5_.1), custom_call_target="tpu_custom_call" | custom-call | flops 1000000000 | tf_op jit(solution)/shard_map/pack/pallas_call | solution.py:120
  1.8 3.1 %collective-permute-start.2 = (bf16[16,256]{1,0:T(8,128)(2,1)S(1)}, bf16[16,256]{1,0:T(8,128)(2,1)S(1)}, u32[]{:S(2)}, u32[]{:S(2)}) collective-permute-start(bf16[16,256]{1,0:T(8,128)(2,1)S(1)} %get-tuple-element.71), channel_id=1, source_target_pairs={{0,2},{1,3},{2,0},{3,1},{4,6},{5,7},{6,4},{7,5},{8,10},{9,11},{10,... | collective-permute-start | bytes 24584 | tf_op jit(solution)/shard_map/ppermute | solution.py:567
  4.8 1.5 %collective-permute-start.1 = (bf16[544,256]{1,0:T(8,128)(2,1)S(1)}, bf16[544,256]{1,0:T(8,128)(2,1)S(1)}, u32[]{:S(2)}, u32[]{:S(2)}) collective-permute-start(bf16[544,256]{1,0:T(8,128)(2,1)S(1)} %get-tuple-element.80.refs_1_), channel_id=1, source_target_pairs={{0,16},{1,17},{2,18},{3,19},{4,20},{5,21},{6,22},{7,23},{8,24},{9,... | collective-permute-start | bytes 835592 | tf_op jit(solution)/shard_map/ppermute | solution.py:567
  6.4 1.5 %collective-permute-start = (bf16[560,256]{1,0:T(8,128)(2,1)S(1)}, bf16[560,256]{1,0:T(8,128)(2,1)S(1)}, u32[]{:S(2)}, u32[]{:S(2)}) collective-permute-start(bf16[560,256]{1,0:T(8,128)(2,1)S(1)} %get-tuple-element.103.refs_0_.refs_3_), channel_id=1, source_target_pairs={{0,1},{1,0},{2,3},{3,2},{4,5},{5,4},{6,7},{7,6},{8,9},{9,8},{10,11... | collective-permute-start | bytes 860168 | tf_op jit(solution)/shard_map/ppermute | solution.py:567
  7.9 0.0 collective-permute-done.2
  7.9 2.6 %collective-permute-start.3 = (bf16[16,512]{1,0:T(8,128)(2,1)S(1)}, bf16[16,512]{1,0:T(8,128)(2,1)S(1)}, u32[]{:S(2)}, u32[]{:S(2)}) collective-permute-start(bf16[16,512]{1,0:T(8,128)(2,1)S(1)} %pad_maximum_fusion), channel_id=1, source_target_pairs={{0,4},{1,5},{2,6},{3,7},{4,0},{5,1},{6,2},{7,3},{8,12},{9,13},{10,... | collective-permute-start | bytes 49160 | tf_op jit(solution)/shard_map/ppermute | solution.py:567
  10.5 0.6 collective-permute-start.7
  11.0 1.5 %collective-permute-start.8 = (bf16[560,256]{1,0:T(8,128)(2,1)S(1)}, bf16[560,256]{1,0:T(8,128)(2,1)S(1)}, u32[]{:S(2)}, u32[]{:S(2)}) collective-permute-start(bf16[560,256]{1,0:T(8,128)(2,1)S(1)} %get-tuple-element.103.refs_0_.refs_3_), channel_id=1, source_target_pairs={{0,16},{1,17},{2,18},{3,19},{4,20},{5,21},{6,22},{7,23},{8,24},{9,... | collective-permute-start | bytes 860168 | tf_op jit(solution)/shard_map/ppermute | solution.py:567
  12.5 0.0 collective-permute-done.3
  12.5 0.0 collective-permute-start.4
  12.5 1.2 %collective-permute-done.4.refs_3_ = bf16[16,1024]{1,0:T(8,128)(2,1)S(1)} collective-permute-done((bf16[16,1024]{1,0:T(8,128)(2,1)S(1)}, bf16[16,1024]{1,0:T(8,128)(2,1)S(1)}, u32[]{:S(2)}, u32[]{:S(2)}) %collective-permute-start.4) | collective-permute-done | bytes 32800 | tf_op jit(solution)/shard_map/ppermute | solution.py:567
  13.7 2.5 %first_product.1 = (bf16[512,64]{1,0:T(8,128)(2,1)S(1)}, bf16[512,64]{1,0:T(8,128)(2,1)S(1)}, bf16[512,64]{1,0:T(8,128)(2,1)S(1)}, bf16[512,64]{1,0:T(8,128)(2,1...) custom-call(bf16[560,256]{1,0:T(8,128)(2,1)S(1)} %get-tuple-element.10, ...), custom_call_target="tpu_custom_call" | custom-call | flops 1000000000 | tf_op jit(solution)/shard_map/first_product/pallas_call | solution.py:181
  16.3 0.0 collective-permute-done.1.refs_1_
  16.3 0.0 collective-permute-done.refs_0_.refs_1_
  16.3 0.6 collective-permute-start.5
  16.9 1.5 %collective-permute-start.6 = (bf16[544,256]{1,0:T(8,128)(2,1)S(1)}, bf16[544,256]{1,0:T(8,128)(2,1)S(1)}, u32[]{:S(2)}, u32[]{:S(2)}) collective-permute-start(bf16[544,256]{1,0:T(8,128)(2,1)S(1)} %collective-permute-done.1.refs_1_), channel_id=1, source_target_pairs={{0,1},{1,0},{2,3},{3,2},{4,5},{5,4},{6,7},{7,6},{8,9},{9,8},{10,11... | collective-permute-start | bytes 835592 | tf_op jit(solution)/shard_map/ppermute | solution.py:567
  18.4 2.5 %product.5 = (f32[512,256]{1,0:T(8,128)S(1)}, f32[512,256]{1,0:T(8,128)S(1)}, f32[512,256]{1,0:T(8,128)S(1)}, f32[512,256]{1,0:T(8,128)S(1)}) custom-call(bf16[560,256]{1,0:T(8,128)(2,1)S(1)} %collective-permute-done.refs_0_.refs_1_, bf16[544,256]{1,0:T(8,128)(2,1)S(1)} %collective-permute-done.1.refs_1_, bf16[512,64]{1,0:T(8,128)(2,1)S(1)} %get-tuple-element.79.refs_2_, ...), custom_call_target="tpu_custom_call" | custom-call | tf_op jit(solution)/shard_map/product/pallas_call | solution.py:209
  20.9 0.3 collective-permute-done.7.refs_0_
  21.2 0.0 collective-permute-done.8.refs_1_
  21.2 2.5 %product.6 = (f32[512,256]{1,0:T(8,128)S(1)}, f32[512,256]{1,0:T(8,128)S(1)}, f32[512,256]{1,0:T(8,128)S(1)}, f32[512,256]{1,0:T(8,128)S(1)}) custom-call(bf16[544,256]{1,0:T(8,128)(2,1)S(1)} %collective-permute-done.7.refs_0_, bf16[560,256]{1,0:T(8,128)(2,1)S(1)} %collective-permute-done.8.refs_1_, bf16[512,64]{1,0:T(8,128)(2,1)S(1)} %get-tuple-element.79.refs_2_, ...), custom_call_target="tpu_custom_call" | custom-call | flops 1000000000 | tf_op jit(solution)/shard_map/product/pallas_call | solution.py:209
  23.7 1.2 %skeletons.1 = (bf16[6,64,128]{2,1,0:T(8,128)(2,1)S(1)}, bf16[192,384]{1,0:T(8,128)(2,1)S(1)}, bf16[192,384]{1,0:T(8,128)(2,1)S(1)}, bf16[16,128]{1,0:T(8,128)(2,1)S(1)}) custom-call(bf16[560,256]{1,0:T(8,128)(2,1)S(1)} %get-tuple-element.103.refs_0_.refs_3_, bf16[560,256]{1,0:T(8,128)(2,1)S(1)} %collective-permute-done.refs_0_.refs_1_), custom_call_target="tpu_custom_call" | custom-call | flops 1000000000 | tf_op jit(solution)/shard_map/skeletons/pallas_call | solution.py:519
  24.9 1.4 %collective-permute-done.6.refs_1_ = bf16[544,256]{1,0:T(8,128)(2,1)S(1)} collective-permute-done((bf16[544,256]{1,0:T(8,128)(2,1)S(1)}, bf16[544,256]{1,0:T(8,128)(2,1)S(1)}, u32[]{:S(2)}, u32[]{:S(2)}) %collective-permute-start.6) | collective-permute-done | bytes 278560 | tf_op jit(solution)/shard_map/ppermute | solution.py:567
  26.3 0.0 collective-permute-done.5.refs_0_
  26.3 0.8 %product.9 = bf16[512,256]{1,0:T(8,128)(2,1)S(1)} custom-call(bf16[560,256]{1,0:T(8,128)(2,1)S(1)} %collective-permute-done.5.refs_0_, bf16[544,256]{1,0:T(8,128)(2,1)S(1)} %collective-permute-done.6.refs_1_, bf16[512,64]{1,0:T(8,128)(2,1)S(1)} %get-tuple-element.84.refs_5_.refs_2_, f32[512,256]{1,0:T(8,128)S(1)} %get-tuple-element.113.refs_3_), custom_call_target="tpu_custom_call" | custom-call | flops 1000000000 | tf_op jit(solution)/shard_map/product/pallas_call | solution.py:209
  27.1 0.1 collective-permute-start.9
  27.2 1.4 %product.8 = (f32[512,256]{1,0:T(8,128)S(1)}, f32[512,256]{1,0:T(8,128)S(1)}) custom-call(bf16[560,256]{1,0:T(8,128)(2,1)S(1)} %collective-permute-done.5.refs_0_, bf16[544,256]{1,0:T(8,128)(2,1)S(1)} %collective-permute-done.6.refs_1_, bf16[512,64]{1,0:T(8,128)(2,1)S(1)} %get-tuple-element.82.refs_3_.refs_2_, ...), custom_call_target="tpu_custom_call" | custom-call | flops 1000000000 | tf_op jit(solution)/shard_map/product/pallas_call | solution.py:209
  28.6 0.2 collective-permute-done.9.refs_1_
  28.8 0.4 collective-permute-start.10
  29.2 0.6 collective-permute-start.11
  29.8 0.8 %product.7.refs_0_ = f32[512,256]{1,0:T(8,128)S(1)} custom-call(bf16[560,256]{1,0:T(8,128)(2,1)S(1)} %collective-permute-done.5.refs_0_, bf16[544,256]{1,0:T(8,128)(2,1)S(1)} %collective-permute-done.6.refs_1_, bf16[512,64]{1,0:T(8,128)(2,1)S(1)} %get-tuple-element.79.refs_2_, f32[512,256]{1,0:T(8,128)S(1)} %get-tuple-element.109.refs_3_), custom_call_target="tpu_custom_call" | custom-call | flops 1000000000 | tf_op jit(solution)/shard_map/product/pallas_call | solution.py:209
  30.6 1.5 %collective-permute-start.14 = (bf16[16,128]{1,0:T(8,128)(2,1)S(1)}, bf16[16,128]{1,0:T(8,128)(2,1)S(1)}, u32[]{:S(2)}, u32[]{:S(2)}) collective-permute-start(bf16[16,128]{1,0:T(8,128)(2,1)S(1)} %get-tuple-element.124.refs_0_), channel_id=1, source_target_pairs={{0,2},{1,3},{2,0},{3,1},{4,6},{5,7},{6,4},{7,5},{8,10},{9,11},{10,... | collective-permute-start | bytes 12296 | tf_op jit(solution)/shard_map/ppermute | solution.py:567
  32.1 0.0 collective-permute-done.10.refs_1_
  32.1 0.1 add_up.4
  32.2 0.7 %collective-permute-start.13 = (bf16[256,256]{1,0:T(8,128)(2,1)S(1)}, bf16[256,256]{1,0:T(8,128)(2,1)S(1)}, u32[]{:S(2)}, u32[]{:S(2)}) collective-permute-start(bf16[256,256]{1,0:T(8,128)(2,1)S(1)} %get-tuple-element.121.refs_2_), channel_id=1, source_target_pairs={{0,2},{1,3},{2,0},{3,1},{4,6},{5,7},{6,4},{7,5},{8,10},{9,11},{10,... | collective-permute-start | bytes 393224 | tf_op jit(solution)/shard_map/ppermute | solution.py:567
  32.9 2.2 %collective-permute-done.11.refs_1_ = bf16[256,256]{1,0:T(8,128)(2,1)S(1)} collective-permute-done((bf16[256,256]{1,0:T(8,128)(2,1)S(1)}, bf16[256,256]{1,0:T(8,128)(2,1)S(1)}, u32[]{:S(2)}, u32[]{:S(2)}) %collective-permute-start.11) | collective-permute-done | bytes 131104 | tf_op jit(solution)/shard_map/ppermute | solution.py:567
  35.1 2.7 %collective-permute-start.12 = (bf16[256,256]{1,0:T(8,128)(2,1)S(1)}, bf16[256,256]{1,0:T(8,128)(2,1)S(1)}, u32[]{:S(2)}, u32[]{:S(2)}) collective-permute-start(bf16[256,256]{1,0:T(8,128)(2,1)S(1)} %add_up.5), channel_id=1, source_target_pairs={{0,4},{1,5},{2,6},{3,7},{4,0},{5,1},{6,2},{7,3},{8,12},{9,13},{10,... | collective-permute-start | bytes 393224 | tf_op jit(solution)/shard_map/ppermute | solution.py:567
  37.8 0.0 collective-permute-done.14.refs_1_
  37.8 0.8 %top_couplings.1 = (bf16[192,384]{1,0:T(8,128)(2,1)S(1)}, bf16[192,384]{1,0:T(8,128)(2,1)S(1)}) custom-call(bf16[16,128]{1,0:T(8,128)(2,1)S(1)} %get-tuple-element.124.refs_0_, bf16[16,128]{1,0:T(8,128)(2,1)S(1)} %collective-permute-done.14.refs_1_, bf16[6,64,128]{2,1,0:T(8,128)(2,1)S(1)} %get-tuple-element.122.refs_2_.refs_4_.refs_5_), custom_call_target="tpu_custom_call" | custom-call | flops 10000000000 | tf_op jit(solution)/shard_map/top_couplings/pallas_call | solution.py:546
  38.6 4.8 %collective-permute-done.12.refs_1_ = bf16[256,256]{1,0:T(8,128)(2,1)S(1)} collective-permute-done((bf16[256,256]{1,0:T(8,128)(2,1)S(1)}, bf16[256,256]{1,0:T(8,128)(2,1)S(1)}, u32[]{:S(2)}, u32[]{:S(2)}) %collective-permute-start.12) | collective-permute-done | bytes 131104 | tf_op jit(solution)/shard_map/ppermute | solution.py:567
  43.4 0.0 collective-permute-done.13.refs_2_
  43.4 5.4 %leaves.1 = (f32[2,64,128]{2,1,0:T(8,128)}, f32[64,128]{1,0:T(8,128)S(1)}, f32[64,256]{1,0:T(8,128)S(1)}, f32[64,256]{1,0:T(8,128)S(1)}, bf16[192,256]{1,0:T(8,128)(2,1)S(1)}) custom-call(f32[256,256]{1,0:T(8,128)S(1)} %get-tuple-element.118.refs_0_, bf16[256,256]{1,0:T(8,128)(2,1)S(1)} %collective-permute-done.12.refs_1_, ...), custom_call_target="tpu_custom_call" | custom-call | flops 1000000000 | tf_op jit(solution)/shard_map/leaves/pallas_call | solution.py:366
  48.8 0.8 %collective-permute-start.17 = (bf16[192,256]{1,0:T(8,128)(2,1)S(1)}, bf16[192,256]{1,0:T(8,128)(2,1)S(1)}, u32[]{:S(2)}, u32[]{:S(2)}) collective-permute-start(bf16[192,256]{1,0:T(8,128)(2,1)S(1)} %get-tuple-element.130), channel_id=1, source_target_pairs={{0,3},{1,2},{2,1},{3,0},{4,7},{5,6},{6,5},{7,4},{8,11},{9,10},{10,... | collective-permute-start | bytes 294920 | tf_op jit(solution)/shard_map/ppermute | solution.py:567
  49.6 2.2 %collective-permute-start.16 = (bf16[192,256]{1,0:T(8,128)(2,1)S(1)}, bf16[192,256]{1,0:T(8,128)(2,1)S(1)}, u32[]{:S(2)}, u32[]{:S(2)}) collective-permute-start(bf16[192,256]{1,0:T(8,128)(2,1)S(1)} %get-tuple-element.130), channel_id=1, source_target_pairs={{0,2},{1,3},{2,0},{3,1},{4,6},{5,7},{6,4},{7,5},{8,10},{9,11},{10,... | collective-permute-start | bytes 294920 | tf_op jit(solution)/shard_map/ppermute | solution.py:567
  51.8 0.5 collective-permute-start.15
  52.4 2.0 %collective-permute-done.17.refs_4_ = bf16[192,256]{1,0:T(8,128)(2,1)S(1)} collective-permute-done((bf16[192,256]{1,0:T(8,128)(2,1)S(1)}, bf16[192,256]{1,0:T(8,128)(2,1)S(1)}, u32[]{:S(2)}, u32[]{:S(2)}) %collective-permute-start.17) | collective-permute-done | bytes 98336 | tf_op jit(solution)/shard_map/ppermute | solution.py:567
  54.4 1.1 %collective-permute-done.16.refs_3_ = bf16[192,256]{1,0:T(8,128)(2,1)S(1)} collective-permute-done((bf16[192,256]{1,0:T(8,128)(2,1)S(1)}, bf16[192,256]{1,0:T(8,128)(2,1)S(1)}, u32[]{:S(2)}, u32[]{:S(2)}) %collective-permute-start.16) | collective-permute-done | bytes 98336 | tf_op jit(solution)/shard_map/ppermute | solution.py:567
  55.5 1.0 %collective-permute-done.15.refs_2_ = bf16[192,256]{1,0:T(8,128)(2,1)S(1)} collective-permute-done((bf16[192,256]{1,0:T(8,128)(2,1)S(1)}, bf16[192,256]{1,0:T(8,128)(2,1)S(1)}, u32[]{:S(2)}, u32[]{:S(2)}) %collective-permute-start.15) | collective-permute-done | bytes 98336 | tf_op jit(solution)/shard_map/ppermute | solution.py:567
  56.4 5.8 %upper_levels.1 = (f32[3,1,64,128]{3,2,1,0:T(8,128)}, f32[2,1,64,256]{3,2,1,0:T(8,128)}) custom-call(f32[64,256]{1,0:T(8,128)S(1)} %get-tuple-element.128.refs_0_, f32[64,256]{1,0:T(8,128)S(1)} %get-tuple-element.129.refs_1_, bf16[192,256]{1,0:T(8,128)(2,1)S(1)} %collective-permute-done.15.refs_2_, bf16[192,256]{1,0:T(8,128)(2,1)S(1)} %collective-permute-done.16.refs_3_, ...), custom_call_target="tpu_custom_call" | custom-call | flops 1000000000 | tf_op jit(solution)/shard_map/upper_levels/pallas_call | solution.py:442
  (5 shorter events, 0.1 us)
Async XLA Ops:
  1.8 6.1 %collective-permute-start.2 = (bf16[16,256]{1,0:T(8,128)(2,1)S(1)}, bf16[16,256]{1,0:T(8,128)(2,1)S(1)}, u32[]{:S(2)}, u32[]{:S(2)}) collective-permute-start(bf16[16,256]{1,0:T(8,128)(2,1)S(1)} %get-tuple-element.71), channel_id=1, source_target_pairs={{0,2},{1,3},{2,0},{3,1},{4,6},{5,7},{6,4},{7,5},{8,10},{9,11},{10,... | collective-permute-start | bytes 24584 | tf_op jit(solution)/shard_map/ppermute | solution.py:567
  4.8 11.4 %collective-permute-start.1 = (bf16[544,256]{1,0:T(8,128)(2,1)S(1)}, bf16[544,256]{1,0:T(8,128)(2,1)S(1)}, u32[]{:S(2)}, u32[]{:S(2)}) collective-permute-start(bf16[544,256]{1,0:T(8,128)(2,1)S(1)} %get-tuple-element.80.refs_1_), channel_id=1, source_target_pairs={{0,16},{1,17},{2,18},{3,19},{4,20},{5,21},{6,22},{7,23},{8,24},{9,... | collective-permute-start | bytes 835592 | tf_op jit(solution)/shard_map/ppermute | solution.py:567
  6.4 9.9 %collective-permute-start = (bf16[560,256]{1,0:T(8,128)(2,1)S(1)}, bf16[560,256]{1,0:T(8,128)(2,1)S(1)}, u32[]{:S(2)}, u32[]{:S(2)}) collective-permute-start(bf16[560,256]{1,0:T(8,128)(2,1)S(1)} %get-tuple-element.103.refs_0_.refs_3_), channel_id=1, source_target_pairs={{0,1},{1,0},{2,3},{3,2},{4,5},{5,4},{6,7},{7,6},{8,9},{9,8},{10,11... | collective-permute-start | bytes 860168 | tf_op jit(solution)/shard_map/ppermute | solution.py:567
  7.9 4.7 %collective-permute-start.3 = (bf16[16,512]{1,0:T(8,128)(2,1)S(1)}, bf16[16,512]{1,0:T(8,128)(2,1)S(1)}, u32[]{:S(2)}, u32[]{:S(2)}) collective-permute-start(bf16[16,512]{1,0:T(8,128)(2,1)S(1)} %pad_maximum_fusion), channel_id=1, source_target_pairs={{0,4},{1,5},{2,6},{3,7},{4,0},{5,1},{6,2},{7,3},{8,12},{9,13},{10,... | collective-permute-start | bytes 49160 | tf_op jit(solution)/shard_map/ppermute | solution.py:567
  10.5 10.8 %collective-permute-start.7 = (bf16[544,256]{1,0:T(8,128)(2,1)S(1)}, bf16[544,256]{1,0:T(8,128)(2,1)S(1)}, u32[]{:S(2)}, u32[]{:S(2)}) collective-permute-start(bf16[544,256]{1,0:T(8,128)(2,1)S(1)} %get-tuple-element.80.refs_1_), channel_id=1, source_target_pairs={{0,1},{1,0},{2,3},{3,2},{4,5},{5,4},{6,7},{7,6},{8,9},{9,8},{10,11... | collective-permute-start | bytes 835592 | tf_op jit(solution)/shard_map/ppermute | solution.py:567
  11.0 10.2 %collective-permute-start.8 = (bf16[560,256]{1,0:T(8,128)(2,1)S(1)}, bf16[560,256]{1,0:T(8,128)(2,1)S(1)}, u32[]{:S(2)}, u32[]{:S(2)}) collective-permute-start(bf16[560,256]{1,0:T(8,128)(2,1)S(1)} %get-tuple-element.103.refs_0_.refs_3_), channel_id=1, source_target_pairs={{0,16},{1,17},{2,18},{3,19},{4,20},{5,21},{6,22},{7,23},{8,24},{9,... | collective-permute-start | bytes 860168 | tf_op jit(solution)/shard_map/ppermute | solution.py:567
  12.5 1.2 %collective-permute-start.4 = (bf16[16,1024]{1,0:T(8,128)(2,1)S(1)}, bf16[16,1024]{1,0:T(8,128)(2,1)S(1)}, u32[]{:S(2)}, u32[]{:S(2)}) collective-permute-start(bf16[16,1024]{1,0:T(8,128)(2,1)S(1)} %constant_dynamic-update-slice_fusion.refs_2_), channel_id=1, source_target_pairs={{0,8},{1,9},{2,10},{3,11},{4,12},{5,13},{6,14},{7,15},{8,0},{9,1},... | collective-permute-start | bytes 98312 | tf_op jit(solution)/shard_map/ppermute | solution.py:567
  16.3 10.0 %collective-permute-start.5 = (bf16[560,256]{1,0:T(8,128)(2,1)S(1)}, bf16[560,256]{1,0:T(8,128)(2,1)S(1)}, u32[]{:S(2)}, u32[]{:S(2)}) collective-permute-start(bf16[560,256]{1,0:T(8,128)(2,1)S(1)} %collective-permute-done.refs_0_.refs_1_), channel_id=1, source_target_pairs={{0,16},{1,17},{2,18},{3,19},{4,20},{5,21},{6,22},{7,23},{8,24},{9,... | collective-permute-start | bytes 860168 | tf_op jit(solution)/shard_map/ppermute | solution.py:567
  16.9 9.4 %collective-permute-start.6 = (bf16[544,256]{1,0:T(8,128)(2,1)S(1)}, bf16[544,256]{1,0:T(8,128)(2,1)S(1)}, u32[]{:S(2)}, u32[]{:S(2)}) collective-permute-start(bf16[544,256]{1,0:T(8,128)(2,1)S(1)} %collective-permute-done.1.refs_1_), channel_id=1, source_target_pairs={{0,1},{1,0},{2,3},{3,2},{4,5},{5,4},{6,7},{7,6},{8,9},{9,8},{10,11... | collective-permute-start | bytes 835592 | tf_op jit(solution)/shard_map/ppermute | solution.py:567
  27.1 1.6 %collective-permute-start.9 = (bf16[512,256]{1,0:T(8,128)(2,1)S(1)}, bf16[512,256]{1,0:T(8,128)(2,1)S(1)}, u32[]{:S(2)}, u32[]{:S(2)}) collective-permute-start(bf16[512,256]{1,0:T(8,128)(2,1)S(1)} %product.9), channel_id=1, source_target_pairs={{0,8},{1,9},{2,10},{3,11},{4,12},{5,13},{6,14},{7,15},{8,0},{9,1},... | collective-permute-start | bytes 786440 | tf_op jit(solution)/shard_map/ppermute | solution.py:567
  28.8 3.4 %collective-permute-start.10 = (f32[512,256]{1,0:T(8,128)S(1)}, f32[512,256]{1,0:T(8,128)S(1)}, u32[]{:S(2)}, u32[]{:S(2)}) collective-permute-start(f32[512,256]{1,0:T(8,128)S(1)} %get-tuple-element.117), channel_id=1, source_target_pairs={{0,8},{1,9},{2,10},{3,11},{4,12},{5,13},{6,14},{7,15},{8,0},{9,1},... | collective-permute-start | bytes 1572872 | tf_op jit(solution)/shard_map/ppermute | solution.py:567
  29.2 5.9 %collective-permute-start.11 = (bf16[256,256]{1,0:T(8,128)(2,1)S(1)}, bf16[256,256]{1,0:T(8,128)(2,1)S(1)}, u32[]{:S(2)}, u32[]{:S(2)}) collective-permute-start(bf16[256,256]{1,0:T(8,128)(2,1)S(1)} %get-tuple-element.120), channel_id=1, source_target_pairs={{0,2},{1,3},{2,0},{3,1},{4,6},{5,7},{6,4},{7,5},{8,10},{9,11},{10,... | collective-permute-start | bytes 393224 | tf_op jit(solution)/shard_map/ppermute | solution.py:567
  30.6 7.1 %collective-permute-start.14 = (bf16[16,128]{1,0:T(8,128)(2,1)S(1)}, bf16[16,128]{1,0:T(8,128)(2,1)S(1)}, u32[]{:S(2)}, u32[]{:S(2)}) collective-permute-start(bf16[16,128]{1,0:T(8,128)(2,1)S(1)} %get-tuple-element.124.refs_0_), channel_id=1, source_target_pairs={{0,2},{1,3},{2,0},{3,1},{4,6},{5,7},{6,4},{7,5},{8,10},{9,11},{10,... | collective-permute-start | bytes 12296 | tf_op jit(solution)/shard_map/ppermute | solution.py:567
  32.2 11.2 %collective-permute-start.13 = (bf16[256,256]{1,0:T(8,128)(2,1)S(1)}, bf16[256,256]{1,0:T(8,128)(2,1)S(1)}, u32[]{:S(2)}, u32[]{:S(2)}) collective-permute-start(bf16[256,256]{1,0:T(8,128)(2,1)S(1)} %get-tuple-element.121.refs_2_), channel_id=1, source_target_pairs={{0,2},{1,3},{2,0},{3,1},{4,6},{5,7},{6,4},{7,5},{8,10},{9,11},{10,... | collective-permute-start | bytes 393224 | tf_op jit(solution)/shard_map/ppermute | solution.py:567
  35.1 8.2 %collective-permute-start.12 = (bf16[256,256]{1,0:T(8,128)(2,1)S(1)}, bf16[256,256]{1,0:T(8,128)(2,1)S(1)}, u32[]{:S(2)}, u32[]{:S(2)}) collective-permute-start(bf16[256,256]{1,0:T(8,128)(2,1)S(1)} %add_up.5), channel_id=1, source_target_pairs={{0,4},{1,5},{2,6},{3,7},{4,0},{5,1},{6,2},{7,3},{8,12},{9,13},{10,... | collective-permute-start | bytes 393224 | tf_op jit(solution)/shard_map/ppermute | solution.py:567
  48.8 5.6 %collective-permute-start.17 = (bf16[192,256]{1,0:T(8,128)(2,1)S(1)}, bf16[192,256]{1,0:T(8,128)(2,1)S(1)}, u32[]{:S(2)}, u32[]{:S(2)}) collective-permute-start(bf16[192,256]{1,0:T(8,128)(2,1)S(1)} %get-tuple-element.130), channel_id=1, source_target_pairs={{0,3},{1,2},{2,1},{3,0},{4,7},{5,6},{6,5},{7,4},{8,11},{9,10},{10,... | collective-permute-start | bytes 294920 | tf_op jit(solution)/shard_map/ppermute | solution.py:567
  49.6 5.9 %collective-permute-start.16 = (bf16[192,256]{1,0:T(8,128)(2,1)S(1)}, bf16[192,256]{1,0:T(8,128)(2,1)S(1)}, u32[]{:S(2)}, u32[]{:S(2)}) collective-permute-start(bf16[192,256]{1,0:T(8,128)(2,1)S(1)} %get-tuple-element.130), channel_id=1, source_target_pairs={{0,2},{1,3},{2,0},{3,1},{4,6},{5,7},{6,4},{7,5},{8,10},{9,11},{10,... | collective-permute-start | bytes 294920 | tf_op jit(solution)/shard_map/ppermute | solution.py:567
  51.8 4.6 %collective-permute-start.15 = (bf16[192,256]{1,0:T(8,128)(2,1)S(1)}, bf16[192,256]{1,0:T(8,128)(2,1)S(1)}, u32[]{:S(2)}, u32[]{:S(2)}) collective-permute-start(bf16[192,256]{1,0:T(8,128)(2,1)S(1)} %get-tuple-element.130), channel_id=1, source_target_pairs={{0,1},{1,0},{2,3},{3,2},{4,5},{5,4},{6,7},{7,6},{8,9},{9,8},{10,11... | collective-permute-start | bytes 294920 | tf_op jit(solution)/shard_map/ppermute | solution.py:567

commit v5 on v4

--- a/solution.py
+++ b/solution.py
@@ -393,7 +393,7 @@
 def upper_body(picks_count, *refs):
     states = [(refs[0][...], refs[1][...])]
     rank = refs[0].shape[0]
-    for got_ref in refs[2:5]:
+    for got_ref in refs[4:1:-1]:
         high, middle, reduced = (got_ref[pl.ds(pos * rank, rank), :] for pos in range(3))
         states.append((high.astype(F32) + middle.astype(F32), reduced.astype(F32)))
     picks_ref, two_ref, other_ref, three_ref, one_ref, upper_out, top_out = refs[5:12]
@@ -454,7 +454,7 @@
         cost_estimate=COST,
         compiler_params=PARAMS,
         name="upper_levels",
-    )(skeleton, reduced, *got, picks, *couplings, interp_one)
+    )(skeleton, reduced, *got[::-1], picks, *couplings, interp_one)
 
 
 def one_hot(chosen, pool):

time: 62.5 us -> 62.1 us (level)
  no operation moved by 1% of the time
where the time goes in v5:
time: 62.1 us; the launch traced here: 61.9 us
  Pallas kernels  24.9 us (40%)
  starting transfers between devices  22.3 us (36%)
  waiting for transfers between devices  13.8 us (22%)
  between operations  0.91 us (1%)
    ppermute x18, starting transfers between devices, swap(): return lax.ppermute(value, ('row', 'col'), pairs)  22.3 us
    ppermute x18, waiting for transfers between devices, swap(): return lax.ppermute(value, ('row', 'col'), pairs)  13.8 us
    pallas_call x5, Pallas kernels, product(): pl.pallas_call(lambda *refs: product_body(span, len(halves), len(rows), *...  7.98 us
    pallas_call x1, Pallas kernels, upper_levels(): pl.pallas_call(lambda *refs: upper_body(picks.shape[0], *refs), out_shape...  5.76 us
    pallas_call x1, Pallas kernels, leaves(): pl.pallas_call(lambda *refs: leaves_body(len(others), *refs), out_shape=(...  5.42 us
    pallas_call x1, Pallas kernels, first_product(): pl.pallas_call(lambda *refs: first_product_body(gain, span, groups, len(p...  2.53 us
  transfers between devices with their start and end apart: 18, of which 9 were waited for; matrix products, arithmetic and copies ran while one was open for 0% of the time, Pallas kernels for 19%

profile of v5, /device:TPU:0, one launch (start us, length us, event | category | flops | bytes accessed | tf_op | source)
XLA Modules:
  0.0 61.9 jit_solution(17941110030237942365)
XLA Ops:
  0.6 1.1 %pack.1 = (bf16[560,256]{1,0:T(8,128)(2,1)S(1)}, bf16[544,256]{1,0:T(8,128)(2,1)S(1)}, bf16[16,256]{1,0:T(8,128)(2,1)S(1)}) custom-call(bf16[1024,256]{1,0:T(8,128)(2,1)} %bitcast.3, bf16[16,4,256]{2,1,0:T(4,128)(2,1)} %refs_1_.1, s32[2,64]{1,0:T(2,128)} %refs_2_.1, s32[1,64]{1,0:T(1,128)} %refs_3_.1, s32[4,64]{1,0:T(4,128)} %refs_4_.1, s32[2,64]{1,0:T(2,128)} %refs_5_.1), custom_call_target="tpu_custom_call" | custom-call | flops 1000000000 | tf_op jit(solution)/shard_map/pack/pallas_call | solution.py:120
  1.8 3.1 %collective-permute-start.2 = (bf16[16,256]{1,0:T(8,128)(2,1)S(1)}, bf16[16,256]{1,0:T(8,128)(2,1)S(1)}, u32[]{:S(2)}, u32[]{:S(2)}) collective-permute-start(bf16[16,256]{1,0:T(8,128)(2,1)S(1)} %get-tuple-element.71), channel_id=1, source_target_pairs={{0,2},{1,3},{2,0},{3,1},{4,6},{5,7},{6,4},{7,5},{8,10},{9,11},{10,... | collective-permute-start | bytes 24584 | tf_op jit(solution)/shard_map/ppermute | solution.py:567
  4.8 1.5 %collective-permute-start.1 = (bf16[544,256]{1,0:T(8,128)(2,1)S(1)}, bf16[544,256]{1,0:T(8,128)(2,1)S(1)}, u32[]{:S(2)}, u32[]{:S(2)}) collective-permute-start(bf16[544,256]{1,0:T(8,128)(2,1)S(1)} %get-tuple-element.80.refs_1_), channel_id=1, source_target_pairs={{0,16},{1,17},{2,18},{3,19},{4,20},{5,21},{6,22},{7,23},{8,24},{9,... | collective-permute-start | bytes 835592 | tf_op jit(solution)/shard_map/ppermute | solution.py:567
  6.4 1.5 %collective-permute-start = (bf16[560,256]{1,0:T(8,128)(2,1)S(1)}, bf16[560,256]{1,0:T(8,128)(2,1)S(1)}, u32[]{:S(2)}, u32[]{:S(2)}) collective-permute-start(bf16[560,256]{1,0:T(8,128)(2,1)S(1)} %get-tuple-element.103.refs_0_.refs_3_), channel_id=1, source_target_pairs={{0,1},{1,0},{2,3},{3,2},{4,5},{5,4},{6,7},{7,6},{8,9},{9,8},{10,11... | collective-permute-start | bytes 860168 | tf_op jit(solution)/shard_map/ppermute | solution.py:567
  7.9 0.0 collective-permute-done.2
  7.9 2.6 %collective-permute-start.3 = (bf16[16,512]{1,0:T(8,128)(2,1)S(1)}, bf16[16,512]{1,0:T(8,128)(2,1)S(1)}, u32[]{:S(2)}, u32[]{:S(2)}) collective-permute-start(bf16[16,512]{1,0:T(8,128)(2,1)S(1)} %pad_maximum_fusion), channel_id=1, source_target_pairs={{0,4},{1,5},{2,6},{3,7},{4,0},{5,1},{6,2},{7,3},{8,12},{9,13},{10,... | collective-permute-start | bytes 49160 | tf_op jit(solution)/shard_map/ppermute | solution.py:567
  10.5 0.6 collective-permute-start.7
  11.0 1.5 %collective-permute-start.8 = (bf16[560,256]{1,0:T(8,128)(2,1)S(1)}, bf16[560,256]{1,0:T(8,128)(2,1)S(1)}, u32[]{:S(2)}, u32[]{:S(2)}) collective-permute-start(bf16[560,256]{1,0:T(8,128)(2,1)S(1)} %get-tuple-element.103.refs_0_.refs_3_), channel_id=1, source_target_pairs={{0,16},{1,17},{2,18},{3,19},{4,20},{5,21},{6,22},{7,23},{8,24},{9,... | collective-permute-start | bytes 860168 | tf_op jit(solution)/shard_map/ppermute | solution.py:567
  12.5 0.0 collective-permute-done.3
  12.5 0.0 collective-permute-start.4
  12.5 1.2 %collective-permute-done.4.refs_3_ = bf16[16,1024]{1,0:T(8,128)(2,1)S(1)} collective-permute-done((bf16[16,1024]{1,0:T(8,128)(2,1)S(1)}, bf16[16,1024]{1,0:T(8,128)(2,1)S(1)}, u32[]{:S(2)}, u32[]{:S(2)}) %collective-permute-start.4) | collective-permute-done | bytes 32800 | tf_op jit(solution)/shard_map/ppermute | solution.py:567
  13.7 2.5 %first_product.1 = (bf16[512,64]{1,0:T(8,128)(2,1)S(1)}, bf16[512,64]{1,0:T(8,128)(2,1)S(1)}, bf16[512,64]{1,0:T(8,128)(2,1)S(1)}, bf16[512,64]{1,0:T(8,128)(2,1...) custom-call(bf16[560,256]{1,0:T(8,128)(2,1)S(1)} %get-tuple-element.10, ...), custom_call_target="tpu_custom_call" | custom-call | flops 1000000000 | tf_op jit(solution)/shard_map/first_product/pallas_call | solution.py:181
  16.3 0.0 collective-permute-done.1.refs_1_
  16.3 0.0 collective-permute-done.refs_0_.refs_1_
  16.3 0.6 collective-permute-start.5
  16.9 1.5 %collective-permute-start.6 = (bf16[544,256]{1,0:T(8,128)(2,1)S(1)}, bf16[544,256]{1,0:T(8,128)(2,1)S(1)}, u32[]{:S(2)}, u32[]{:S(2)}) collective-permute-start(bf16[544,256]{1,0:T(8,128)(2,1)S(1)} %collective-permute-done.1.refs_1_), channel_id=1, source_target_pairs={{0,1},{1,0},{2,3},{3,2},{4,5},{5,4},{6,7},{7,6},{8,9},{9,8},{10,11... | collective-permute-start | bytes 835592 | tf_op jit(solution)/shard_map/ppermute | solution.py:567
  18.4 2.5 %product.5 = (f32[512,256]{1,0:T(8,128)S(1)}, f32[512,256]{1,0:T(8,128)S(1)}, f32[512,256]{1,0:T(8,128)S(1)}, f32[512,256]{1,0:T(8,128)S(1)}) custom-call(bf16[560,256]{1,0:T(8,128)(2,1)S(1)} %collective-permute-done.refs_0_.refs_1_, bf16[544,256]{1,0:T(8,128)(2,1)S(1)} %collective-permute-done.1.refs_1_, bf16[512,64]{1,0:T(8,128)(2,1)S(1)} %get-tuple-element.79.refs_2_, ...), custom_call_target="tpu_custom_call" | custom-call | tf_op jit(solution)/shard_map/product/pallas_call | solution.py:209
  20.9 0.3 collective-permute-done.7.refs_0_
  21.2 0.0 collective-permute-done.8.refs_1_
  21.2 2.5 %product.6 = (f32[512,256]{1,0:T(8,128)S(1)}, f32[512,256]{1,0:T(8,128)S(1)}, f32[512,256]{1,0:T(8,128)S(1)}, f32[512,256]{1,0:T(8,128)S(1)}) custom-call(bf16[544,256]{1,0:T(8,128)(2,1)S(1)} %collective-permute-done.7.refs_0_, bf16[560,256]{1,0:T(8,128)(2,1)S(1)} %collective-permute-done.8.refs_1_, bf16[512,64]{1,0:T(8,128)(2,1)S(1)} %get-tuple-element.79.refs_2_, ...), custom_call_target="tpu_custom_call" | custom-call | flops 1000000000 | tf_op jit(solution)/shard_map/product/pallas_call | solution.py:209
  23.7 1.2 %skeletons.1 = (bf16[6,64,128]{2,1,0:T(8,128)(2,1)S(1)}, bf16[192,384]{1,0:T(8,128)(2,1)S(1)}, bf16[192,384]{1,0:T(8,128)(2,1)S(1)}, bf16[16,128]{1,0:T(8,128)(2,1)S(1)}) custom-call(bf16[560,256]{1,0:T(8,128)(2,1)S(1)} %get-tuple-element.103.refs_0_.refs_3_, bf16[560,256]{1,0:T(8,128)(2,1)S(1)} %collective-permute-done.refs_0_.refs_1_), custom_call_target="tpu_custom_call" | custom-call | flops 1000000000 | tf_op jit(solution)/shard_map/skeletons/pallas_call | solution.py:519
  24.9 1.4 %collective-permute-done.6.refs_1_ = bf16[544,256]{1,0:T(8,128)(2,1)S(1)} collective-permute-done((bf16[544,256]{1,0:T(8,128)(2,1)S(1)}, bf16[544,256]{1,0:T(8,128)(2,1)S(1)}, u32[]{:S(2)}, u32[]{:S(2)}) %collective-permute-start.6) | collective-permute-done | bytes 278560 | tf_op jit(solution)/shard_map/ppermute | solution.py:567
  26.3 0.0 collective-permute-done.5.refs_0_
  26.3 0.8 %product.9 = bf16[512,256]{1,0:T(8,128)(2,1)S(1)} custom-call(bf16[560,256]{1,0:T(8,128)(2,1)S(1)} %collective-permute-done.5.refs_0_, bf16[544,256]{1,0:T(8,128)(2,1)S(1)} %collective-permute-done.6.refs_1_, bf16[512,64]{1,0:T(8,128)(2,1)S(1)} %get-tuple-element.84.refs_5_.refs_2_, f32[512,256]{1,0:T(8,128)S(1)} %get-tuple-element.113.refs_3_), custom_call_target="tpu_custom_call" | custom-call | flops 1000000000 | tf_op jit(solution)/shard_map/product/pallas_call | solution.py:209
  27.1 0.1 collective-permute-start.9
  27.2 1.4 %product.8 = (f32[512,256]{1,0:T(8,128)S(1)}, f32[512,256]{1,0:T(8,128)S(1)}) custom-call(bf16[560,256]{1,0:T(8,128)(2,1)S(1)} %collective-permute-done.5.refs_0_, bf16[544,256]{1,0:T(8,128)(2,1)S(1)} %collective-permute-done.6.refs_1_, bf16[512,64]{1,0:T(8,128)(2,1)S(1)} %get-tuple-element.82.refs_3_.refs_2_, ...), custom_call_target="tpu_custom_call" | custom-call | flops 1000000000 | tf_op jit(solution)/shard_map/product/pallas_call | solution.py:209
  28.6 0.2 collective-permute-done.9.refs_1_
  28.8 0.4 collective-permute-start.10
  29.2 0.6 collective-permute-start.11
  29.8 0.8 %product.7.refs_0_ = f32[512,256]{1,0:T(8,128)S(1)} custom-call(bf16[560,256]{1,0:T(8,128)(2,1)S(1)} %collective-permute-done.5.refs_0_, bf16[544,256]{1,0:T(8,128)(2,1)S(1)} %collective-permute-done.6.refs_1_, bf16[512,64]{1,0:T(8,128)(2,1)S(1)} %get-tuple-element.79.refs_2_, f32[512,256]{1,0:T(8,128)S(1)} %get-tuple-element.109.refs_3_), custom_call_target="tpu_custom_call" | custom-call | flops 1000000000 | tf_op jit(solution)/shard_map/product/pallas_call | solution.py:209
  30.6 1.5 %collective-permute-start.14 = (bf16[16,128]{1,0:T(8,128)(2,1)S(1)}, bf16[16,128]{1,0:T(8,128)(2,1)S(1)}, u32[]{:S(2)}, u32[]{:S(2)}) collective-permute-start(bf16[16,128]{1,0:T(8,128)(2,1)S(1)} %get-tuple-element.124.refs_0_), channel_id=1, source_target_pairs={{0,2},{1,3},{2,0},{3,1},{4,6},{5,7},{6,4},{7,5},{8,10},{9,11},{10,... | collective-permute-start | bytes 12296 | tf_op jit(solution)/shard_map/ppermute | solution.py:567
  32.1 0.0 collective-permute-done.10.refs_1_
  32.1 0.1 add_up.4
  32.2 0.7 %collective-permute-start.13 = (bf16[256,256]{1,0:T(8,128)(2,1)S(1)}, bf16[256,256]{1,0:T(8,128)(2,1)S(1)}, u32[]{:S(2)}, u32[]{:S(2)}) collective-permute-start(bf16[256,256]{1,0:T(8,128)(2,1)S(1)} %get-tuple-element.121.refs_2_), channel_id=1, source_target_pairs={{0,2},{1,3},{2,0},{3,1},{4,6},{5,7},{6,4},{7,5},{8,10},{9,11},{10,... | collective-permute-start | bytes 393224 | tf_op jit(solution)/shard_map/ppermute | solution.py:567
  32.9 2.2 %collective-permute-done.11.refs_1_ = bf16[256,256]{1,0:T(8,128)(2,1)S(1)} collective-permute-done((bf16[256,256]{1,0:T(8,128)(2,1)S(1)}, bf16[256,256]{1,0:T(8,128)(2,1)S(1)}, u32[]{:S(2)}, u32[]{:S(2)}) %collective-permute-start.11) | collective-permute-done | bytes 131104 | tf_op jit(solution)/shard_map/ppermute | solution.py:567
  35.1 2.7 %collective-permute-start.12 = (bf16[256,256]{1,0:T(8,128)(2,1)S(1)}, bf16[256,256]{1,0:T(8,128)(2,1)S(1)}, u32[]{:S(2)}, u32[]{:S(2)}) collective-permute-start(bf16[256,256]{1,0:T(8,128)(2,1)S(1)} %add_up.5), channel_id=1, source_target_pairs={{0,4},{1,5},{2,6},{3,7},{4,0},{5,1},{6,2},{7,3},{8,12},{9,13},{10,... | collective-permute-start | bytes 393224 | tf_op jit(solution)/shard_map/ppermute | solution.py:567
  37.8 0.0 collective-permute-done.14.refs_1_
  37.8 0.8 %top_couplings.1 = (bf16[192,384]{1,0:T(8,128)(2,1)S(1)}, bf16[192,384]{1,0:T(8,128)(2,1)S(1)}) custom-call(bf16[16,128]{1,0:T(8,128)(2,1)S(1)} %get-tuple-element.124.refs_0_, bf16[16,128]{1,0:T(8,128)(2,1)S(1)} %collective-permute-done.14.refs_1_, bf16[6,64,128]{2,1,0:T(8,128)(2,1)S(1)} %get-tuple-element.122.refs_2_.refs_4_.refs_5_), custom_call_target="tpu_custom_call" | custom-call | flops 10000000000 | tf_op jit(solution)/shard_map/top_couplings/pallas_call | solution.py:546
  38.6 4.8 %collective-permute-done.12.refs_1_ = bf16[256,256]{1,0:T(8,128)(2,1)S(1)} collective-permute-done((bf16[256,256]{1,0:T(8,128)(2,1)S(1)}, bf16[256,256]{1,0:T(8,128)(2,1)S(1)}, u32[]{:S(2)}, u32[]{:S(2)}) %collective-permute-start.12) | collective-permute-done | bytes 131104 | tf_op jit(solution)/shard_map/ppermute | solution.py:567
  43.4 0.0 collective-permute-done.13.refs_2_
  43.4 5.4 %leaves.1 = (f32[2,64,128]{2,1,0:T(8,128)}, f32[64,128]{1,0:T(8,128)S(1)}, f32[64,256]{1,0:T(8,128)S(1)}, f32[64,256]{1,0:T(8,128)S(1)}, bf16[192,256]{1,0:T(8,128)(2,1)S(1)}) custom-call(f32[256,256]{1,0:T(8,128)S(1)} %get-tuple-element.118.refs_0_, bf16[256,256]{1,0:T(8,128)(2,1)S(1)} %collective-permute-done.12.refs_1_, ...), custom_call_target="tpu_custom_call" | custom-call | flops 1000000000 | tf_op jit(solution)/shard_map/leaves/pallas_call | solution.py:366
  48.8 1.6 %collective-permute-start.17 = (bf16[192,256]{1,0:T(8,128)(2,1)S(1)}, bf16[192,256]{1,0:T(8,128)(2,1)S(1)}, u32[]{:S(2)}, u32[]{:S(2)}) collective-permute-start(bf16[192,256]{1,0:T(8,128)(2,1)S(1)} %get-tuple-element.130), channel_id=1, source_target_pairs={{0,1},{1,0},{2,3},{3,2},{4,5},{5,4},{6,7},{7,6},{8,9},{9,8},{10,11... | collective-permute-start | bytes 294920 | tf_op jit(solution)/shard_map/ppermute | solution.py:567
  50.4 0.0 collective-permute-start.16
  50.4 2.0 %collective-permute-start.15 = (bf16[192,256]{1,0:T(8,128)(2,1)S(1)}, bf16[192,256]{1,0:T(8,128)(2,1)S(1)}, u32[]{:S(2)}, u32[]{:S(2)}) collective-permute-start(bf16[192,256]{1,0:T(8,128)(2,1)S(1)} %get-tuple-element.130), channel_id=1, source_target_pairs={{0,3},{1,2},{2,1},{3,0},{4,7},{5,6},{6,5},{7,4},{8,11},{9,10},{10,... | collective-permute-start | bytes 294920 | tf_op jit(solution)/shard_map/ppermute | solution.py:567
  52.4 1.9 %collective-permute-done.17.refs_4_ = bf16[192,256]{1,0:T(8,128)(2,1)S(1)} collective-permute-done((bf16[192,256]{1,0:T(8,128)(2,1)S(1)}, bf16[192,256]{1,0:T(8,128)(2,1)S(1)}, u32[]{:S(2)}, u32[]{:S(2)}) %collective-permute-start.17) | collective-permute-done | bytes 98336 | tf_op jit(solution)/shard_map/ppermute | solution.py:567
  54.2 0.7 %collective-permute-done.16.refs_3_ = bf16[192,256]{1,0:T(8,128)(2,1)S(1)} collective-permute-done((bf16[192,256]{1,0:T(8,128)(2,1)S(1)}, bf16[192,256]{1,0:T(8,128)(2,1)S(1)}, u32[]{:S(2)}, u32[]{:S(2)}) %collective-permute-start.16) | collective-permute-done | bytes 98336 | tf_op jit(solution)/shard_map/ppermute | solution.py:567
  55.0 1.0 %collective-permute-done.15.refs_2_ = bf16[192,256]{1,0:T(8,128)(2,1)S(1)} collective-permute-done((bf16[192,256]{1,0:T(8,128)(2,1)S(1)}, bf16[192,256]{1,0:T(8,128)(2,1)S(1)}, u32[]{:S(2)}, u32[]{:S(2)}) %collective-permute-start.15) | collective-permute-done | bytes 98336 | tf_op jit(solution)/shard_map/ppermute | solution.py:567
  56.0 5.8 %upper_levels.1 = (f32[3,1,64,128]{3,2,1,0:T(8,128)}, f32[2,1,64,256]{3,2,1,0:T(8,128)}) custom-call(f32[64,256]{1,0:T(8,128)S(1)} %get-tuple-element.128.refs_0_, f32[64,256]{1,0:T(8,128)S(1)} %get-tuple-element.129.refs_1_, bf16[192,256]{1,0:T(8,128)(2,1)S(1)} %collective-permute-done.15.refs_2_, bf16[192,256]{1,0:T(8,128)(2,1)S(1)} %collective-permute-done.16.refs_3_, ...), custom_call_target="tpu_custom_call" | custom-call | flops 1000000000 | tf_op jit(solution)/shard_map/upper_levels/pallas_call | solution.py:442
  (5 shorter events, 0.1 us)
Async XLA Ops:
  1.8 6.1 %collective-permute-start.2 = (bf16[16,256]{1,0:T(8,128)(2,1)S(1)}, bf16[16,256]{1,0:T(8,128)(2,1)S(1)}, u32[]{:S(2)}, u32[]{:S(2)}) collective-permute-start(bf16[16,256]{1,0:T(8,128)(2,1)S(1)} %get-tuple-element.71), channel_id=1, source_target_pairs={{0,2},{1,3},{2,0},{3,1},{4,6},{5,7},{6,4},{7,5},{8,10},{9,11},{10,... | collective-permute-start | bytes 24584 | tf_op jit(solution)/shard_map/ppermute | solution.py:567
  4.8 11.4 %collective-permute-start.1 = (bf16[544,256]{1,0:T(8,128)(2,1)S(1)}, bf16[544,256]{1,0:T(8,128)(2,1)S(1)}, u32[]{:S(2)}, u32[]{:S(2)}) collective-permute-start(bf16[544,256]{1,0:T(8,128)(2,1)S(1)} %get-tuple-element.80.refs_1_), channel_id=1, source_target_pairs={{0,16},{1,17},{2,18},{3,19},{4,20},{5,21},{6,22},{7,23},{8,24},{9,... | collective-permute-start | bytes 835592 | tf_op jit(solution)/shard_map/ppermute | solution.py:567
  6.4 9.9 %collective-permute-start = (bf16[560,256]{1,0:T(8,128)(2,1)S(1)}, bf16[560,256]{1,0:T(8,128)(2,1)S(1)}, u32[]{:S(2)}, u32[]{:S(2)}) collective-permute-start(bf16[560,256]{1,0:T(8,128)(2,1)S(1)} %get-tuple-element.103.refs_0_.refs_3_), channel_id=1, source_target_pairs={{0,1},{1,0},{2,3},{3,2},{4,5},{5,4},{6,7},{7,6},{8,9},{9,8},{10,11... | collective-permute-start | bytes 860168 | tf_op jit(solution)/shard_map/ppermute | solution.py:567
  7.9 4.7 %collective-permute-start.3 = (bf16[16,512]{1,0:T(8,128)(2,1)S(1)}, bf16[16,512]{1,0:T(8,128)(2,1)S(1)}, u32[]{:S(2)}, u32[]{:S(2)}) collective-permute-start(bf16[16,512]{1,0:T(8,128)(2,1)S(1)} %pad_maximum_fusion), channel_id=1, source_target_pairs={{0,4},{1,5},{2,6},{3,7},{4,0},{5,1},{6,2},{7,3},{8,12},{9,13},{10,... | collective-permute-start | bytes 49160 | tf_op jit(solution)/shard_map/ppermute | solution.py:567
  10.5 10.8 %collective-permute-start.7 = (bf16[544,256]{1,0:T(8,128)(2,1)S(1)}, bf16[544,256]{1,0:T(8,128)(2,1)S(1)}, u32[]{:S(2)}, u32[]{:S(2)}) collective-permute-start(bf16[544,256]{1,0:T(8,128)(2,1)S(1)} %get-tuple-element.80.refs_1_), channel_id=1, source_target_pairs={{0,1},{1,0},{2,3},{3,2},{4,5},{5,4},{6,7},{7,6},{8,9},{9,8},{10,11... | collective-permute-start | bytes 835592 | tf_op jit(solution)/shard_map/ppermute | solution.py:567
  11.0 10.2 %collective-permute-start.8 = (bf16[560,256]{1,0:T(8,128)(2,1)S(1)}, bf16[560,256]{1,0:T(8,128)(2,1)S(1)}, u32[]{:S(2)}, u32[]{:S(2)}) collective-permute-start(bf16[560,256]{1,0:T(8,128)(2,1)S(1)} %get-tuple-element.103.refs_0_.refs_3_), channel_id=1, source_target_pairs={{0,16},{1,17},{2,18},{3,19},{4,20},{5,21},{6,22},{7,23},{8,24},{9,... | collective-permute-start | bytes 860168 | tf_op jit(solution)/shard_map/ppermute | solution.py:567
  12.5 1.2 %collective-permute-start.4 = (bf16[16,1024]{1,0:T(8,128)(2,1)S(1)}, bf16[16,1024]{1,0:T(8,128)(2,1)S(1)}, u32[]{:S(2)}, u32[]{:S(2)}) collective-permute-start(bf16[16,1024]{1,0:T(8,128)(2,1)S(1)} %constant_dynamic-update-slice_fusion.refs_2_), channel_id=1, source_target_pairs={{0,8},{1,9},{2,10},{3,11},{4,12},{5,13},{6,14},{7,15},{8,0},{9,1},... | collective-permute-start | bytes 98312 | tf_op jit(solution)/shard_map/ppermute | solution.py:567
  16.3 10.0 %collective-permute-start.5 = (bf16[560,256]{1,0:T(8,128)(2,1)S(1)}, bf16[560,256]{1,0:T(8,128)(2,1)S(1)}, u32[]{:S(2)}, u32[]{:S(2)}) collective-permute-start(bf16[560,256]{1,0:T(8,128)(2,1)S(1)} %collective-permute-done.refs_0_.refs_1_), channel_id=1, source_target_pairs={{0,16},{1,17},{2,18},{3,19},{4,20},{5,21},{6,22},{7,23},{8,24},{9,... | collective-permute-start | bytes 860168 | tf_op jit(solution)/shard_map/ppermute | solution.py:567
  16.9 9.4 %collective-permute-start.6 = (bf16[544,256]{1,0:T(8,128)(2,1)S(1)}, bf16[544,256]{1,0:T(8,128)(2,1)S(1)}, u32[]{:S(2)}, u32[]{:S(2)}) collective-permute-start(bf16[544,256]{1,0:T(8,128)(2,1)S(1)} %collective-permute-done.1.refs_1_), channel_id=1, source_target_pairs={{0,1},{1,0},{2,3},{3,2},{4,5},{5,4},{6,7},{7,6},{8,9},{9,8},{10,11... | collective-permute-start | bytes 835592 | tf_op jit(solution)/shard_map/ppermute | solution.py:567
  27.1 1.6 %collective-permute-start.9 = (bf16[512,256]{1,0:T(8,128)(2,1)S(1)}, bf16[512,256]{1,0:T(8,128)(2,1)S(1)}, u32[]{:S(2)}, u32[]{:S(2)}) collective-permute-start(bf16[512,256]{1,0:T(8,128)(2,1)S(1)} %product.9), channel_id=1, source_target_pairs={{0,8},{1,9},{2,10},{3,11},{4,12},{5,13},{6,14},{7,15},{8,0},{9,1},... | collective-permute-start | bytes 786440 | tf_op jit(solution)/shard_map/ppermute | solution.py:567
  28.8 3.4 %collective-permute-start.10 = (f32[512,256]{1,0:T(8,128)S(1)}, f32[512,256]{1,0:T(8,128)S(1)}, u32[]{:S(2)}, u32[]{:S(2)}) collective-permute-start(f32[512,256]{1,0:T(8,128)S(1)} %get-tuple-element.117), channel_id=1, source_target_pairs={{0,8},{1,9},{2,10},{3,11},{4,12},{5,13},{6,14},{7,15},{8,0},{9,1},... | collective-permute-start | bytes 1572872 | tf_op jit(solution)/shard_map/ppermute | solution.py:567
  29.2 5.9 %collective-permute-start.11 = (bf16[256,256]{1,0:T(8,128)(2,1)S(1)}, bf16[256,256]{1,0:T(8,128)(2,1)S(1)}, u32[]{:S(2)}, u32[]{:S(2)}) collective-permute-start(bf16[256,256]{1,0:T(8,128)(2,1)S(1)} %get-tuple-element.120), channel_id=1, source_target_pairs={{0,2},{1,3},{2,0},{3,1},{4,6},{5,7},{6,4},{7,5},{8,10},{9,11},{10,... | collective-permute-start | bytes 393224 | tf_op jit(solution)/shard_map/ppermute | solution.py:567
  30.6 7.1 %collective-permute-start.14 = (bf16[16,128]{1,0:T(8,128)(2,1)S(1)}, bf16[16,128]{1,0:T(8,128)(2,1)S(1)}, u32[]{:S(2)}, u32[]{:S(2)}) collective-permute-start(bf16[16,128]{1,0:T(8,128)(2,1)S(1)} %get-tuple-element.124.refs_0_), channel_id=1, source_target_pairs={{0,2},{1,3},{2,0},{3,1},{4,6},{5,7},{6,4},{7,5},{8,10},{9,11},{10,... | collective-permute-start | bytes 12296 | tf_op jit(solution)/shard_map/ppermute | solution.py:567
  32.2 11.2 %collective-permute-start.13 = (bf16[256,256]{1,0:T(8,128)(2,1)S(1)}, bf16[256,256]{1,0:T(8,128)(2,1)S(1)}, u32[]{:S(2)}, u32[]{:S(2)}) collective-permute-start(bf16[256,256]{1,0:T(8,128)(2,1)S(1)} %get-tuple-element.121.refs_2_), channel_id=1, source_target_pairs={{0,2},{1,3},{2,0},{3,1},{4,6},{5,7},{6,4},{7,5},{8,10},{9,11},{10,... | collective-permute-start | bytes 393224 | tf_op jit(solution)/shard_map/ppermute | solution.py:567
  35.1 8.2 %collective-permute-start.12 = (bf16[256,256]{1,0:T(8,128)(2,1)S(1)}, bf16[256,256]{1,0:T(8,128)(2,1)S(1)}, u32[]{:S(2)}, u32[]{:S(2)}) collective-permute-start(bf16[256,256]{1,0:T(8,128)(2,1)S(1)} %add_up.5), channel_id=1, source_target_pairs={{0,4},{1,5},{2,6},{3,7},{4,0},{5,1},{6,2},{7,3},{8,12},{9,13},{10,... | collective-permute-start | bytes 393224 | tf_op jit(solution)/shard_map/ppermute | solution.py:567
  48.8 5.4 %collective-permute-start.17 = (bf16[192,256]{1,0:T(8,128)(2,1)S(1)}, bf16[192,256]{1,0:T(8,128)(2,1)S(1)}, u32[]{:S(2)}, u32[]{:S(2)}) collective-permute-start(bf16[192,256]{1,0:T(8,128)(2,1)S(1)} %get-tuple-element.130), channel_id=1, source_target_pairs={{0,1},{1,0},{2,3},{3,2},{4,5},{5,4},{6,7},{7,6},{8,9},{9,8},{10,11... | collective-permute-start | bytes 294920 | tf_op jit(solution)/shard_map/ppermute | solution.py:567
  50.4 4.6 %collective-permute-start.16 = (bf16[192,256]{1,0:T(8,128)(2,1)S(1)}, bf16[192,256]{1,0:T(8,128)(2,1)S(1)}, u32[]{:S(2)}, u32[]{:S(2)}) collective-permute-start(bf16[192,256]{1,0:T(8,128)(2,1)S(1)} %get-tuple-element.130), channel_id=1, source_target_pairs={{0,2},{1,3},{2,0},{3,1},{4,6},{5,7},{6,4},{7,5},{8,10},{9,11},{10,... | collective-permute-start | bytes 294920 | tf_op jit(solution)/shard_map/ppermute | solution.py:567
  50.4 5.6 %collective-permute-start.15 = (bf16[192,256]{1,0:T(8,128)(2,1)S(1)}, bf16[192,256]{1,0:T(8,128)(2,1)S(1)}, u32[]{:S(2)}, u32[]{:S(2)}) collective-permute-start(bf16[192,256]{1,0:T(8,128)(2,1)S(1)} %get-tuple-element.130), channel_id=1, source_target_pairs={{0,3},{1,2},{2,1},{3,0},{4,7},{5,6},{6,5},{7,4},{8,11},{9,10},{10,... | collective-permute-start | bytes 294920 | tf_op jit(solution)/shard_map/ppermute | solution.py:567

commit v6 on v5

--- a/solution.py
+++ b/solution.py
@@ -235,6 +235,27 @@
     )(mine, theirs, *after)
 
 
+def near_up_body(mine_ref, theirs_ref, points_ref, own_ref, sent_ref):
+    span, samples = own_ref.shape
+    own_ref[...] = mine_ref[pl.ds(0, span), :] + theirs_ref[pl.ds(0, span), :]
+    place = pl.ds(span, span)
+    sent_ref[pl.ds(0, span), :] = (mine_ref[place, :] + theirs_ref[place, :]).astype(BF16)
+    rows, width = points_ref.shape
+    rest = jnp.zeros((rows, samples - width), BF16)
+    sent_ref[pl.ds(span, rows), :] = jnp.concatenate([points_ref[...], rest], axis=1)
+
+
+def near_up(mine, theirs, points, span):
+    samples = mine.shape[1]
+    return pl.pallas_call(
+        near_up_body,
+        out_shape=(vmem((span, samples), F32), vmem((span + points.shape[0], samples), BF16)),
+        cost_estimate=COST,
+        compiler_params=PARAMS,
+        name="near_up",
+    )(mine, theirs, points)
+
+
 def wide_product(first, second):
     high, middle, low = split(first)
     other_high, other_middle, other_low = split(second)
@@ -335,7 +356,7 @@
     leaf_ref, upper_ref, skeleton_ref, reduced_ref, sent_ref, held_ref, sem = refs[-7:]
     total = own_ref[...]
     for other in others:
-        total = total + other[...].astype(F32)
+        total = total + other[pl.ds(0, total.shape[0]), :].astype(F32)
     count = total.shape[0] // LEAF
     stacks = [total[leaf * LEAF : (leaf + 1) * LEAF] for leaf in range(count)]
     skeletons = [select_rows(picks_ref[leaf], stack) for leaf, stack in enumerate(stacks)]
@@ -533,7 +554,9 @@
 def top_couplings_body(gain, mine_ref, theirs_ref, picks_ref, other_ref, three_ref):
     count, rank, _ = picks_ref.shape
     picks = [picks_ref[count - pos].astype(F32).T for pos in (3, 2, 1)]
-    mine, theirs = mine_ref[...].astype(F32), theirs_ref[...].astype(F32)
+    rows, width = mine_ref.shape
+    mine = mine_ref[...].astype(F32)
+    theirs = theirs_ref[pl.ds(theirs_ref.shape[0] - rows, rows), :width].astype(F32)
     couple(theirs[:, :rank], theirs[:, rank:], picks[1], gain, other_ref)
     mine, theirs = over(mine, picks[0], 1, 0), over(theirs, picks[1], 1, 0)
     mine_first = first_of_pair(3)
@@ -610,7 +633,7 @@
     arrived = swap(sent, 0, 2)
     from_sibling = swap(theirs, 1, 0)
     (mine,) = product(diagonal, feats[:1], totals[:1], span)
-    own_sum, near_sent = add_up(mine, from_sibling, [([0], F32), ([1], BF16)], span)
+    own_sum, near_sent = near_up(mine, from_sibling, points_two, span)
     near_sum = swap(near_sent, 0, 2)
     received = []
     chunks = list(range(2, line, 2))
@@ -628,8 +651,7 @@
         chunks = [chunks[pos] for pos in kept_places]
         bit *= 2
     received.append(near_sum)
-    other_points = swap(points_two, 0, 2)
-    later = top_couplings(points_two, other_points, picks, gain)
+    later = top_couplings(points_two, near_sum, picks, gain)
 
     leaf_interp, interp_one, skeleton, reduced, sent = leaves(
         own_sum, received, first, picks, couplings_one, later, leaf_skeleton.shape[0]

time: 62.1 us -> 62.6 us (level)
  waiting for transfers between devices: 13.8 us -> 15 us
  starting transfers between devices: 22.3 us -> 21.6 us
    ppermute x18 -> x17, waiting for transfers between devices: 13.8 us -> 15 us  [swap(): return lax.ppermute(value, ('row', 'col'), pairs)]
    ppermute x18 -> x17, starting transfers between devices: 22.3 us -> 21.6 us  [swap(): return lax.ppermute(value, ('row', 'col'), pairs)]
  transfers between devices with their start and end apart: 18 -> 17, of which waited for: 9 -> 10; matrix products, arithmetic and copies ran while one was open for 0% -> 0% of each run, Pallas kernels for 19% -> 19%
where the time goes in v6:
time: 62.6 us; the launch traced here: 62.5 us
  Pallas kernels  25.1 us (40%)
  starting transfers between devices  21.6 us (35%)
  waiting for transfers between devices  15 us (24%)
  between operations  0.91 us (1%)
    ppermute x17, starting transfers between devices, swap(): return lax.ppermute(value, ('row', 'col'), pairs)  21.6 us
    ppermute x17, waiting for transfers between devices, swap(): return lax.ppermute(value, ('row', 'col'), pairs)  15 us
    pallas_call x5, Pallas kernels, product(): pl.pallas_call(lambda *refs: product_body(span, len(halves), len(rows), *...  7.98 us
    pallas_call x1, Pallas kernels, upper_levels(): pl.pallas_call(lambda *refs: upper_body(picks.shape[0], *refs), out_shape...  5.76 us
    pallas_call x1, Pallas kernels, leaves(): pl.pallas_call(lambda *refs: leaves_body(len(others), *refs), out_shape=(...  5.61 us
    pallas_call x1, Pallas kernels, first_product(): pl.pallas_call(lambda *refs: first_product_body(gain, span, groups, len(p...  2.53 us
  transfers between devices with their start and end apart: 17, of which 10 were waited for; matrix products, arithmetic and copies ran while one was open for 0% of the time, Pallas kernels for 19%

profile of v6, /device:TPU:0, one launch (start us, length us, event | category | flops | bytes accessed | tf_op | source)
XLA Modules:
  0.0 62.5 jit_solution(15550225973224943369)
XLA Ops:
  0.6 1.1 %pack.1 = (bf16[560,256]{1,0:T(8,128)(2,1)S(1)}, bf16[544,256]{1,0:T(8,128)(2,1)S(1)}, bf16[16,256]{1,0:T(8,128)(2,1)S(1)}) custom-call(bf16[1024,256]{1,0:T(8,128)(2,1)} %bitcast.3, bf16[16,4,256]{2,1,0:T(4,128)(2,1)} %refs_1_.1, s32[2,64]{1,0:T(2,128)} %refs_2_.1, s32[1,64]{1,0:T(1,128)} %refs_3_.1, s32[4,64]{1,0:T(4,128)} %refs_4_.1, s32[2,64]{1,0:T(2,128)} %refs_5_.1), custom_call_target="tpu_custom_call" | custom-call | flops 1000000000 | tf_op jit(solution)/shard_map/pack/pallas_call | solution.py:120
  1.8 3.1 %collective-permute-start.2 = (bf16[16,256]{1,0:T(8,128)(2,1)S(1)}, bf16[16,256]{1,0:T(8,128)(2,1)S(1)}, u32[]{:S(2)}, u32[]{:S(2)}) collective-permute-start(bf16[16,256]{1,0:T(8,128)(2,1)S(1)} %get-tuple-element.71), channel_id=1, source_target_pairs={{0,2},{1,3},{2,0},{3,1},{4,6},{5,7},{6,4},{7,5},{8,10},{9,11},{10,... | collective-permute-start | bytes 24584 | tf_op jit(solution)/shard_map/ppermute | solution.py:590
  4.8 1.5 %collective-permute-start.1 = (bf16[544,256]{1,0:T(8,128)(2,1)S(1)}, bf16[544,256]{1,0:T(8,128)(2,1)S(1)}, u32[]{:S(2)}, u32[]{:S(2)}) collective-permute-start(bf16[544,256]{1,0:T(8,128)(2,1)S(1)} %get-tuple-element.80.refs_1_), channel_id=1, source_target_pairs={{0,16},{1,17},{2,18},{3,19},{4,20},{5,21},{6,22},{7,23},{8,24},{9,... | collective-permute-start | bytes 835592 | tf_op jit(solution)/shard_map/ppermute | solution.py:590
  6.4 1.5 %collective-permute-start = (bf16[560,256]{1,0:T(8,128)(2,1)S(1)}, bf16[560,256]{1,0:T(8,128)(2,1)S(1)}, u32[]{:S(2)}, u32[]{:S(2)}) collective-permute-start(bf16[560,256]{1,0:T(8,128)(2,1)S(1)} %get-tuple-element.103.refs_0_.refs_3_), channel_id=1, source_target_pairs={{0,1},{1,0},{2,3},{3,2},{4,5},{5,4},{6,7},{7,6},{8,9},{9,8},{10,11... | collective-permute-start | bytes 860168 | tf_op jit(solution)/shard_map/ppermute | solution.py:590
  7.9 0.0 collective-permute-done.2
  7.9 2.6 %collective-permute-start.3 = (bf16[16,512]{1,0:T(8,128)(2,1)S(1)}, bf16[16,512]{1,0:T(8,128)(2,1)S(1)}, u32[]{:S(2)}, u32[]{:S(2)}) collective-permute-start(bf16[16,512]{1,0:T(8,128)(2,1)S(1)} %pad_maximum_fusion), channel_id=1, source_target_pairs={{0,4},{1,5},{2,6},{3,7},{4,0},{5,1},{6,2},{7,3},{8,12},{9,13},{10,... | collective-permute-start | bytes 49160 | tf_op jit(solution)/shard_map/ppermute | solution.py:590
  10.5 0.6 collective-permute-start.7
  11.0 1.5 %collective-permute-start.8 = (bf16[560,256]{1,0:T(8,128)(2,1)S(1)}, bf16[560,256]{1,0:T(8,128)(2,1)S(1)}, u32[]{:S(2)}, u32[]{:S(2)}) collective-permute-start(bf16[560,256]{1,0:T(8,128)(2,1)S(1)} %get-tuple-element.103.refs_0_.refs_3_), channel_id=1, source_target_pairs={{0,16},{1,17},{2,18},{3,19},{4,20},{5,21},{6,22},{7,23},{8,24},{9,... | collective-permute-start | bytes 860168 | tf_op jit(solution)/shard_map/ppermute | solution.py:590
  12.5 0.0 collective-permute-done.3
  12.5 0.0 collective-permute-start.4
  12.5 1.2 %collective-permute-done.4.refs_3_ = bf16[16,1024]{1,0:T(8,128)(2,1)S(1)} collective-permute-done((bf16[16,1024]{1,0:T(8,128)(2,1)S(1)}, bf16[16,1024]{1,0:T(8,128)(2,1)S(1)}, u32[]{:S(2)}, u32[]{:S(2)}) %collective-permute-start.4) | collective-permute-done | bytes 32800 | tf_op jit(solution)/shard_map/ppermute | solution.py:590
  13.7 2.5 %first_product.1 = (bf16[512,64]{1,0:T(8,128)(2,1)S(1)}, bf16[512,64]{1,0:T(8,128)(2,1)S(1)}, bf16[512,64]{1,0:T(8,128)(2,1)S(1)}, bf16[512,64]{1,0:T(8,128)(2,1...) custom-call(bf16[560,256]{1,0:T(8,128)(2,1)S(1)} %get-tuple-element.10, ...), custom_call_target="tpu_custom_call" | custom-call | flops 1000000000 | tf_op jit(solution)/shard_map/first_product/pallas_call | solution.py:181
  16.3 0.0 collective-permute-done.1.refs_1_
  16.3 0.0 collective-permute-done.refs_0_.refs_1_
  16.3 0.6 collective-permute-start.5
  16.9 1.5 %collective-permute-start.6 = (bf16[544,256]{1,0:T(8,128)(2,1)S(1)}, bf16[544,256]{1,0:T(8,128)(2,1)S(1)}, u32[]{:S(2)}, u32[]{:S(2)}) collective-permute-start(bf16[544,256]{1,0:T(8,128)(2,1)S(1)} %collective-permute-done.1.refs_1_), channel_id=1, source_target_pairs={{0,1},{1,0},{2,3},{3,2},{4,5},{5,4},{6,7},{7,6},{8,9},{9,8},{10,11... | collective-permute-start | bytes 835592 | tf_op jit(solution)/shard_map/ppermute | solution.py:590
  18.4 2.5 %product.5 = (f32[512,256]{1,0:T(8,128)S(1)}, f32[512,256]{1,0:T(8,128)S(1)}, f32[512,256]{1,0:T(8,128)S(1)}, f32[512,256]{1,0:T(8,128)S(1)}) custom-call(bf16[560,256]{1,0:T(8,128)(2,1)S(1)} %collective-permute-done.refs_0_.refs_1_, bf16[544,256]{1,0:T(8,128)(2,1)S(1)} %collective-permute-done.1.refs_1_, bf16[512,64]{1,0:T(8,128)(2,1)S(1)} %get-tuple-element.79.refs_2_, ...), custom_call_target="tpu_custom_call" | custom-call | tf_op jit(solution)/shard_map/product/pallas_call | solution.py:209
  20.9 0.3 collective-permute-done.7.refs_0_
  21.2 0.0 collective-permute-done.8.refs_1_
  21.2 2.5 %product.6 = (f32[512,256]{1,0:T(8,128)S(1)}, f32[512,256]{1,0:T(8,128)S(1)}, f32[512,256]{1,0:T(8,128)S(1)}, f32[512,256]{1,0:T(8,128)S(1)}) custom-call(bf16[544,256]{1,0:T(8,128)(2,1)S(1)} %collective-permute-done.7.refs_0_, bf16[560,256]{1,0:T(8,128)(2,1)S(1)} %collective-permute-done.8.refs_1_, bf16[512,64]{1,0:T(8,128)(2,1)S(1)} %get-tuple-element.79.refs_2_, ...), custom_call_target="tpu_custom_call" | custom-call | flops 1000000000 | tf_op jit(solution)/shard_map/product/pallas_call | solution.py:209
  23.7 1.2 %skeletons.1 = (bf16[6,64,128]{2,1,0:T(8,128)(2,1)S(1)}, bf16[192,384]{1,0:T(8,128)(2,1)S(1)}, bf16[192,384]{1,0:T(8,128)(2,1)S(1)}, bf16[16,128]{1,0:T(8,128)(2,1)S(1)}) custom-call(bf16[560,256]{1,0:T(8,128)(2,1)S(1)} %get-tuple-element.103.refs_0_.refs_3_, bf16[560,256]{1,0:T(8,128)(2,1)S(1)} %collective-permute-done.refs_0_.refs_1_), custom_call_target="tpu_custom_call" | custom-call | flops 1000000000 | tf_op jit(solution)/shard_map/skeletons/pallas_call | solution.py:540
  24.9 1.4 %collective-permute-done.6.refs_1_ = bf16[544,256]{1,0:T(8,128)(2,1)S(1)} collective-permute-done((bf16[544,256]{1,0:T(8,128)(2,1)S(1)}, bf16[544,256]{1,0:T(8,128)(2,1)S(1)}, u32[]{:S(2)}, u32[]{:S(2)}) %collective-permute-start.6) | collective-permute-done | bytes 278560 | tf_op jit(solution)/shard_map/ppermute | solution.py:590
  26.3 0.0 collective-permute-done.5.refs_0_
  26.3 0.8 %product.9 = bf16[512,256]{1,0:T(8,128)(2,1)S(1)} custom-call(bf16[560,256]{1,0:T(8,128)(2,1)S(1)} %collective-permute-done.5.refs_0_, bf16[544,256]{1,0:T(8,128)(2,1)S(1)} %collective-permute-done.6.refs_1_, bf16[512,64]{1,0:T(8,128)(2,1)S(1)} %get-tuple-element.84.refs_5_.refs_2_, f32[512,256]{1,0:T(8,128)S(1)} %get-tuple-element.113.refs_3_), custom_call_target="tpu_custom_call" | custom-call | flops 1000000000 | tf_op jit(solution)/shard_map/product/pallas_call | solution.py:209
  27.1 0.1 collective-permute-start.9
  27.2 1.4 %product.8 = (f32[512,256]{1,0:T(8,128)S(1)}, f32[512,256]{1,0:T(8,128)S(1)}) custom-call(bf16[560,256]{1,0:T(8,128)(2,1)S(1)} %collective-permute-done.5.refs_0_, bf16[544,256]{1,0:T(8,128)(2,1)S(1)} %collective-permute-done.6.refs_1_, bf16[512,64]{1,0:T(8,128)(2,1)S(1)} %get-tuple-element.82.refs_3_.refs_2_, ...), custom_call_target="tpu_custom_call" | custom-call | flops 1000000000 | tf_op jit(solution)/shard_map/product/pallas_call | solution.py:209
  28.6 0.2 collective-permute-done.9.refs_1_
  28.8 0.4 collective-permute-start.10
  29.2 0.6 collective-permute-start.11
  29.8 0.8 %product.7.mine_ref = f32[512,256]{1,0:T(8,128)S(1)} custom-call(bf16[560,256]{1,0:T(8,128)(2,1)S(1)} %collective-permute-done.5.refs_0_, bf16[544,256]{1,0:T(8,128)(2,1)S(1)} %collective-permute-done.6.refs_1_, bf16[512,64]{1,0:T(8,128)(2,1)S(1)} %get-tuple-element.79.refs_2_, f32[512,256]{1,0:T(8,128)S(1)} %get-tuple-element.109.refs_3_), custom_call_target="tpu_custom_call" | custom-call | flops 1000000000 | tf_op jit(solution)/shard_map/product/pallas_call | solution.py:209
  30.6 0.1 collective-permute-done.10.theirs_ref
  30.8 0.1 near_up.1
  30.8 1.4 %collective-permute-start.13 = (bf16[272,256]{1,0:T(8,128)(2,1)S(1)}, bf16[272,256]{1,0:T(8,128)(2,1)S(1)}, u32[]{:S(2)}, u32[]{:S(2)}) collective-permute-start(bf16[272,256]{1,0:T(8,128)(2,1)S(1)} %get-tuple-element.122.refs_2_), channel_id=1, source_target_pairs={{0,2},{1,3},{2,0},{3,1},{4,6},{5,7},{6,4},{7,5},{8,10},{9,11},{10,... | collective-permute-start | bytes 417800 | tf_op jit(solution)/shard_map/ppermute | solution.py:590
  32.2 3.3 %collective-permute-done.11.refs_1_ = bf16[256,256]{1,0:T(8,128)(2,1)S(1)} collective-permute-done((bf16[256,256]{1,0:T(8,128)(2,1)S(1)}, bf16[256,256]{1,0:T(8,128)(2,1)S(1)}, u32[]{:S(2)}, u32[]{:S(2)}) %collective-permute-start.11) | collective-permute-done | bytes 131104 | tf_op jit(solution)/shard_map/ppermute | solution.py:590
  35.6 2.7 %collective-permute-start.12 = (bf16[256,256]{1,0:T(8,128)(2,1)S(1)}, bf16[256,256]{1,0:T(8,128)(2,1)S(1)}, u32[]{:S(2)}, u32[]{:S(2)}) collective-permute-start(bf16[256,256]{1,0:T(8,128)(2,1)S(1)} %add_up.3), channel_id=1, source_target_pairs={{0,4},{1,5},{2,6},{3,7},{4,0},{5,1},{6,2},{7,3},{8,12},{9,13},{10,... | collective-permute-start | bytes 393224 | tf_op jit(solution)/shard_map/ppermute | solution.py:590
  38.2 0.0 collective-permute-done.13.refs_1_.refs_2_
  38.2 0.8 %top_couplings.1 = (bf16[192,384]{1,0:T(8,128)(2,1)S(1)}, bf16[192,384]{1,0:T(8,128)(2,1)S(1)}) custom-call(bf16[16,128]{1,0:T(8,128)(2,1)S(1)} %get-tuple-element.118.points_ref.refs_0_, bf16[272,256]{1,0:T(8,128)(2,1)S(1)} %collective-permute-done.13.refs_1_.refs_2_, bf16[6,64,128]{2,1,0:T(8,128)(2,1)S(1)} %get-tuple-element.123.refs_2_.refs_4_.refs_5_), custom_call_target="tpu_custom_call" | custom-call | flops 10000000000 | tf_op jit(solution)/shard_map/top_couplings/pallas_call | solution.py:569
  39.0 4.7 %collective-permute-done.12.refs_1_ = bf16[256,256]{1,0:T(8,128)(2,1)S(1)} collective-permute-done((bf16[256,256]{1,0:T(8,128)(2,1)S(1)}, bf16[256,256]{1,0:T(8,128)(2,1)S(1)}, u32[]{:S(2)}, u32[]{:S(2)}) %collective-permute-start.12) | collective-permute-done | bytes 131104 | tf_op jit(solution)/shard_map/ppermute | solution.py:590
  43.8 5.6 %leaves.1 = (f32[2,64,128]{2,1,0:T(8,128)}, f32[64,128]{1,0:T(8,128)S(1)}, f32[64,256]{1,0:T(8,128)S(1)}, f32[64,256]{1,0:T(8,128)S(1)}, bf16[192,256]{1,0:T(8,128)(2,1)S(1)}) custom-call(f32[256,256]{1,0:T(8,128)S(1)} %get-tuple-element.119.refs_0_, bf16[256,256]{1,0:T(8,128)(2,1)S(1)} %collective-permute-done.12.refs_1_, ...), custom_call_target="tpu_custom_call" | custom-call | flops 1000000000 | tf_op jit(solution)/shard_map/leaves/pallas_call | solution.py:387
  49.4 1.6 %collective-permute-start.16 = (bf16[192,256]{1,0:T(8,128)(2,1)S(1)}, bf16[192,256]{1,0:T(8,128)(2,1)S(1)}, u32[]{:S(2)}, u32[]{:S(2)}) collective-permute-start(bf16[192,256]{1,0:T(8,128)(2,1)S(1)} %get-tuple-element.130), channel_id=1, source_target_pairs={{0,1},{1,0},{2,3},{3,2},{4,5},{5,4},{6,7},{7,6},{8,9},{9,8},{10,11... | collective-permute-start | bytes 294920 | tf_op jit(solution)/shard_map/ppermute | solution.py:590
  50.9 0.0 collective-permute-start.15
  50.9 2.0 %collective-permute-start.14 = (bf16[192,256]{1,0:T(8,128)(2,1)S(1)}, bf16[192,256]{1,0:T(8,128)(2,1)S(1)}, u32[]{:S(2)}, u32[]{:S(2)}) collective-permute-start(bf16[192,256]{1,0:T(8,128)(2,1)S(1)} %get-tuple-element.130), channel_id=1, source_target_pairs={{0,3},{1,2},{2,1},{3,0},{4,7},{5,6},{6,5},{7,4},{8,11},{9,10},{10,... | collective-permute-start | bytes 294920 | tf_op jit(solution)/shard_map/ppermute | solution.py:590
  52.9 1.8 %collective-permute-done.16.refs_4_ = bf16[192,256]{1,0:T(8,128)(2,1)S(1)} collective-permute-done((bf16[192,256]{1,0:T(8,128)(2,1)S(1)}, bf16[192,256]{1,0:T(8,128)(2,1)S(1)}, u32[]{:S(2)}, u32[]{:S(2)}) %collective-permute-start.16) | collective-permute-done | bytes 98336 | tf_op jit(solution)/shard_map/ppermute | solution.py:590
  54.7 0.8 %collective-permute-done.15.refs_3_ = bf16[192,256]{1,0:T(8,128)(2,1)S(1)} collective-permute-done((bf16[192,256]{1,0:T(8,128)(2,1)S(1)}, bf16[192,256]{1,0:T(8,128)(2,1)S(1)}, u32[]{:S(2)}, u32[]{:S(2)}) %collective-permute-start.15) | collective-permute-done | bytes 98336 | tf_op jit(solution)/shard_map/ppermute | solution.py:590
  55.6 1.0 %collective-permute-done.14.refs_2_ = bf16[192,256]{1,0:T(8,128)(2,1)S(1)} collective-permute-done((bf16[192,256]{1,0:T(8,128)(2,1)S(1)}, bf16[192,256]{1,0:T(8,128)(2,1)S(1)}, u32[]{:S(2)}, u32[]{:S(2)}) %collective-permute-start.14) | collective-permute-done | bytes 98336 | tf_op jit(solution)/shard_map/ppermute | solution.py:590
  56.6 5.8 %upper_levels.1 = (f32[3,1,64,128]{3,2,1,0:T(8,128)}, f32[2,1,64,256]{3,2,1,0:T(8,128)}) custom-call(f32[64,256]{1,0:T(8,128)S(1)} %get-tuple-element.128.refs_0_, f32[64,256]{1,0:T(8,128)S(1)} %get-tuple-element.129.refs_1_, bf16[192,256]{1,0:T(8,128)(2,1)S(1)} %collective-permute-done.14.refs_2_, bf16[192,256]{1,0:T(8,128)(2,1)S(1)} %collective-permute-done.15.refs_3_, ...), custom_call_target="tpu_custom_call" | custom-call | flops 1000000000 | tf_op jit(solution)/shard_map/upper_levels/pallas_call | solution.py:463
  (5 shorter events, 0.1 us)
Async XLA Ops:
  1.8 6.1 %collective-permute-start.2 = (bf16[16,256]{1,0:T(8,128)(2,1)S(1)}, bf16[16,256]{1,0:T(8,128)(2,1)S(1)}, u32[]{:S(2)}, u32[]{:S(2)}) collective-permute-start(bf16[16,256]{1,0:T(8,128)(2,1)S(1)} %get-tuple-element.71), channel_id=1, source_target_pairs={{0,2},{1,3},{2,0},{3,1},{4,6},{5,7},{6,4},{7,5},{8,10},{9,11},{10,... | collective-permute-start | bytes 24584 | tf_op jit(solution)/shard_map/ppermute | solution.py:590
  4.8 11.4 %collective-permute-start.1 = (bf16[544,256]{1,0:T(8,128)(2,1)S(1)}, bf16[544,256]{1,0:T(8,128)(2,1)S(1)}, u32[]{:S(2)}, u32[]{:S(2)}) collective-permute-start(bf16[544,256]{1,0:T(8,128)(2,1)S(1)} %get-tuple-element.80.refs_1_), channel_id=1, source_target_pairs={{0,16},{1,17},{2,18},{3,19},{4,20},{5,21},{6,22},{7,23},{8,24},{9,... | collective-permute-start | bytes 835592 | tf_op jit(solution)/shard_map/ppermute | solution.py:590
  6.4 9.9 %collective-permute-start = (bf16[560,256]{1,0:T(8,128)(2,1)S(1)}, bf16[560,256]{1,0:T(8,128)(2,1)S(1)}, u32[]{:S(2)}, u32[]{:S(2)}) collective-permute-start(bf16[560,256]{1,0:T(8,128)(2,1)S(1)} %get-tuple-element.103.refs_0_.refs_3_), channel_id=1, source_target_pairs={{0,1},{1,0},{2,3},{3,2},{4,5},{5,4},{6,7},{7,6},{8,9},{9,8},{10,11... | collective-permute-start | bytes 860168 | tf_op jit(solution)/shard_map/ppermute | solution.py:590
  7.9 4.7 %collective-permute-start.3 = (bf16[16,512]{1,0:T(8,128)(2,1)S(1)}, bf16[16,512]{1,0:T(8,128)(2,1)S(1)}, u32[]{:S(2)}, u32[]{:S(2)}) collective-permute-start(bf16[16,512]{1,0:T(8,128)(2,1)S(1)} %pad_maximum_fusion), channel_id=1, source_target_pairs={{0,4},{1,5},{2,6},{3,7},{4,0},{5,1},{6,2},{7,3},{8,12},{9,13},{10,... | collective-permute-start | bytes 49160 | tf_op jit(solution)/shard_map/ppermute | solution.py:590
  10.5 10.8 %collective-permute-start.7 = (bf16[544,256]{1,0:T(8,128)(2,1)S(1)}, bf16[544,256]{1,0:T(8,128)(2,1)S(1)}, u32[]{:S(2)}, u32[]{:S(2)}) collective-permute-start(bf16[544,256]{1,0:T(8,128)(2,1)S(1)} %get-tuple-element.80.refs_1_), channel_id=1, source_target_pairs={{0,1},{1,0},{2,3},{3,2},{4,5},{5,4},{6,7},{7,6},{8,9},{9,8},{10,11... | collective-permute-start | bytes 835592 | tf_op jit(solution)/shard_map/ppermute | solution.py:590
  11.0 10.2 %collective-permute-start.8 = (bf16[560,256]{1,0:T(8,128)(2,1)S(1)}, bf16[560,256]{1,0:T(8,128)(2,1)S(1)}, u32[]{:S(2)}, u32[]{:S(2)}) collective-permute-start(bf16[560,256]{1,0:T(8,128)(2,1)S(1)} %get-tuple-element.103.refs_0_.refs_3_), channel_id=1, source_target_pairs={{0,16},{1,17},{2,18},{3,19},{4,20},{5,21},{6,22},{7,23},{8,24},{9,... | collective-permute-start | bytes 860168 | tf_op jit(solution)/shard_map/ppermute | solution.py:590
  12.5 1.2 %collective-permute-start.4 = (bf16[16,1024]{1,0:T(8,128)(2,1)S(1)}, bf16[16,1024]{1,0:T(8,128)(2,1)S(1)}, u32[]{:S(2)}, u32[]{:S(2)}) collective-permute-start(bf16[16,1024]{1,0:T(8,128)(2,1)S(1)} %constant_dynamic-update-slice_fusion.refs_2_), channel_id=1, source_target_pairs={{0,8},{1,9},{2,10},{3,11},{4,12},{5,13},{6,14},{7,15},{8,0},{9,1},... | collective-permute-start | bytes 98312 | tf_op jit(solution)/shard_map/ppermute | solution.py:590
  16.3 10.0 %collective-permute-start.5 = (bf16[560,256]{1,0:T(8,128)(2,1)S(1)}, bf16[560,256]{1,0:T(8,128)(2,1)S(1)}, u32[]{:S(2)}, u32[]{:S(2)}) collective-permute-start(bf16[560,256]{1,0:T(8,128)(2,1)S(1)} %collective-permute-done.refs_0_.refs_1_), channel_id=1, source_target_pairs={{0,16},{1,17},{2,18},{3,19},{4,20},{5,21},{6,22},{7,23},{8,24},{9,... | collective-permute-start | bytes 860168 | tf_op jit(solution)/shard_map/ppermute | solution.py:590
  16.9 9.4 %collective-permute-start.6 = (bf16[544,256]{1,0:T(8,128)(2,1)S(1)}, bf16[544,256]{1,0:T(8,128)(2,1)S(1)}, u32[]{:S(2)}, u32[]{:S(2)}) collective-permute-start(bf16[544,256]{1,0:T(8,128)(2,1)S(1)} %collective-permute-done.1.refs_1_), channel_id=1, source_target_pairs={{0,1},{1,0},{2,3},{3,2},{4,5},{5,4},{6,7},{7,6},{8,9},{9,8},{10,11... | collective-permute-start | bytes 835592 | tf_op jit(solution)/shard_map/ppermute | solution.py:590
  27.1 1.6 %collective-permute-start.9 = (bf16[512,256]{1,0:T(8,128)(2,1)S(1)}, bf16[512,256]{1,0:T(8,128)(2,1)S(1)}, u32[]{:S(2)}, u32[]{:S(2)}) collective-permute-start(bf16[512,256]{1,0:T(8,128)(2,1)S(1)} %product.9), channel_id=1, source_target_pairs={{0,8},{1,9},{2,10},{3,11},{4,12},{5,13},{6,14},{7,15},{8,0},{9,1},... | collective-permute-start | bytes 786440 | tf_op jit(solution)/shard_map/ppermute | solution.py:590
  28.8 2.0 %collective-permute-start.10 = (f32[512,256]{1,0:T(8,128)S(1)}, f32[512,256]{1,0:T(8,128)S(1)}, u32[]{:S(2)}, u32[]{:S(2)}) collective-permute-start(f32[512,256]{1,0:T(8,128)S(1)} %get-tuple-element.117), channel_id=1, source_target_pairs={{0,8},{1,9},{2,10},{3,11},{4,12},{5,13},{6,14},{7,15},{8,0},{9,1},... | collective-permute-start | bytes 1572872 | tf_op jit(solution)/shard_map/ppermute | solution.py:590
  29.2 6.3 %collective-permute-start.11 = (bf16[256,256]{1,0:T(8,128)(2,1)S(1)}, bf16[256,256]{1,0:T(8,128)(2,1)S(1)}, u32[]{:S(2)}, u32[]{:S(2)}) collective-permute-start(bf16[256,256]{1,0:T(8,128)(2,1)S(1)} %get-tuple-element.121), channel_id=1, source_target_pairs={{0,2},{1,3},{2,0},{3,1},{4,6},{5,7},{6,4},{7,5},{8,10},{9,11},{10,... | collective-permute-start | bytes 393224 | tf_op jit(solution)/shard_map/ppermute | solution.py:590
  30.8 7.4 %collective-permute-start.13 = (bf16[272,256]{1,0:T(8,128)(2,1)S(1)}, bf16[272,256]{1,0:T(8,128)(2,1)S(1)}, u32[]{:S(2)}, u32[]{:S(2)}) collective-permute-start(bf16[272,256]{1,0:T(8,128)(2,1)S(1)} %get-tuple-element.122.refs_2_), channel_id=1, source_target_pairs={{0,2},{1,3},{2,0},{3,1},{4,6},{5,7},{6,4},{7,5},{8,10},{9,11},{10,... | collective-permute-start | bytes 417800 | tf_op jit(solution)/shard_map/ppermute | solution.py:590
  35.6 8.2 %collective-permute-start.12 = (bf16[256,256]{1,0:T(8,128)(2,1)S(1)}, bf16[256,256]{1,0:T(8,128)(2,1)S(1)}, u32[]{:S(2)}, u32[]{:S(2)}) collective-permute-start(bf16[256,256]{1,0:T(8,128)(2,1)S(1)} %add_up.3), channel_id=1, source_target_pairs={{0,4},{1,5},{2,6},{3,7},{4,0},{5,1},{6,2},{7,3},{8,12},{9,13},{10,... | collective-permute-start | bytes 393224 | tf_op jit(solution)/shard_map/ppermute | solution.py:590
  49.4 5.3 %collective-permute-start.16 = (bf16[192,256]{1,0:T(8,128)(2,1)S(1)}, bf16[192,256]{1,0:T(8,128)(2,1)S(1)}, u32[]{:S(2)}, u32[]{:S(2)}) collective-permute-start(bf16[192,256]{1,0:T(8,128)(2,1)S(1)} %get-tuple-element.130), channel_id=1, source_target_pairs={{0,1},{1,0},{2,3},{3,2},{4,5},{5,4},{6,7},{7,6},{8,9},{9,8},{10,11... | collective-permute-start | bytes 294920 | tf_op jit(solution)/shard_map/ppermute | solution.py:590
  50.9 4.6 %collective-permute-start.15 = (bf16[192,256]{1,0:T(8,128)(2,1)S(1)}, bf16[192,256]{1,0:T(8,128)(2,1)S(1)}, u32[]{:S(2)}, u32[]{:S(2)}) collective-permute-start(bf16[192,256]{1,0:T(8,128)(2,1)S(1)} %get-tuple-element.130), channel_id=1, source_target_pairs={{0,2},{1,3},{2,0},{3,1},{4,6},{5,7},{6,4},{7,5},{8,10},{9,11},{10,... | collective-permute-start | bytes 294920 | tf_op jit(solution)/shard_map/ppermute | solution.py:590
  50.9 5.6 %collective-permute-start.14 = (bf16[192,256]{1,0:T(8,128)(2,1)S(1)}, bf16[192,256]{1,0:T(8,128)(2,1)S(1)}, u32[]{:S(2)}, u32[]{:S(2)}) collective-permute-start(bf16[192,256]{1,0:T(8,128)(2,1)S(1)} %get-tuple-element.130), channel_id=1, source_target_pairs={{0,3},{1,2},{2,1},{3,0},{4,7},{5,6},{6,5},{7,4},{8,11},{9,10},{10,... | collective-permute-start | bytes 294920 | tf_op jit(solution)/shard_map/ppermute | solution.py:590

commit v7 on v5

--- a/solution.py
+++ b/solution.py
@@ -297,8 +297,13 @@
         products = wide_product(skeleton, jnp.concatenate([stack, skeleton, skeleton], axis=0))
         ridge = 0.05 * jnp.sum(skeleton * skeleton, keepdims=True) / rank + 1e-05
         inverse = 1.0 / (640.0 * ridge)
-        states.append((products[:, :pool], eyes - products[:, pool:] * inverse, inverse))
-    for number, tau in enumerate(TAUS):
+        cross, gram = products[:, :pool], products[:, pool:]
+        parts = [jnp.concatenate(pair, axis=1) for pair in zip(split(cross), split(gram))]
+        both = twice_product(gram, split(gram), parts)
+        solved = cross + (cross - both[:, :pool] * inverse) * (1.0 / TAUS[0])
+        power = eyes + (both[:, pool:] * inverse - 2.0 * gram) * (2.0 * inverse)
+        states.append((solved, power, inverse))
+    for number, tau in enumerate(TAUS[1:], 1):
         last = number == DOUBLINGS - 1
         later = []
         for solved, power, inverse in states:

time: 62.1 us -> 63.1 us (1.016)
  Pallas kernels: 24.9 us -> 25.9 us
where the time goes in v7:
time: 63.1 us; the launch traced here: 62.9 us
  Pallas kernels  25.9 us (41%)
  starting transfers between devices  22.3 us (35%)
  waiting for transfers between devices  13.8 us (22%)
  between operations  0.91 us (1%)
    ppermute x18, starting transfers between devices, swap(): return lax.ppermute(value, ('row', 'col'), pairs)  22.3 us
    ppermute x18, waiting for transfers between devices, swap(): return lax.ppermute(value, ('row', 'col'), pairs)  13.8 us
    pallas_call x5, Pallas kernels, product(): pl.pallas_call(lambda *refs: product_body(span, len(halves), len(rows), *...  7.98 us
    pallas_call x1, Pallas kernels, upper_levels(): pl.pallas_call(lambda *refs: upper_body(picks.shape[0], *refs), out_shape...  6.22 us
    pallas_call x1, Pallas kernels, leaves(): pl.pallas_call(lambda *refs: leaves_body(len(others), *refs), out_shape=(...  5.96 us
    pallas_call x1, Pallas kernels, first_product(): pl.pallas_call(lambda *refs: first_product_body(gain, span, groups, len(p...  2.53 us
  transfers between devices with their start and end apart: 18, of which 9 were waited for; matrix products, arithmetic and copies ran while one was open for 0% of the time, Pallas kernels for 19%

profile of v7, /device:TPU:0, one launch (start us, length us, event | category | flops | bytes accessed | tf_op | source)
XLA Modules:
  0.0 62.9 jit_solution(8664526467988380704)
XLA Ops:
  0.6 1.1 %pack.1 = (bf16[560,256]{1,0:T(8,128)(2,1)S(1)}, bf16[544,256]{1,0:T(8,128)(2,1)S(1)}, bf16[16,256]{1,0:T(8,128)(2,1)S(1)}) custom-call(bf16[1024,256]{1,0:T(8,128)(2,1)} %bitcast.3, bf16[16,4,256]{2,1,0:T(4,128)(2,1)} %refs_1_.1, s32[2,64]{1,0:T(2,128)} %refs_2_.1, s32[1,64]{1,0:T(1,128)} %refs_3_.1, s32[4,64]{1,0:T(4,128)} %refs_4_.1, s32[2,64]{1,0:T(2,128)} %refs_5_.1), custom_call_target="tpu_custom_call" | custom-call | flops 1000000000 | tf_op jit(solution)/shard_map/pack/pallas_call | solution.py:120
  1.8 3.1 %collective-permute-start.2 = (bf16[16,256]{1,0:T(8,128)(2,1)S(1)}, bf16[16,256]{1,0:T(8,128)(2,1)S(1)}, u32[]{:S(2)}, u32[]{:S(2)}) collective-permute-start(bf16[16,256]{1,0:T(8,128)(2,1)S(1)} %get-tuple-element.71), channel_id=1, source_target_pairs={{0,2},{1,3},{2,0},{3,1},{4,6},{5,7},{6,4},{7,5},{8,10},{9,11},{10,... | collective-permute-start | bytes 24584 | tf_op jit(solution)/shard_map/ppermute | solution.py:572
  4.8 1.5 %collective-permute-start.1 = (bf16[544,256]{1,0:T(8,128)(2,1)S(1)}, bf16[544,256]{1,0:T(8,128)(2,1)S(1)}, u32[]{:S(2)}, u32[]{:S(2)}) collective-permute-start(bf16[544,256]{1,0:T(8,128)(2,1)S(1)} %get-tuple-element.80.refs_1_), channel_id=1, source_target_pairs={{0,16},{1,17},{2,18},{3,19},{4,20},{5,21},{6,22},{7,23},{8,24},{9,... | collective-permute-start | bytes 835592 | tf_op jit(solution)/shard_map/ppermute | solution.py:572
  6.4 1.5 %collective-permute-start = (bf16[560,256]{1,0:T(8,128)(2,1)S(1)}, bf16[560,256]{1,0:T(8,128)(2,1)S(1)}, u32[]{:S(2)}, u32[]{:S(2)}) collective-permute-start(bf16[560,256]{1,0:T(8,128)(2,1)S(1)} %get-tuple-element.103.refs_0_.refs_3_), channel_id=1, source_target_pairs={{0,1},{1,0},{2,3},{3,2},{4,5},{5,4},{6,7},{7,6},{8,9},{9,8},{10,11... | collective-permute-start | bytes 860168 | tf_op jit(solution)/shard_map/ppermute | solution.py:572
  7.9 0.0 collective-permute-done.2
  7.9 2.6 %collective-permute-start.3 = (bf16[16,512]{1,0:T(8,128)(2,1)S(1)}, bf16[16,512]{1,0:T(8,128)(2,1)S(1)}, u32[]{:S(2)}, u32[]{:S(2)}) collective-permute-start(bf16[16,512]{1,0:T(8,128)(2,1)S(1)} %pad_maximum_fusion), channel_id=1, source_target_pairs={{0,4},{1,5},{2,6},{3,7},{4,0},{5,1},{6,2},{7,3},{8,12},{9,13},{10,... | collective-permute-start | bytes 49160 | tf_op jit(solution)/shard_map/ppermute | solution.py:572
  10.5 0.6 collective-permute-start.7
  11.0 1.5 %collective-permute-start.8 = (bf16[560,256]{1,0:T(8,128)(2,1)S(1)}, bf16[560,256]{1,0:T(8,128)(2,1)S(1)}, u32[]{:S(2)}, u32[]{:S(2)}) collective-permute-start(bf16[560,256]{1,0:T(8,128)(2,1)S(1)} %get-tuple-element.103.refs_0_.refs_3_), channel_id=1, source_target_pairs={{0,16},{1,17},{2,18},{3,19},{4,20},{5,21},{6,22},{7,23},{8,24},{9,... | collective-permute-start | bytes 860168 | tf_op jit(solution)/shard_map/ppermute | solution.py:572
  12.5 0.0 collective-permute-done.3
  12.5 0.0 collective-permute-start.4
  12.5 1.2 %collective-permute-done.4.refs_3_ = bf16[16,1024]{1,0:T(8,128)(2,1)S(1)} collective-permute-done((bf16[16,1024]{1,0:T(8,128)(2,1)S(1)}, bf16[16,1024]{1,0:T(8,128)(2,1)S(1)}, u32[]{:S(2)}, u32[]{:S(2)}) %collective-permute-start.4) | collective-permute-done | bytes 32800 | tf_op jit(solution)/shard_map/ppermute | solution.py:572
  13.7 2.5 %first_product.1 = (bf16[512,64]{1,0:T(8,128)(2,1)S(1)}, bf16[512,64]{1,0:T(8,128)(2,1)S(1)}, bf16[512,64]{1,0:T(8,128)(2,1)S(1)}, bf16[512,64]{1,0:T(8,128)(2,1...) custom-call(bf16[560,256]{1,0:T(8,128)(2,1)S(1)} %get-tuple-element.10, ...), custom_call_target="tpu_custom_call" | custom-call | flops 1000000000 | tf_op jit(solution)/shard_map/first_product/pallas_call | solution.py:181
  16.3 0.0 collective-permute-done.1.refs_1_
  16.3 0.0 collective-permute-done.refs_0_.refs_1_
  16.3 0.6 collective-permute-start.5
  16.9 1.5 %collective-permute-start.6 = (bf16[544,256]{1,0:T(8,128)(2,1)S(1)}, bf16[544,256]{1,0:T(8,128)(2,1)S(1)}, u32[]{:S(2)}, u32[]{:S(2)}) collective-permute-start(bf16[544,256]{1,0:T(8,128)(2,1)S(1)} %collective-permute-done.1.refs_1_), channel_id=1, source_target_pairs={{0,1},{1,0},{2,3},{3,2},{4,5},{5,4},{6,7},{7,6},{8,9},{9,8},{10,11... | collective-permute-start | bytes 835592 | tf_op jit(solution)/shard_map/ppermute | solution.py:572
  18.4 2.5 %product.5 = (f32[512,256]{1,0:T(8,128)S(1)}, f32[512,256]{1,0:T(8,128)S(1)}, f32[512,256]{1,0:T(8,128)S(1)}, f32[512,256]{1,0:T(8,128)S(1)}) custom-call(bf16[560,256]{1,0:T(8,128)(2,1)S(1)} %collective-permute-done.refs_0_.refs_1_, bf16[544,256]{1,0:T(8,128)(2,1)S(1)} %collective-permute-done.1.refs_1_, bf16[512,64]{1,0:T(8,128)(2,1)S(1)} %get-tuple-element.79.refs_2_, ...), custom_call_target="tpu_custom_call" | custom-call | tf_op jit(solution)/shard_map/product/pallas_call | solution.py:209
  20.9 0.3 collective-permute-done.7.refs_0_
  21.2 0.0 collective-permute-done.8.refs_1_
  21.2 2.5 %product.6 = (f32[512,256]{1,0:T(8,128)S(1)}, f32[512,256]{1,0:T(8,128)S(1)}, f32[512,256]{1,0:T(8,128)S(1)}, f32[512,256]{1,0:T(8,128)S(1)}) custom-call(bf16[544,256]{1,0:T(8,128)(2,1)S(1)} %collective-permute-done.7.refs_0_, bf16[560,256]{1,0:T(8,128)(2,1)S(1)} %collective-permute-done.8.refs_1_, bf16[512,64]{1,0:T(8,128)(2,1)S(1)} %get-tuple-element.79.refs_2_, ...), custom_call_target="tpu_custom_call" | custom-call | flops 1000000000 | tf_op jit(solution)/shard_map/product/pallas_call | solution.py:209
  23.7 1.2 %skeletons.1 = (bf16[6,64,128]{2,1,0:T(8,128)(2,1)S(1)}, bf16[192,384]{1,0:T(8,128)(2,1)S(1)}, bf16[192,384]{1,0:T(8,128)(2,1)S(1)}, bf16[16,128]{1,0:T(8,128)(2,1)S(1)}) custom-call(bf16[560,256]{1,0:T(8,128)(2,1)S(1)} %get-tuple-element.103.refs_0_.refs_3_, bf16[560,256]{1,0:T(8,128)(2,1)S(1)} %collective-permute-done.refs_0_.refs_1_), custom_call_target="tpu_custom_call" | custom-call | flops 1000000000 | tf_op jit(solution)/shard_map/skeletons/pallas_call | solution.py:524
  24.9 1.4 %collective-permute-done.6.refs_1_ = bf16[544,256]{1,0:T(8,128)(2,1)S(1)} collective-permute-done((bf16[544,256]{1,0:T(8,128)(2,1)S(1)}, bf16[544,256]{1,0:T(8,128)(2,1)S(1)}, u32[]{:S(2)}, u32[]{:S(2)}) %collective-permute-start.6) | collective-permute-done | bytes 278560 | tf_op jit(solution)/shard_map/ppermute | solution.py:572
  26.3 0.0 collective-permute-done.5.refs_0_
  26.3 0.8 %product.9 = bf16[512,256]{1,0:T(8,128)(2,1)S(1)} custom-call(bf16[560,256]{1,0:T(8,128)(2,1)S(1)} %collective-permute-done.5.refs_0_, bf16[544,256]{1,0:T(8,128)(2,1)S(1)} %collective-permute-done.6.refs_1_, bf16[512,64]{1,0:T(8,128)(2,1)S(1)} %get-tuple-element.84.refs_5_.refs_2_, f32[512,256]{1,0:T(8,128)S(1)} %get-tuple-element.113.refs_3_), custom_call_target="tpu_custom_call" | custom-call | flops 1000000000 | tf_op jit(solution)/shard_map/product/pallas_call | solution.py:209
  27.1 0.1 collective-permute-start.9
  27.2 1.4 %product.8 = (f32[512,256]{1,0:T(8,128)S(1)}, f32[512,256]{1,0:T(8,128)S(1)}) custom-call(bf16[560,256]{1,0:T(8,128)(2,1)S(1)} %collective-permute-done.5.refs_0_, bf16[544,256]{1,0:T(8,128)(2,1)S(1)} %collective-permute-done.6.refs_1_, bf16[512,64]{1,0:T(8,128)(2,1)S(1)} %get-tuple-element.82.refs_3_.refs_2_, ...), custom_call_target="tpu_custom_call" | custom-call | flops 1000000000 | tf_op jit(solution)/shard_map/product/pallas_call | solution.py:209
  28.6 0.2 collective-permute-done.9.refs_1_
  28.8 0.4 collective-permute-start.10
  29.2 0.6 collective-permute-start.11
  29.8 0.8 %product.7.refs_0_ = f32[512,256]{1,0:T(8,128)S(1)} custom-call(bf16[560,256]{1,0:T(8,128)(2,1)S(1)} %collective-permute-done.5.refs_0_, bf16[544,256]{1,0:T(8,128)(2,1)S(1)} %collective-permute-done.6.refs_1_, bf16[512,64]{1,0:T(8,128)(2,1)S(1)} %get-tuple-element.79.refs_2_, f32[512,256]{1,0:T(8,128)S(1)} %get-tuple-element.109.refs_3_), custom_call_target="tpu_custom_call" | custom-call | flops 1000000000 | tf_op jit(solution)/shard_map/product/pallas_call | solution.py:209
  30.6 1.5 %collective-permute-start.14 = (bf16[16,128]{1,0:T(8,128)(2,1)S(1)}, bf16[16,128]{1,0:T(8,128)(2,1)S(1)}, u32[]{:S(2)}, u32[]{:S(2)}) collective-permute-start(bf16[16,128]{1,0:T(8,128)(2,1)S(1)} %get-tuple-element.124.refs_0_), channel_id=1, source_target_pairs={{0,2},{1,3},{2,0},{3,1},{4,6},{5,7},{6,4},{7,5},{8,10},{9,11},{10,... | collective-permute-start | bytes 12296 | tf_op jit(solution)/shard_map/ppermute | solution.py:572
  32.1 0.0 collective-permute-done.10.refs_1_
  32.1 0.1 add_up.4
  32.2 0.7 %collective-permute-start.13 = (bf16[256,256]{1,0:T(8,128)(2,1)S(1)}, bf16[256,256]{1,0:T(8,128)(2,1)S(1)}, u32[]{:S(2)}, u32[]{:S(2)}) collective-permute-start(bf16[256,256]{1,0:T(8,128)(2,1)S(1)} %get-tuple-element.121.refs_2_), channel_id=1, source_target_pairs={{0,2},{1,3},{2,0},{3,1},{4,6},{5,7},{6,4},{7,5},{8,10},{9,11},{10,... | collective-permute-start | bytes 393224 | tf_op jit(solution)/shard_map/ppermute | solution.py:572
  32.9 2.2 %collective-permute-done.11.refs_1_ = bf16[256,256]{1,0:T(8,128)(2,1)S(1)} collective-permute-done((bf16[256,256]{1,0:T(8,128)(2,1)S(1)}, bf16[256,256]{1,0:T(8,128)(2,1)S(1)}, u32[]{:S(2)}, u32[]{:S(2)}) %collective-permute-start.11) | collective-permute-done | bytes 131104 | tf_op jit(solution)/shard_map/ppermute | solution.py:572
  35.1 2.7 %collective-permute-start.12 = (bf16[256,256]{1,0:T(8,128)(2,1)S(1)}, bf16[256,256]{1,0:T(8,128)(2,1)S(1)}, u32[]{:S(2)}, u32[]{:S(2)}) collective-permute-start(bf16[256,256]{1,0:T(8,128)(2,1)S(1)} %add_up.5), channel_id=1, source_target_pairs={{0,4},{1,5},{2,6},{3,7},{4,0},{5,1},{6,2},{7,3},{8,12},{9,13},{10,... | collective-permute-start | bytes 393224 | tf_op jit(solution)/shard_map/ppermute | solution.py:572
  37.8 0.0 collective-permute-done.14.refs_1_
  37.8 0.8 %top_couplings.1 = (bf16[192,384]{1,0:T(8,128)(2,1)S(1)}, bf16[192,384]{1,0:T(8,128)(2,1)S(1)}) custom-call(bf16[16,128]{1,0:T(8,128)(2,1)S(1)} %get-tuple-element.124.refs_0_, bf16[16,128]{1,0:T(8,128)(2,1)S(1)} %collective-permute-done.14.refs_1_, bf16[6,64,128]{2,1,0:T(8,128)(2,1)S(1)} %get-tuple-element.122.refs_2_.refs_4_.refs_5_), custom_call_target="tpu_custom_call" | custom-call | flops 10000000000 | tf_op jit(solution)/shard_map/top_couplings/pallas_call | solution.py:551
  38.6 4.8 %collective-permute-done.12.refs_1_ = bf16[256,256]{1,0:T(8,128)(2,1)S(1)} collective-permute-done((bf16[256,256]{1,0:T(8,128)(2,1)S(1)}, bf16[256,256]{1,0:T(8,128)(2,1)S(1)}, u32[]{:S(2)}, u32[]{:S(2)}) %collective-permute-start.12) | collective-permute-done | bytes 131104 | tf_op jit(solution)/shard_map/ppermute | solution.py:572
  43.4 0.0 collective-permute-done.13.refs_2_
  43.4 6.0 %leaves.1 = (f32[2,64,128]{2,1,0:T(8,128)}, f32[64,128]{1,0:T(8,128)S(1)}, f32[64,256]{1,0:T(8,128)S(1)}, f32[64,256]{1,0:T(8,128)S(1)}, bf16[192,256]{1,0:T(8,128)(2,1)S(1)}) custom-call(f32[256,256]{1,0:T(8,128)S(1)} %get-tuple-element.118.refs_0_, bf16[256,256]{1,0:T(8,128)(2,1)S(1)} %collective-permute-done.12.refs_1_, ...), custom_call_target="tpu_custom_call" | custom-call | flops 1000000000 | tf_op jit(solution)/shard_map/leaves/pallas_call | solution.py:371
  49.3 1.6 %collective-permute-start.17 = (bf16[192,256]{1,0:T(8,128)(2,1)S(1)}, bf16[192,256]{1,0:T(8,128)(2,1)S(1)}, u32[]{:S(2)}, u32[]{:S(2)}) collective-permute-start(bf16[192,256]{1,0:T(8,128)(2,1)S(1)} %get-tuple-element.130), channel_id=1, source_target_pairs={{0,1},{1,0},{2,3},{3,2},{4,5},{5,4},{6,7},{7,6},{8,9},{9,8},{10,11... | collective-permute-start | bytes 294920 | tf_op jit(solution)/shard_map/ppermute | solution.py:572
  50.9 0.0 collective-permute-start.16
  50.9 2.0 %collective-permute-start.15 = (bf16[192,256]{1,0:T(8,128)(2,1)S(1)}, bf16[192,256]{1,0:T(8,128)(2,1)S(1)}, u32[]{:S(2)}, u32[]{:S(2)}) collective-permute-start(bf16[192,256]{1,0:T(8,128)(2,1)S(1)} %get-tuple-element.130), channel_id=1, source_target_pairs={{0,3},{1,2},{2,1},{3,0},{4,7},{5,6},{6,5},{7,4},{8,11},{9,10},{10,... | collective-permute-start | bytes 294920 | tf_op jit(solution)/shard_map/ppermute | solution.py:572
  52.9 1.9 %collective-permute-done.17.refs_4_ = bf16[192,256]{1,0:T(8,128)(2,1)S(1)} collective-permute-done((bf16[192,256]{1,0:T(8,128)(2,1)S(1)}, bf16[192,256]{1,0:T(8,128)(2,1)S(1)}, u32[]{:S(2)}, u32[]{:S(2)}) %collective-permute-start.17) | collective-permute-done | bytes 98336 | tf_op jit(solution)/shard_map/ppermute | solution.py:572
  54.8 0.7 %collective-permute-done.16.refs_3_ = bf16[192,256]{1,0:T(8,128)(2,1)S(1)} collective-permute-done((bf16[192,256]{1,0:T(8,128)(2,1)S(1)}, bf16[192,256]{1,0:T(8,128)(2,1)S(1)}, u32[]{:S(2)}, u32[]{:S(2)}) %collective-permute-start.16) | collective-permute-done | bytes 98336 | tf_op jit(solution)/shard_map/ppermute | solution.py:572
  55.5 1.0 %collective-permute-done.15.refs_2_ = bf16[192,256]{1,0:T(8,128)(2,1)S(1)} collective-permute-done((bf16[192,256]{1,0:T(8,128)(2,1)S(1)}, bf16[192,256]{1,0:T(8,128)(2,1)S(1)}, u32[]{:S(2)}, u32[]{:S(2)}) %collective-permute-start.15) | collective-permute-done | bytes 98336 | tf_op jit(solution)/shard_map/ppermute | solution.py:572
  56.5 6.2 %upper_levels.1 = (f32[3,1,64,128]{3,2,1,0:T(8,128)}, f32[2,1,64,256]{3,2,1,0:T(8,128)}) custom-call(f32[64,256]{1,0:T(8,128)S(1)} %get-tuple-element.128.refs_0_, f32[64,256]{1,0:T(8,128)S(1)} %get-tuple-element.129.refs_1_, bf16[192,256]{1,0:T(8,128)(2,1)S(1)} %collective-permute-done.15.refs_2_, bf16[192,256]{1,0:T(8,128)(2,1)S(1)} %collective-permute-done.16.refs_3_, ...), custom_call_target="tpu_custom_call" | custom-call | flops 1000000000 | tf_op jit(solution)/shard_map/upper_levels/pallas_call | solution.py:447
  (5 shorter events, 0.1 us)
Async XLA Ops:
  1.8 6.1 %collective-permute-start.2 = (bf16[16,256]{1,0:T(8,128)(2,1)S(1)}, bf16[16,256]{1,0:T(8,128)(2,1)S(1)}, u32[]{:S(2)}, u32[]{:S(2)}) collective-permute-start(bf16[16,256]{1,0:T(8,128)(2,1)S(1)} %get-tuple-element.71), channel_id=1, source_target_pairs={{0,2},{1,3},{2,0},{3,1},{4,6},{5,7},{6,4},{7,5},{8,10},{9,11},{10,... | collective-permute-start | bytes 24584 | tf_op jit(solution)/shard_map/ppermute | solution.py:572
  4.8 11.4 %collective-permute-start.1 = (bf16[544,256]{1,0:T(8,128)(2,1)S(1)}, bf16[544,256]{1,0:T(8,128)(2,1)S(1)}, u32[]{:S(2)}, u32[]{:S(2)}) collective-permute-start(bf16[544,256]{1,0:T(8,128)(2,1)S(1)} %get-tuple-element.80.refs_1_), channel_id=1, source_target_pairs={{0,16},{1,17},{2,18},{3,19},{4,20},{5,21},{6,22},{7,23},{8,24},{9,... | collective-permute-start | bytes 835592 | tf_op jit(solution)/shard_map/ppermute | solution.py:572
  6.4 9.9 %collective-permute-start = (bf16[560,256]{1,0:T(8,128)(2,1)S(1)}, bf16[560,256]{1,0:T(8,128)(2,1)S(1)}, u32[]{:S(2)}, u32[]{:S(2)}) collective-permute-start(bf16[560,256]{1,0:T(8,128)(2,1)S(1)} %get-tuple-element.103.refs_0_.refs_3_), channel_id=1, source_target_pairs={{0,1},{1,0},{2,3},{3,2},{4,5},{5,4},{6,7},{7,6},{8,9},{9,8},{10,11... | collective-permute-start | bytes 860168 | tf_op jit(solution)/shard_map/ppermute | solution.py:572
  7.9 4.7 %collective-permute-start.3 = (bf16[16,512]{1,0:T(8,128)(2,1)S(1)}, bf16[16,512]{1,0:T(8,128)(2,1)S(1)}, u32[]{:S(2)}, u32[]{:S(2)}) collective-permute-start(bf16[16,512]{1,0:T(8,128)(2,1)S(1)} %pad_maximum_fusion), channel_id=1, source_target_pairs={{0,4},{1,5},{2,6},{3,7},{4,0},{5,1},{6,2},{7,3},{8,12},{9,13},{10,... | collective-permute-start | bytes 49160 | tf_op jit(solution)/shard_map/ppermute | solution.py:572
  10.5 10.8 %collective-permute-start.7 = (bf16[544,256]{1,0:T(8,128)(2,1)S(1)}, bf16[544,256]{1,0:T(8,128)(2,1)S(1)}, u32[]{:S(2)}, u32[]{:S(2)}) collective-permute-start(bf16[544,256]{1,0:T(8,128)(2,1)S(1)} %get-tuple-element.80.refs_1_), channel_id=1, source_target_pairs={{0,1},{1,0},{2,3},{3,2},{4,5},{5,4},{6,7},{7,6},{8,9},{9,8},{10,11... | collective-permute-start | bytes 835592 | tf_op jit(solution)/shard_map/ppermute | solution.py:572
  11.0 10.2 %collective-permute-start.8 = (bf16[560,256]{1,0:T(8,128)(2,1)S(1)}, bf16[560,256]{1,0:T(8,128)(2,1)S(1)}, u32[]{:S(2)}, u32[]{:S(2)}) collective-permute-start(bf16[560,256]{1,0:T(8,128)(2,1)S(1)} %get-tuple-element.103.refs_0_.refs_3_), channel_id=1, source_target_pairs={{0,16},{1,17},{2,18},{3,19},{4,20},{5,21},{6,22},{7,23},{8,24},{9,... | collective-permute-start | bytes 860168 | tf_op jit(solution)/shard_map/ppermute | solution.py:572
  12.5 1.2 %collective-permute-start.4 = (bf16[16,1024]{1,0:T(8,128)(2,1)S(1)}, bf16[16,1024]{1,0:T(8,128)(2,1)S(1)}, u32[]{:S(2)}, u32[]{:S(2)}) collective-permute-start(bf16[16,1024]{1,0:T(8,128)(2,1)S(1)} %constant_dynamic-update-slice_fusion.refs_2_), channel_id=1, source_target_pairs={{0,8},{1,9},{2,10},{3,11},{4,12},{5,13},{6,14},{7,15},{8,0},{9,1},... | collective-permute-start | bytes 98312 | tf_op jit(solution)/shard_map/ppermute | solution.py:572
  16.3 10.0 %collective-permute-start.5 = (bf16[560,256]{1,0:T(8,128)(2,1)S(1)}, bf16[560,256]{1,0:T(8,128)(2,1)S(1)}, u32[]{:S(2)}, u32[]{:S(2)}) collective-permute-start(bf16[560,256]{1,0:T(8,128)(2,1)S(1)} %collective-permute-done.refs_0_.refs_1_), channel_id=1, source_target_pairs={{0,16},{1,17},{2,18},{3,19},{4,20},{5,21},{6,22},{7,23},{8,24},{9,... | collective-permute-start | bytes 860168 | tf_op jit(solution)/shard_map/ppermute | solution.py:572
  16.9 9.4 %collective-permute-start.6 = (bf16[544,256]{1,0:T(8,128)(2,1)S(1)}, bf16[544,256]{1,0:T(8,128)(2,1)S(1)}, u32[]{:S(2)}, u32[]{:S(2)}) collective-permute-start(bf16[544,256]{1,0:T(8,128)(2,1)S(1)} %collective-permute-done.1.refs_1_), channel_id=1, source_target_pairs={{0,1},{1,0},{2,3},{3,2},{4,5},{5,4},{6,7},{7,6},{8,9},{9,8},{10,11... | collective-permute-start | bytes 835592 | tf_op jit(solution)/shard_map/ppermute | solution.py:572
  27.1 1.6 %collective-permute-start.9 = (bf16[512,256]{1,0:T(8,128)(2,1)S(1)}, bf16[512,256]{1,0:T(8,128)(2,1)S(1)}, u32[]{:S(2)}, u32[]{:S(2)}) collective-permute-start(bf16[512,256]{1,0:T(8,128)(2,1)S(1)} %product.9), channel_id=1, source_target_pairs={{0,8},{1,9},{2,10},{3,11},{4,12},{5,13},{6,14},{7,15},{8,0},{9,1},... | collective-permute-start | bytes 786440 | tf_op jit(solution)/shard_map/ppermute | solution.py:572
  28.8 3.4 %collective-permute-start.10 = (f32[512,256]{1,0:T(8,128)S(1)}, f32[512,256]{1,0:T(8,128)S(1)}, u32[]{:S(2)}, u32[]{:S(2)}) collective-permute-start(f32[512,256]{1,0:T(8,128)S(1)} %get-tuple-element.117), channel_id=1, source_target_pairs={{0,8},{1,9},{2,10},{3,11},{4,12},{5,13},{6,14},{7,15},{8,0},{9,1},... | collective-permute-start | bytes 1572872 | tf_op jit(solution)/shard_map/ppermute | solution.py:572
  29.2 5.9 %collective-permute-start.11 = (bf16[256,256]{1,0:T(8,128)(2,1)S(1)}, bf16[256,256]{1,0:T(8,128)(2,1)S(1)}, u32[]{:S(2)}, u32[]{:S(2)}) collective-permute-start(bf16[256,256]{1,0:T(8,128)(2,1)S(1)} %get-tuple-element.120), channel_id=1, source_target_pairs={{0,2},{1,3},{2,0},{3,1},{4,6},{5,7},{6,4},{7,5},{8,10},{9,11},{10,... | collective-permute-start | bytes 393224 | tf_op jit(solution)/shard_map/ppermute | solution.py:572
  30.6 7.1 %collective-permute-start.14 = (bf16[16,128]{1,0:T(8,128)(2,1)S(1)}, bf16[16,128]{1,0:T(8,128)(2,1)S(1)}, u32[]{:S(2)}, u32[]{:S(2)}) collective-permute-start(bf16[16,128]{1,0:T(8,128)(2,1)S(1)} %get-tuple-element.124.refs_0_), channel_id=1, source_target_pairs={{0,2},{1,3},{2,0},{3,1},{4,6},{5,7},{6,4},{7,5},{8,10},{9,11},{10,... | collective-permute-start | bytes 12296 | tf_op jit(solution)/shard_map/ppermute | solution.py:572
  32.2 11.2 %collective-permute-start.13 = (bf16[256,256]{1,0:T(8,128)(2,1)S(1)}, bf16[256,256]{1,0:T(8,128)(2,1)S(1)}, u32[]{:S(2)}, u32[]{:S(2)}) collective-permute-start(bf16[256,256]{1,0:T(8,128)(2,1)S(1)} %get-tuple-element.121.refs_2_), channel_id=1, source_target_pairs={{0,2},{1,3},{2,0},{3,1},{4,6},{5,7},{6,4},{7,5},{8,10},{9,11},{10,... | collective-permute-start | bytes 393224 | tf_op jit(solution)/shard_map/ppermute | solution.py:572
  35.1 8.2 %collective-permute-start.12 = (bf16[256,256]{1,0:T(8,128)(2,1)S(1)}, bf16[256,256]{1,0:T(8,128)(2,1)S(1)}, u32[]{:S(2)}, u32[]{:S(2)}) collective-permute-start(bf16[256,256]{1,0:T(8,128)(2,1)S(1)} %add_up.5), channel_id=1, source_target_pairs={{0,4},{1,5},{2,6},{3,7},{4,0},{5,1},{6,2},{7,3},{8,12},{9,13},{10,... | collective-permute-start | bytes 393224 | tf_op jit(solution)/shard_map/ppermute | solution.py:572
  49.3 5.4 %collective-permute-start.17 = (bf16[192,256]{1,0:T(8,128)(2,1)S(1)}, bf16[192,256]{1,0:T(8,128)(2,1)S(1)}, u32[]{:S(2)}, u32[]{:S(2)}) collective-permute-start(bf16[192,256]{1,0:T(8,128)(2,1)S(1)} %get-tuple-element.130), channel_id=1, source_target_pairs={{0,1},{1,0},{2,3},{3,2},{4,5},{5,4},{6,7},{7,6},{8,9},{9,8},{10,11... | collective-permute-start | bytes 294920 | tf_op jit(solution)/shard_map/ppermute | solution.py:572
  50.9 4.6 %collective-permute-start.16 = (bf16[192,256]{1,0:T(8,128)(2,1)S(1)}, bf16[192,256]{1,0:T(8,128)(2,1)S(1)}, u32[]{:S(2)}, u32[]{:S(2)}) collective-permute-start(bf16[192,256]{1,0:T(8,128)(2,1)S(1)} %get-tuple-element.130), channel_id=1, source_target_pairs={{0,2},{1,3},{2,0},{3,1},{4,6},{5,7},{6,4},{7,5},{8,10},{9,11},{10,... | collective-permute-start | bytes 294920 | tf_op jit(solution)/shard_map/ppermute | solution.py:572
  50.9 5.6 %collective-permute-start.15 = (bf16[192,256]{1,0:T(8,128)(2,1)S(1)}, bf16[192,256]{1,0:T(8,128)(2,1)S(1)}, u32[]{:S(2)}, u32[]{:S(2)}) collective-permute-start(bf16[192,256]{1,0:T(8,128)(2,1)S(1)} %get-tuple-element.130), channel_id=1, source_target_pairs={{0,3},{1,2},{2,1},{3,0},{4,7},{5,6},{6,5},{7,4},{8,11},{9,10},{10,... | collective-permute-start | bytes 294920 | tf_op jit(solution)/shard_map/ppermute | solution.py:572
